TPU v7x, 256 devices: a whole 4x4x8 slice. The times are simulated.
256 devices in a mesh: turn: 32 (over x, y, core), hist: 8 (over z).
Axes of the slice: x: 4, y: 4, z: 8, core: 2. Of those that a mesh axis runs over, the one named last changes fastest.
Arguments:
- flop_reach: float32 [1326, 128], P(None, 'hist'), may hold values from 0 to 0.01
- turn_policy: int32 [32, 1326, 128], P('turn', None, 'hist'), may hold values from 0 to 256
- river_policy: int32 [32, 5431296], P('turn', 'hist'), may hold values from 0 to 256
- hand_rank: int32 [32, 32, 1326], P('turn', 'hist'), may hold values from 0 to 7461
- turn_cards: int32 [32], P('turn'), may hold values from 3 to 51, as said below
- river_cards: int32 [32, 32], P('turn'), may hold values from 3 to 51, as said below
- children: int32 [64, 2], replicated, may hold values from 0 to 127
- pot: int32 [128], replicated, may hold values from 1 to 24
Outputs:
- turn_value: float32 [32, 84864], P('turn')
- flop_value: float32 [84864], replicated
Inputs may be any that keep to these rules, and one draw needn't show every extreme that they name: `turn_cards`: distinct cards, none of the flop cards 0, 1, 2. `river_cards`: for each turn card, distinct cards, none of the flop cards and not that turn card.
All inputs are finite; a program needn't handle non-finite values.
Results may differ from a plain program's by a relative error of at most 0.0003.
Values sent between devices are 32-bit elements; how exact they have to be, the bound alone decides.
No kernel may reach another device: no remote copies, remote signals or barrier semaphores. Data moves between devices by JAX's collectives and lax.ppermute only.
A program may use at most 64 MiB of HBM per device.

v0:
```python
import functools

import jax
import jax.numpy as jnp
import numpy as np
from jax import lax
from jax.experimental import pallas as pl
from jax.experimental.pallas import tpu as pltpu
from jax.sharding import PartitionSpec as P

HANDS = 1326
LOW = 150
BASE = 245
SLOTS = HANDS - BASE
TILES = 9
WIDE = TILES * 128
ROWS = 17
VMEM_LIMIT = 56 * 1024 * 1024


def slot_cards():
    first, second = np.triu_indices(52, 1)
    a = np.full((WIDE,), 200, np.int32)
    b = np.full((WIDE,), 201, np.int32)
    a[:SLOTS], b[:SLOTS] = first[BASE:], second[BASE:]
    return a, b


def compat_table():
    a, b = slot_cards()
    real = np.arange(WIDE) < SLOTS
    shares = (
        (a[:, None] == a[None, :])
        | (a[:, None] == b[None, :])
        | (b[:, None] == a[None, :])
        | (b[:, None] == b[None, :])
    )
    return (~shares & real[:, None] & real[None, :]).astype(np.float32)


def renamed(t, r):
    return jnp.where(r == 3, 4, 3), jnp.where(t == 4, 3, 4)


def source_lanes(a, b, t, r):
    card_t, card_r = renamed(t, r)
    off_t = jnp.where(card_t == 3, -4, 43)
    off_r = jnp.where(card_r == 3, -4, 43)
    has_t = (a == t) | (b == t)
    has_r = (a == r) | (b == r)
    from_t = jnp.where(a == t, b, a) + off_t
    from_r = jnp.where(a == r, b, a) + off_r
    one = jnp.where(has_t, from_t, jnp.where(has_r, from_r, -1))
    return jnp.where(has_t & has_r, 0, one)


def home_slots(lane, t, r):
    card_t, card_r = renamed(t, r)
    t_high, r_high = t >= 5, r >= 5
    none = jnp.int32(-1)
    name3 = jnp.where(t_high & (card_t == 3), t, jnp.where(r_high & (card_r == 3), r, none))
    name4 = jnp.where(t_high & (card_t == 4), t, jnp.where(r_high & (card_r == 4), r, none))
    of3 = lane < 48
    x = jnp.where(of3, lane + 4, lane - 43)
    p = jnp.where(of3, name3, name4)
    q = jnp.where(x == 4, name4, x)
    good = (lane < 95) & (p >= 5) & (q >= 5) & (x != t) & (x != r)
    low, high = jnp.minimum(p, q), jnp.maximum(p, q)
    u = low - 5
    slot = u * 46 - ((u * (u - 1)) >> 1) + high - low - 1
    return jnp.where(good, slot, -1)


def lanes_of(shape):
    return lax.broadcasted_iota(jnp.int32, shape, 1)


def pick(values, index):
    return jnp.take_along_axis(values, index, axis=1, mode="promise_in_bounds")


def tile(ref, j):
    return ref[:, 128 * j : 128 * j + 128]


def pack_kernel(scal, policy, flop_reach, turn_policy, slot_a, slot_b, *rest):
    outs, (raw, own, low) = rest[:8], rest[8:]
    me, t = scal[0], scal[1]
    lane = lanes_of((8, 128))
    reach = flop_reach[...] * (turn_policy[...].astype(jnp.float32) * (1.0 / 256.0)) * (1.0 / 256.0)
    reach = jnp.concatenate([reach, jnp.zeros((16, 1408 - HANDS), jnp.float32)], axis=1)
    for j in range(11):
        raw[16 * j : 16 * j + 16, :] = reach[:, 128 * j : 128 * j + 128]
    wide = lanes_of((8, 1408))
    for p in range(2):
        reach = jnp.concatenate([raw[pl.ds(16 * j + p, 8, stride=2), :] for j in range(11)], axis=1)
        moved = pltpu.roll(reach, 1408 - BASE, 1)
        own[p] = jnp.where(wide < SLOTS, moved, 0.0)[:, :WIDE]
        moved = pltpu.roll(reach, 1408 - LOW, 1)
        low[p] = jnp.where(wide < 95, moved, 0.0)[:, :128]

    def one_river(out, rl, river):
        r = scal[2 + river]
        index = [source_lanes(tile(slot_a, j), tile(slot_b, j), t, r) for j in range(TILES)]
        tails = []
        for p in range(2):

            def aligned(start, count):
                row, shift = start >> 7, start & 127
                turn = (128 - shift) & 127
                rolled = [
                    pltpu.roll(policy[pl.ds(jnp.minimum(row + i, 662), 8, stride=663), :], turn, 1)
                    for i in range(count + 1)
                ]
                keep = lane < 128 - shift
                return [
                    jnp.where(keep, rolled[i], rolled[i + 1]).astype(jnp.float32) for i in range(count)
                ]

            start = p * 42432 + river * HANDS + LOW
            source = aligned(start, 1)[0] * low[p]
            plain = aligned(start + (BASE - LOW), TILES)
            for j in range(TILES):
                kept = plain[j] * own[p, :, 128 * j : 128 * j + 128]
                taken = pick(source, jnp.maximum(index[j], 0))
                value = jnp.where(index[j] >= 0, taken, kept)
                if j < 8:
                    out[rl, 8 * p + j] = value
                else:
                    tails.append(value)
        out[rl, 16] = tails[0] + pltpu.roll(tails[1], 64, 1)

    for s in range(8):
        group = (me + s) & 7

        @pl.loop(0, 4)
        def _(rl, out=outs[s], group=group):
            one_river(out, rl, group * 4 + rl)


def pack(scal, policy, flop_reach, turn_policy, slot_a, slot_b):
    smem = pl.BlockSpec(memory_space=pltpu.SMEM)
    vmem = pl.BlockSpec(memory_space=pltpu.VMEM)
    return pl.pallas_call(
        pack_kernel,
        out_shape=[jax.ShapeDtypeStruct((4, ROWS, 8, 128), jnp.float32)] * 8,
        in_specs=[smem] + [vmem] * 5,
        out_specs=[vmem] * 8,
        scratch_shapes=[
            pltpu.VMEM((176, 128), jnp.float32),
            pltpu.VMEM((2, 8, WIDE), jnp.float32),
            pltpu.VMEM((2, 8, 128), jnp.float32),
        ],
        compiler_params=pltpu.CompilerParams(vmem_limit_bytes=VMEM_LIMIT),
        name="pack",
    )(scal, policy, flop_reach, turn_policy, slot_a, slot_b)


def payoff_kernel(scal, ranks, compat, slot_a, slot_b, out, rows, strip):
    rl = pl.program_id(0)
    t = scal[1]
    r = scal[2 + 4 * scal[0] + rl]
    raw = ranks[...]
    value = (128 + (raw & 127)).astype(jnp.float32)
    for bit in range(6):
        value = value * jnp.where(((raw >> (7 + bit)) & 1) == 1, float(2 ** (2**bit)), 1.0)
    rows[...] = jnp.zeros_like(rows)
    rows[0:4, :HANDS] = value
    row = jnp.broadcast_to(rows[pl.ds(rl, 1), :], (8, 1408))
    plain = pltpu.roll(row, 1408 - BASE, 1)
    source = pltpu.roll(row, 1408 - LOW, 1)[:, :128]
    for j in range(TILES):
        index = source_lanes(tile(slot_a, j), tile(slot_b, j), t, r)
        taken = pick(source, jnp.maximum(index, 0))
        strip[:, 128 * j : 128 * j + 128] = jnp.where(index >= 0, taken, plain[:, 128 * j : 128 * j + 128])
    across = [
        jnp.broadcast_to(strip[0:1, 128 * j : 128 * j + 128], (128, 128)).astype(jnp.bfloat16)
        for j in range(TILES)
    ]
    for i in range(TILES):
        down = jnp.transpose(jnp.broadcast_to(strip[0:1, 128 * i : 128 * i + 128], (128, 128)))
        down = down.astype(jnp.bfloat16)
        for j in range(TILES):
            mask = compat[128 * i : 128 * i + 128, 128 * j : 128 * j + 128]
            out[0, 128 * i : 128 * i + 128, 128 * j : 128 * j + 128] = jnp.minimum(
                jnp.maximum(across[j] - down, -mask), mask
            )


def payoffs(scal, ranks, compat, slot_a, slot_b):
    smem = pl.BlockSpec(memory_space=pltpu.SMEM)
    vmem = pl.BlockSpec(memory_space=pltpu.VMEM)
    return pl.pallas_call(
        payoff_kernel,
        grid=(4,),
        out_shape=jax.ShapeDtypeStruct((4, WIDE, WIDE), jnp.bfloat16),
        in_specs=[smem] + [vmem] * 4,
        out_specs=pl.BlockSpec((1, WIDE, WIDE), lambda i: (i, 0, 0)),
        scratch_shapes=[pltpu.VMEM((8, 1408), jnp.float32), pltpu.VMEM((8, WIDE), jnp.float32)],
        compiler_params=pltpu.CompilerParams(vmem_limit_bytes=VMEM_LIMIT),
        cost_estimate=pl.CostEstimate(flops=4 * 4 * WIDE * WIDE, bytes_accessed=10 * WIDE * WIDE, transcendentals=0),
        name="payoff",
    )(scal, ranks, compat, slot_a, slot_b)


def reply_kernel(scal, payoff, select, scale, slot_a, slot_b, *rest):
    blocks, out, high, rest_low = rest[:8], rest[8], rest[9], rest[10]
    rl = pl.program_id(0)
    t = scal[1]
    r = scal[2 + 4 * scal[0] + rl]
    lane = lanes_of((8, 128))
    for s in range(8):
        for j in range(TILES):
            if j < 8:
                pair = [blocks[s][0, j], blocks[s][0, 8 + j]]
            else:
                tails = blocks[s][0, 16]
                pair = [jnp.where(lane < 64, v, 0.0) for v in (tails, pltpu.roll(tails, 64, 1))]
            both = jnp.concatenate(pair, axis=0)
            upper = both.astype(jnp.bfloat16)
            high[16 * s : 16 * s + 16, 128 * j : 128 * j + 128] = upper
            rest_low[16 * s : 16 * s + 16, 128 * j : 128 * j + 128] = (
                both - upper.astype(jnp.float32)
            ).astype(jnp.bfloat16)
    dot = functools.partial(jnp.dot, preferred_element_type=jnp.float32)
    chosen = jnp.concatenate(
        [dot(select[...], high[...]).astype(jnp.bfloat16), dot(select[...], rest_low[...]).astype(jnp.bfloat16)],
        axis=0,
    )
    value = dot(chosen, payoff[0])
    value = (value[:128] + value[128:]) * scale[...]
    reply = jnp.maximum(value[:64], value[64:])

    @pl.when(rl == 0)
    def _():
        out[...] = jnp.zeros_like(out)

    home = home_slots(lane, t, r)
    for j in range(TILES):
        moved = source_lanes(tile(slot_a, j), tile(slot_b, j), t, r) >= 0
        for g in range(8):
            part = reply[8 * g : 8 * g + 8, 128 * j : 128 * j + 128]
            out[g, 1 + j] += jnp.where(moved, 0.0, part)
            out[g, 0] += jnp.where((home >> 7) == j, pick(part, home & 127), 0.0)


def replies(scal, payoff, select, scale, slot_a, slot_b, blocks):
    smem = pl.BlockSpec(memory_space=pltpu.SMEM)
    vmem = pl.BlockSpec(memory_space=pltpu.VMEM)
    block = pl.BlockSpec((1, ROWS, 8, 128), lambda i: (i, 0, 0, 0))
    return pl.pallas_call(
        reply_kernel,
        grid=(4,),
        out_shape=jax.ShapeDtypeStruct((8, TILES + 1, 8, 128), jnp.float32),
        in_specs=[smem, pl.BlockSpec((1, WIDE, WIDE), lambda i: (i, 0, 0))] + [vmem] * 4 + [block] * 8,
        out_specs=vmem,
        scratch_shapes=[pltpu.VMEM((128, WIDE), jnp.bfloat16)] * 2,
        compiler_params=pltpu.CompilerParams(vmem_limit_bytes=VMEM_LIMIT),
        cost_estimate=pl.CostEstimate(
            flops=4 * 2 * 256 * WIDE * WIDE, bytes_accessed=8 * WIDE * WIDE, transcendentals=0
        ),
        name="reply",
    )(scal, payoff, select, scale, slot_a, slot_b, *blocks)


def flat(nodes):
    rows = jnp.transpose(nodes, (0, 2, 1, 3)).reshape(64, TILES + 1, 128)
    body = rows[:, 1:].reshape(64, WIDE)[:, :SLOTS]
    return jnp.concatenate([jnp.zeros((64, LOW), jnp.float32), rows[:, 0, :95], body], axis=1).reshape(-1)


def turn_sum(value, size):
    bit = 1
    while bit < size:
        value = value + lax.ppermute(value, "turn", [(i, i ^ bit) for i in range(size)])
        bit *= 2
    return value


def per_device(flop_reach, turn_policy, river_policy, hand_rank, turn_cards, river_cards, children, pot):
    groups = lax.axis_size("hist")
    turns = lax.axis_size("turn")
    me = lax.axis_index("hist")
    a, b = slot_cards()
    slot_a = jnp.asarray(np.broadcast_to(a, (8, WIDE)))
    slot_b = jnp.asarray(np.broadcast_to(b, (8, WIDE)))
    compat = jnp.asarray(compat_table(), jnp.bfloat16)
    scal = jnp.concatenate([me.reshape(1).astype(jnp.int32), turn_cards, river_cards[0]])
    packed = pack(
        scal,
        river_policy.reshape(5304, 128),
        jnp.transpose(flop_reach),
        jnp.transpose(turn_policy[0]),
        slot_a,
        slot_b,
    )
    blocks = [packed[0]]
    for s in range(1, groups):
        blocks.append(lax.ppermute(packed[s], "hist", [(i, (i + s) % groups) for i in range(groups)]))
    payoff = payoffs(scal, hand_rank[0], compat, slot_a, slot_b)
    child = jnp.transpose(children).reshape(128)
    place = (((me - (child >> 4)) & 7) << 4) + ((child & 1) << 3) + ((child >> 1) & 7)
    select = (place[:, None] == jnp.arange(128)[None, :]).astype(jnp.bfloat16)
    scale = jnp.sum(
        jnp.where(child[:, None] == jnp.arange(128)[None, :], pot.astype(jnp.float32)[None, :], 0.0),
        axis=1,
        keepdims=True,
    )
    partial = replies(scal, payoff, select, scale, slot_a, slot_b, blocks)
    arrived = lax.all_to_all(partial, "hist", 0, 0, tiled=True)
    value = jnp.sum(arrived, axis=0) * (1.0 / 32.0)
    mean = turn_sum(value, turns) * (1.0 / turns)
    both = jnp.stack([value, mean])
    spread = lax.all_to_all(jnp.broadcast_to(both, (groups,) + both.shape), "hist", 0, 0, tiled=True)
    return (flat(spread[:, 0]).reshape(1, -1), flat(spread[:, 1]))


def solution(mesh):
    return jax.shard_map(
        per_device,
        mesh=mesh,
        in_specs=(
            P(None, "hist"),
            P("turn", None, "hist"),
            P("turn", "hist"),
            P("turn", "hist", None),
            P("turn"),
            P("turn", None),
            P(),
            P(),
        ),
        out_specs=(P("turn", None), P()),
        check_vma=False,
    )
```

profile of v0, /device:TPU:6, one launch (start us, length us, event | category | flops | bytes accessed | tf_op | source)
XLA Modules:
  0.0 145.4 jit_solution(9818155427437859462)
XLA Ops:
  0.6 0.0 copy-start.7
  0.6 0.0 copy-start.8
  1.3 1.3 pad_add_fusion.scal
  2.6 1.3 jit_solution_.6.slot_a
  3.9 1.3 jit_solution_.7.slot_b
  5.2 10.3 %pack.1 = (f32[4,17,8,128]{3,2,1,0:T(8,128)}, f32[4,17,8,128]{3,2,1,0:T(8,128)}, f32[4,17,8,128]{3,2,1,0:T(8,128)}, f32[4,17,8,128]{3,2,1,0:T(8,128)}, f32[4,17,...) custom-call(s32[34]{0:T(128)} %pad_add_fusion.scal, ...), custom_call_target="tpu_custom_call" | custom-call | tf_op jit(solution)/shard_map/pack/pallas_call | solution.py:144
  15.5 1.9 %collective-permute-start = (f32[4,17,8,128]{3,2,1,0:T(8,128)}, f32[4,17,8,128]{3,2,1,0:T(8,128)S(1)}, u32[]{:S(2)}, u32[]{:S(2)}) collective-permute-start(f32[4,17,8,128]{3,2,1,0:T(8,128)} %get-tuple-element.11), channel_id=1, source_target_pairs={{0,1},{1,2},{2,3},{3,4},{4,5},{5,6},{6,7},{7,0},{8,9},{9,10},{10,1... | collective-permute-start | bytes 835592 | tf_op jit(solution)/shard_map/ppermute | solution.py:299
  17.4 3.3 %collective-permute-start.1 = (f32[4,17,8,128]{3,2,1,0:T(8,128)}, f32[4,17,8,128]{3,2,1,0:T(8,128)S(1)}, u32[]{:S(2)}, u32[]{:S(2)}) collective-permute-start(f32[4,17,8,128]{3,2,1,0:T(8,128)} %get-tuple-element.12), channel_id=1, source_target_pairs={{0,2},{1,3},{2,4},{3,5},{4,6},{5,7},{6,0},{7,1},{8,10},{9,11},{10,... | collective-permute-start | bytes 835592 | tf_op jit(solution)/shard_map/ppermute | solution.py:299
  20.7 4.0 %collective-permute-start.2 = (f32[4,17,8,128]{3,2,1,0:T(8,128)}, f32[4,17,8,128]{3,2,1,0:T(8,128)S(1)}, u32[]{:S(2)}, u32[]{:S(2)}) collective-permute-start(f32[4,17,8,128]{3,2,1,0:T(8,128)} %get-tuple-element.13), channel_id=1, source_target_pairs={{0,3},{1,4},{2,5},{3,6},{4,7},{5,0},{6,1},{7,2},{8,11},{9,12},{10,... | collective-permute-start | bytes 835592 | tf_op jit(solution)/shard_map/ppermute | solution.py:299
  24.7 0.5 collective-permute-start.3
  25.3 4.9 %collective-permute-start.4 = (f32[4,17,8,128]{3,2,1,0:T(8,128)}, f32[4,17,8,128]{3,2,1,0:T(8,128)S(1)}, u32[]{:S(2)}, u32[]{:S(2)}) collective-permute-start(f32[4,17,8,128]{3,2,1,0:T(8,128)} %get-tuple-element.15), channel_id=1, source_target_pairs={{0,5},{1,6},{2,7},{3,0},{4,1},{5,2},{6,3},{7,4},{8,13},{9,14},{10,... | collective-permute-start | bytes 835592 | tf_op jit(solution)/shard_map/ppermute | solution.py:299
  30.2 0.1 reshape.60
  30.3 0.0 collective-permute-done.rest_1_
  30.3 6.9 %collective-permute-start.5 = (f32[4,17,8,128]{3,2,1,0:T(8,128)}, f32[4,17,8,128]{3,2,1,0:T(8,128)S(1)}, u32[]{:S(2)}, u32[]{:S(2)}) collective-permute-start(f32[4,17,8,128]{3,2,1,0:T(8,128)} %get-tuple-element.16), channel_id=1, source_target_pairs={{0,6},{1,7},{2,0},{3,1},{4,2},{5,3},{6,4},{7,5},{8,14},{9,15},{10,... | collective-permute-start | bytes 835592 | tf_op jit(solution)/shard_map/ppermute | solution.py:299
  37.2 6.9 %collective-permute-done.1.rest_2_ = f32[4,17,8,128]{3,2,1,0:T(8,128)S(1)} collective-permute-done((f32[4,17,8,128]{3,2,1,0:T(8,128)}, f32[4,17,8,128]{3,2,1,0:T(8,128)S(1)}, u32[]{:S(2)}, u32[]{:S(2)}) %collective-permute-start.1) | collective-permute-done | bytes 278560 | tf_op jit(solution)/shard_map/ppermute | solution.py:299
  44.1 2.4 %collective-permute-start.6 = (f32[4,17,8,128]{3,2,1,0:T(8,128)}, f32[4,17,8,128]{3,2,1,0:T(8,128)S(1)}, u32[]{:S(2)}, u32[]{:S(2)}) collective-permute-start(f32[4,17,8,128]{3,2,1,0:T(8,128)} %get-tuple-element.17), channel_id=1, source_target_pairs={{0,7},{1,0},{2,1},{3,2},{4,3},{5,4},{6,5},{7,6},{8,15},{9,8},{10,9... | collective-permute-start | bytes 835592 | tf_op jit(solution)/shard_map/ppermute | solution.py:299
  46.4 0.2 select_reduce_fusion
  46.6 0.8 copy.23.scale
  47.4 8.6 %payoff.1 = bf16[4,1152,1152]{2,1,0:T(8,128)(2,1)} custom-call(s32[34]{0:T(128)} %pad_add_fusion.scal, s32[4,1326]{1,0:T(4,128)} %bitcast.47, bf16[1152,1152]{1,0:T(8,128)(2,1)} %constant.25.clone.compat, s32[8,1152]{1,0:T(8,128)} %jit_solution_.6.slot_a, s32[8,1152]{1,0:T(8,128)} %jit_solution_.7.slot_b), custom_call_target="tpu_custom_call" | custom-call | flops 21233664 | bytes 13271040 | tf_op jit(solution)/shard_map/payoff/pallas_call | solution.py:193
  56.0 0.0 copy-done.1
  56.0 0.7 fusion.select
  56.7 7.7 %collective-permute-done.2.rest_3_ = f32[4,17,8,128]{3,2,1,0:T(8,128)S(1)} collective-permute-done((f32[4,17,8,128]{3,2,1,0:T(8,128)}, f32[4,17,8,128]{3,2,1,0:T(8,128)S(1)}, u32[]{:S(2)}, u32[]{:S(2)}) %collective-permute-start.2) | collective-permute-done | bytes 278560 | tf_op jit(solution)/shard_map/ppermute | solution.py:299
  64.4 0.0 collective-permute-done.3.rest_4_
  64.4 0.0 collective-permute-done.4.rest_5_
  64.4 0.0 copy-start.4
  64.4 6.5 %collective-permute-done.5.rest_6_ = f32[4,17,8,128]{3,2,1,0:T(8,128)S(1)} collective-permute-done((f32[4,17,8,128]{3,2,1,0:T(8,128)}, f32[4,17,8,128]{3,2,1,0:T(8,128)S(1)}, u32[]{:S(2)}, u32[]{:S(2)}) %collective-permute-start.5) | collective-permute-done | bytes 278560 | tf_op jit(solution)/shard_map/ppermute | solution.py:299
  71.0 3.8 %collective-permute-done.6.rest_7_ = f32[4,17,8,128]{3,2,1,0:T(8,128)S(1)} collective-permute-done((f32[4,17,8,128]{3,2,1,0:T(8,128)}, f32[4,17,8,128]{3,2,1,0:T(8,128)S(1)}, u32[]{:S(2)}, u32[]{:S(2)}) %collective-permute-start.6) | collective-permute-done | bytes 278560 | tf_op jit(solution)/shard_map/ppermute | solution.py:299
  74.8 0.0 copy-done.3
  74.8 0.0 copy-done.5
  74.8 0.7 copy-done.6
  75.5 8.8 %reply.1 = f32[8,10,8,128]{3,2,1,0:T(8,128)} custom-call(s32[34]{0:T(128)} %pad_add_fusion.scal, bf16[4,1152,1152]{2,1,0:T(8,128)(2,1)} %payoff.1, bf16[128,128]{1,0:T(8,128)(2,1)} %fusion.select, f32[128,1]{1,0:T(8,128)} %copy.23.scale, s32[8,1152]{1,0:T(8,128)} %jit_solution_.6.slot_a, s32[8,1152]{1,0:T(8,128)} %jit_solution_.7.slot_b, ...), custom_call_target="tpu_custom_call" | custom-call | flops 2717908992 | bytes 10616832 | tf_op jit(solution)/shard_map/reply/pallas_call | solution.py:251
  84.3 18.9 %all_to_all.10 = f32[8,10,8,128]{3,2,1,0:T(8,128)S(1)} all-to-all(f32[8,10,8,128]{3,2,1,0:T(8,128)} %reply.1), channel_id=1, replica_groups=mesh['turn'=32,'hist'=8] {'hist'}, dimensions={0} | all-to-all | bytes 655360 | tf_op jit(solution)/shard_map/all_to_all | solution.py:310
  103.2 0.1 collective-permute-start.7
  103.3 1.2 collective-permute-done.7
  104.5 1.7 %collective-permute-start.8 = (f32[10,8,128]{2,1,0:T(8,128)S(1)}, f32[10,8,128]{2,1,0:T(8,128)S(1)}, u32[]{:S(2)}, u32[]{:S(2)}) collective-permute-start(f32[10,8,128]{2,1,0:T(8,128)S(1)} %get-tuple-element.21), channel_id=1, source_target_pairs={{0,16},{8,24},{16,0},{24,8},{32,48},{40,56},{48,32},{56,40},{64,80... | collective-permute-start | bytes 122888 | tf_op jit(solution)/shard_map/ppermute | solution.py:275
  106.2 2.4 %collective-permute-done.8 = f32[10,8,128]{2,1,0:T(8,128)S(1)} collective-permute-done((f32[10,8,128]{2,1,0:T(8,128)S(1)}, f32[10,8,128]{2,1,0:T(8,128)S(1)}, u32[]{:S(2)}, u32[]{:S(2)}) %collective-permute-start.8) | collective-permute-done | bytes 40992 | tf_op jit(solution)/shard_map/ppermute | solution.py:275
  108.6 3.2 %collective-permute-start.9 = (f32[10,8,128]{2,1,0:T(8,128)S(1)}, f32[10,8,128]{2,1,0:T(8,128)S(1)}, u32[]{:S(2)}, u32[]{:S(2)}) collective-permute-start(f32[10,8,128]{2,1,0:T(8,128)S(1)} %add.32), channel_id=1, source_target_pairs={{0,32},{8,40},{16,48},{24,56},{32,0},{40,8},{48,16},{56,24},{64,96... | collective-permute-start | bytes 122888 | tf_op jit(solution)/shard_map/ppermute | solution.py:275
  111.8 2.3 %collective-permute-done.9 = f32[10,8,128]{2,1,0:T(8,128)S(1)} collective-permute-done((f32[10,8,128]{2,1,0:T(8,128)S(1)}, f32[10,8,128]{2,1,0:T(8,128)S(1)}, u32[]{:S(2)}, u32[]{:S(2)}) %collective-permute-start.9) | collective-permute-done | bytes 40992 | tf_op jit(solution)/shard_map/ppermute | solution.py:275
  114.1 0.8 collective-permute-start.10
  115.0 3.2 %collective-permute-done.10 = f32[10,8,128]{2,1,0:T(8,128)S(1)} collective-permute-done((f32[10,8,128]{2,1,0:T(8,128)S(1)}, f32[10,8,128]{2,1,0:T(8,128)S(1)}, u32[]{:S(2)}, u32[]{:S(2)}) %collective-permute-start.10) | collective-permute-done | bytes 40992 | tf_op jit(solution)/shard_map/ppermute | solution.py:275
  118.1 1.4 collective-permute-start.11
  119.5 4.1 %collective-permute-done.11 = f32[10,8,128]{2,1,0:T(8,128)S(1)} collective-permute-done((f32[10,8,128]{2,1,0:T(8,128)S(1)}, f32[10,8,128]{2,1,0:T(8,128)S(1)}, u32[]{:S(2)}, u32[]{:S(2)}) %collective-permute-start.11) | collective-permute-done | bytes 40992 | tf_op jit(solution)/shard_map/ppermute | solution.py:275
  123.7 18.7 %all_to_all.11 = f32[8,2,10,8,128]{4,3,2,1,0:T(8,128)S(1)} all-to-all(f32[8,2,10,8,128]{4,3,2,1,0:T(8,128)S(1)} %broadcast_in_dim.25), channel_id=1, replica_groups=mesh['turn'=32,'hist'=8] {'hist'}, dimensions={0} | all-to-all | bytes 1310720 | tf_op jit(solution)/shard_map/all_to_all | solution.py:314
  142.5 0.1 copy_bitcast_fusion
  142.6 0.2 concatenate.11
  142.8 1.0 reshape.66
  143.8 0.2 concatenate.10
  144.0 1.3 reshape_reshape.3
  (28 shorter events, 0.2 us)
Async XLA Ops:
  0.6 29.6 %copy-start.7 = (s32[64,2]{0,1:T(2,128)S(1)}, s32[64,2]{0,1:T(2,128)}, u32[]{:S(2)}) copy-start(s32[64,2]{0,1:T(2,128)} %param.17) | copy-start | bytes 1540
  0.6 29.7 %copy-start.8 = (s32[128]{0:T(128)S(1)}, s32[128]{0:T(128)}, u32[]{:S(2)}) copy-start(s32[128]{0:T(128)} %param.18) | copy-start | bytes 1540
  15.5 14.8 %collective-permute-start = (f32[4,17,8,128]{3,2,1,0:T(8,128)}, f32[4,17,8,128]{3,2,1,0:T(8,128)S(1)}, u32[]{:S(2)}, u32[]{:S(2)}) collective-permute-start(f32[4,17,8,128]{3,2,1,0:T(8,128)} %get-tuple-element.11), channel_id=1, source_target_pairs={{0,1},{1,2},{2,3},{3,4},{4,5},{5,6},{6,7},{7,0},{8,9},{9,10},{10,1... | collective-permute-start | bytes 835592 | tf_op jit(solution)/shard_map/ppermute | solution.py:299
  17.4 26.7 %collective-permute-start.1 = (f32[4,17,8,128]{3,2,1,0:T(8,128)}, f32[4,17,8,128]{3,2,1,0:T(8,128)S(1)}, u32[]{:S(2)}, u32[]{:S(2)}) collective-permute-start(f32[4,17,8,128]{3,2,1,0:T(8,128)} %get-tuple-element.12), channel_id=1, source_target_pairs={{0,2},{1,3},{2,4},{3,5},{4,6},{5,7},{6,0},{7,1},{8,10},{9,11},{10,... | collective-permute-start | bytes 835592 | tf_op jit(solution)/shard_map/ppermute | solution.py:299
  20.7 43.7 %collective-permute-start.2 = (f32[4,17,8,128]{3,2,1,0:T(8,128)}, f32[4,17,8,128]{3,2,1,0:T(8,128)S(1)}, u32[]{:S(2)}, u32[]{:S(2)}) collective-permute-start(f32[4,17,8,128]{3,2,1,0:T(8,128)} %get-tuple-element.13), channel_id=1, source_target_pairs={{0,3},{1,4},{2,5},{3,6},{4,7},{5,0},{6,1},{7,2},{8,11},{9,12},{10,... | collective-permute-start | bytes 835592 | tf_op jit(solution)/shard_map/ppermute | solution.py:299
  24.7 39.7 %collective-permute-start.3 = (f32[4,17,8,128]{3,2,1,0:T(8,128)}, f32[4,17,8,128]{3,2,1,0:T(8,128)S(1)}, u32[]{:S(2)}, u32[]{:S(2)}) collective-permute-start(f32[4,17,8,128]{3,2,1,0:T(8,128)} %get-tuple-element.14), channel_id=1, source_target_pairs={{0,4},{1,5},{2,6},{3,7},{4,0},{5,1},{6,2},{7,3},{8,12},{9,13},{10,... | collective-permute-start | bytes 835592 | tf_op jit(solution)/shard_map/ppermute | solution.py:299
  25.3 39.2 %collective-permute-start.4 = (f32[4,17,8,128]{3,2,1,0:T(8,128)}, f32[4,17,8,128]{3,2,1,0:T(8,128)S(1)}, u32[]{:S(2)}, u32[]{:S(2)}) collective-permute-start(f32[4,17,8,128]{3,2,1,0:T(8,128)} %get-tuple-element.15), channel_id=1, source_target_pairs={{0,5},{1,6},{2,7},{3,0},{4,1},{5,2},{6,3},{7,4},{8,13},{9,14},{10,... | collective-permute-start | bytes 835592 | tf_op jit(solution)/shard_map/ppermute | solution.py:299
  30.3 25.7 %copy-start = (f32[4,17,8,128]{3,2,1,0:T(8,128)}, f32[4,17,8,128]{3,2,1,0:T(8,128)S(1)}, u32[]{:S(2)}) copy-start(f32[4,17,8,128]{3,2,1,0:T(8,128)S(1)} %collective-permute-done.rest_1_) | copy-start | bytes 835588
  30.3 40.6 %collective-permute-start.5 = (f32[4,17,8,128]{3,2,1,0:T(8,128)}, f32[4,17,8,128]{3,2,1,0:T(8,128)S(1)}, u32[]{:S(2)}, u32[]{:S(2)}) collective-permute-start(f32[4,17,8,128]{3,2,1,0:T(8,128)} %get-tuple-element.16), channel_id=1, source_target_pairs={{0,6},{1,7},{2,0},{3,1},{4,2},{5,3},{6,4},{7,5},{8,14},{9,15},{10,... | collective-permute-start | bytes 835592 | tf_op jit(solution)/shard_map/ppermute | solution.py:299
  44.1 11.9 %copy-start.1 = (f32[4,17,8,128]{3,2,1,0:T(8,128)}, f32[4,17,8,128]{3,2,1,0:T(8,128)S(1)}, u32[]{:S(2)}) copy-start(f32[4,17,8,128]{3,2,1,0:T(8,128)S(1)} %collective-permute-done.1.rest_2_) | copy-start | bytes 835588
  44.1 30.7 %collective-permute-start.6 = (f32[4,17,8,128]{3,2,1,0:T(8,128)}, f32[4,17,8,128]{3,2,1,0:T(8,128)S(1)}, u32[]{:S(2)}, u32[]{:S(2)}) collective-permute-start(f32[4,17,8,128]{3,2,1,0:T(8,128)} %get-tuple-element.17), channel_id=1, source_target_pairs={{0,7},{1,0},{2,1},{3,2},{4,3},{5,4},{6,5},{7,6},{8,15},{9,8},{10,9... | collective-permute-start | bytes 835592 | tf_op jit(solution)/shard_map/ppermute | solution.py:299
  64.4 10.4 %copy-start.2 = (f32[4,17,8,128]{3,2,1,0:T(8,128)}, f32[4,17,8,128]{3,2,1,0:T(8,128)S(1)}, u32[]{:S(2)}) copy-start(f32[4,17,8,128]{3,2,1,0:T(8,128)S(1)} %collective-permute-done.2.rest_3_) | copy-start | bytes 835588
  64.4 10.4 %copy-start.3 = (f32[4,17,8,128]{3,2,1,0:T(8,128)}, f32[4,17,8,128]{3,2,1,0:T(8,128)S(1)}, u32[]{:S(2)}) copy-start(f32[4,17,8,128]{3,2,1,0:T(8,128)S(1)} %collective-permute-done.3.rest_4_) | copy-start | bytes 835588
  64.4 10.4 %copy-start.4 = (f32[4,17,8,128]{3,2,1,0:T(8,128)}, f32[4,17,8,128]{3,2,1,0:T(8,128)S(1)}, u32[]{:S(2)}) copy-start(f32[4,17,8,128]{3,2,1,0:T(8,128)S(1)} %collective-permute-done.4.rest_5_) | copy-start | bytes 835588
  71.0 3.8 %copy-start.5 = (f32[4,17,8,128]{3,2,1,0:T(8,128)}, f32[4,17,8,128]{3,2,1,0:T(8,128)S(1)}, u32[]{:S(2)}) copy-start(f32[4,17,8,128]{3,2,1,0:T(8,128)S(1)} %collective-permute-done.5.rest_6_) | copy-start | bytes 835588
  74.8 0.7 copy-start.6
  103.2 1.3 collective-permute-start.7
  104.5 4.1 %collective-permute-start.8 = (f32[10,8,128]{2,1,0:T(8,128)S(1)}, f32[10,8,128]{2,1,0:T(8,128)S(1)}, u32[]{:S(2)}, u32[]{:S(2)}) collective-permute-start(f32[10,8,128]{2,1,0:T(8,128)S(1)} %get-tuple-element.21), channel_id=1, source_target_pairs={{0,16},{8,24},{16,0},{24,8},{32,48},{40,56},{48,32},{56,40},{64,80... | collective-permute-start | bytes 122888 | tf_op jit(solution)/shard_map/ppermute | solution.py:275
  108.6 5.5 %collective-permute-start.9 = (f32[10,8,128]{2,1,0:T(8,128)S(1)}, f32[10,8,128]{2,1,0:T(8,128)S(1)}, u32[]{:S(2)}, u32[]{:S(2)}) collective-permute-start(f32[10,8,128]{2,1,0:T(8,128)S(1)} %add.32), channel_id=1, source_target_pairs={{0,32},{8,40},{16,48},{24,56},{32,0},{40,8},{48,16},{56,24},{64,96... | collective-permute-start | bytes 122888 | tf_op jit(solution)/shard_map/ppermute | solution.py:275
  114.1 4.0 %collective-permute-start.10 = (f32[10,8,128]{2,1,0:T(8,128)S(1)}, f32[10,8,128]{2,1,0:T(8,128)S(1)}, u32[]{:S(2)}, u32[]{:S(2)}) collective-permute-start(f32[10,8,128]{2,1,0:T(8,128)S(1)} %add.33), channel_id=1, source_target_pairs={{0,64},{8,72},{16,80},{24,88},{32,96},{40,104},{48,112},{56,120},{... | collective-permute-start | bytes 122888 | tf_op jit(solution)/shard_map/ppermute | solution.py:275
  118.1 5.5 %collective-permute-start.11 = (f32[10,8,128]{2,1,0:T(8,128)S(1)}, f32[10,8,128]{2,1,0:T(8,128)S(1)}, u32[]{:S(2)}, u32[]{:S(2)}) collective-permute-start(f32[10,8,128]{2,1,0:T(8,128)S(1)} %add.34), channel_id=1, source_target_pairs={{0,128},{8,136},{16,144},{24,152},{32,160},{40,168},{48,176},{56,1... | collective-permute-start | bytes 122888 | tf_op jit(solution)/shard_map/ppermute | solution.py:275
where the time goes:
time: 146 us; the launch traced here: 145 us
  waiting for transfers between devices  38.2 us (26%)
  blocking collectives  37.6 us (26%)
  starting transfers between devices  31.1 us (21%)
  Pallas kernels  27.7 us (19%)
  local copies, waits for them, and re-layouts  7.1 us (5%)
  other arithmetic  2.24 us (2%)
  between operations  1.49 us (1%)
    ppermute x7, waiting for transfers between devices, per_device(): lax.ppermute(packed[s], 'hist', [(i, (i + s) % groups) for i in range(gro...  24.9 us
    ppermute x7, starting transfers between devices, per_device(): lax.ppermute(packed[s], 'hist', [(i, (i + s) % groups) for i in range(gro...  24 us
    all_to_all x1, blocking collectives, per_device(): arrived = lax.all_to_all(partial, 'hist', 0, 0, tiled=True)  18.9 us
    all_to_all x1, blocking collectives, per_device(): lax.all_to_all(jnp.broadcast_to(both, (groups,) + both.shape), 'hist', 0,...  18.7 us
    ppermute x5, waiting for transfers between devices, turn_sum(): lax.ppermute(value, 'turn', [(i, i ^ bit) for i in range(size)])  13.2 us
    pallas_call x1, Pallas kernels, pack(): pl.pallas_call(pack_kernel, out_shape=[jax.ShapeDtypeStruct((4, ROWS, 8,...  10.3 us
    pallas_call x1, Pallas kernels, replies(): pl.pallas_call(reply_kernel, grid=(4,), out_shape=jax.ShapeDtypeStruct((8...  8.81 us
    pallas_call x1, Pallas kernels, payoffs(): pl.pallas_call(payoff_kernel, grid=(4,), out_shape=jax.ShapeDtypeStruct((...  8.63 us
  transfers between devices with their start and end apart: 12, of which 9 were waited for; matrix products, arithmetic and copies ran while one was open for 1% of the time, Pallas kernels for 6%

commit v1 on v0

--- a/solution.py
+++ b/solution.py
@@ -15,6 +15,8 @@
 TILES = 9
 WIDE = TILES * 128
 ROWS = 17
+ORDER = (4, 3, 5, 2, 6, 1, 7, 0)
+CHUNK = 256
 VMEM_LIMIT = 56 * 1024 * 1024
 
 
@@ -83,9 +85,15 @@
     return ref[:, 128 * j : 128 * j + 128]
 
 
-def pack_kernel(scal, policy, flop_reach, turn_policy, slot_a, slot_b, *rest):
-    outs, (raw, own, low) = rest[:8], rest[8:]
-    me, t = scal[0], scal[1]
+def cards_of(table, j):
+    return [jnp.broadcast_to(table[i : i + 1, 128 * j : 128 * j + 128], (8, 128)) for i in range(2)]
+
+
+def pack_kernel(first, turn_card, river_card, policy_hbm, flop_reach, turn_policy, table, *rest):
+    outs, (policy, staged, raw, own, low, in_sem, out_sem) = (rest[:1] if first else rest[1:8]), rest[-7:]
+    fetch = pltpu.make_async_copy(policy_hbm, policy, in_sem)
+    fetch.start()
+    me, t = lax.axis_index("hist"), turn_card[0]
     lane = lanes_of((8, 128))
     reach = flop_reach[...] * (turn_policy[...].astype(jnp.float32) * (1.0 / 256.0)) * (1.0 / 256.0)
     reach = jnp.concatenate([reach, jnp.zeros((16, 1408 - HANDS), jnp.float32)], axis=1)
@@ -100,8 +108,8 @@
         low[p] = jnp.where(wide < 95, moved, 0.0)[:, :128]
 
     def one_river(out, rl, river):
-        r = scal[2 + river]
-        index = [source_lanes(tile(slot_a, j), tile(slot_b, j), t, r) for j in range(TILES)]
+        r = river_card[0, river]
+        index = [source_lanes(*cards_of(table, j), t, r) for j in range(TILES)]
         tails = []
         for p in range(2):
 
@@ -130,36 +138,56 @@
                     tails.append(value)
         out[rl, 16] = tails[0] + pltpu.roll(tails[1], 64, 1)
 
-    for s in range(8):
-        group = (me + s) & 7
-
-        @pl.loop(0, 4)
-        def _(rl, out=outs[s], group=group):
-            one_river(out, rl, group * 4 + rl)
-
-
-def pack(scal, policy, flop_reach, turn_policy, slot_a, slot_b):
+    fetch.wait()
+    stores = [pltpu.make_async_copy(staged.at[i], out, out_sem.at[i]) for i, out in enumerate(outs)]
+
+    @pl.loop(0, 2 * len(outs))
+    def _(step):
+        i, rl = step >> 1, 2 * (step & 1)
+        shift = 4 if first else jnp.where((i & 1) == 1, 5 + (i >> 1), 3 - (i >> 1))
+        river = ((me + shift) & 7) * 4 + rl
+        one_river(staged.at[i], rl, river)
+        one_river(staged.at[i], rl + 1, river + 1)
+        for k, store in enumerate(stores):
+
+            @pl.when(step == 2 * k + 1)
+            def _(store=store):
+                store.start()
+
+    for store in stores:
+        store.wait()
+
+
+def pack(turn_cards, river_cards, policy, flop_reach, turn_policy, table, after):
+    count = 7 if after else 1
     smem = pl.BlockSpec(memory_space=pltpu.SMEM)
     vmem = pl.BlockSpec(memory_space=pltpu.VMEM)
+    anywhere = pl.BlockSpec(memory_space=pl.ANY)
+    message = (4, ROWS, 8, 128)
     return pl.pallas_call(
-        pack_kernel,
-        out_shape=[jax.ShapeDtypeStruct((4, ROWS, 8, 128), jnp.float32)] * 8,
-        in_specs=[smem] + [vmem] * 5,
-        out_specs=[vmem] * 8,
+        functools.partial(pack_kernel, not after),
+        out_shape=[jax.ShapeDtypeStruct(message, jnp.float32)] * count,
+        in_specs=[smem] * 2 + [anywhere] + [vmem] * 3 + [anywhere] * len(after),
+        out_specs=[anywhere] * count,
         scratch_shapes=[
+            pltpu.VMEM((5304, 128), jnp.int32),
+            pltpu.VMEM((count,) + message, jnp.float32),
             pltpu.VMEM((176, 128), jnp.float32),
             pltpu.VMEM((2, 8, WIDE), jnp.float32),
             pltpu.VMEM((2, 8, 128), jnp.float32),
+            pltpu.SemaphoreType.DMA,
+            pltpu.SemaphoreType.DMA((count,)),
         ],
         compiler_params=pltpu.CompilerParams(vmem_limit_bytes=VMEM_LIMIT),
+        cost_estimate=pl.CostEstimate(flops=3000000, bytes_accessed=4000000, transcendentals=0),
         name="pack",
-    )(scal, policy, flop_reach, turn_policy, slot_a, slot_b)
-
-
-def payoff_kernel(scal, ranks, compat, slot_a, slot_b, out, rows, strip):
+    )(turn_cards, river_cards, policy, flop_reach, turn_policy, table, *after)
+
+
+def payoff_kernel(turn_card, river_card, ranks, compat, table, after, out, rows, strip):
     rl = pl.program_id(0)
-    t = scal[1]
-    r = scal[2 + 4 * scal[0] + rl]
+    t = turn_card[0]
+    r = river_card[0, 4 * lax.axis_index("hist") + rl]
     raw = ranks[...]
     value = (128 + (raw & 127)).astype(jnp.float32)
     for bit in range(6):
@@ -170,16 +198,19 @@
     plain = pltpu.roll(row, 1408 - BASE, 1)
     source = pltpu.roll(row, 1408 - LOW, 1)[:, :128]
     for j in range(TILES):
-        index = source_lanes(tile(slot_a, j), tile(slot_b, j), t, r)
+        index = source_lanes(*cards_of(table, j), t, r)
         taken = pick(source, jnp.maximum(index, 0))
         strip[:, 128 * j : 128 * j + 128] = jnp.where(index >= 0, taken, plain[:, 128 * j : 128 * j + 128])
     across = [
         jnp.broadcast_to(strip[0:1, 128 * j : 128 * j + 128], (128, 128)).astype(jnp.bfloat16)
         for j in range(TILES)
     ]
+    code = jnp.where(lax.broadcasted_iota(jnp.int32, (8, WIDE), 0) == 0, strip[...], 0.0).astype(jnp.bfloat16)
+    column = lax.dot_general(
+        code, jnp.ones((8, 128), jnp.bfloat16), (((0,), (0,)), ((), ())), preferred_element_type=jnp.float32
+    ).astype(jnp.bfloat16)
     for i in range(TILES):
-        down = jnp.transpose(jnp.broadcast_to(strip[0:1, 128 * i : 128 * i + 128], (128, 128)))
-        down = down.astype(jnp.bfloat16)
+        down = column[128 * i : 128 * i + 128]
         for j in range(TILES):
             mask = compat[128 * i : 128 * i + 128, 128 * j : 128 * j + 128]
             out[0, 128 * i : 128 * i + 128, 128 * j : 128 * j + 128] = jnp.minimum(
@@ -187,27 +218,27 @@
             )
 
 
-def payoffs(scal, ranks, compat, slot_a, slot_b):
+def payoffs(turn_cards, river_cards, ranks, compat, table, after):
     smem = pl.BlockSpec(memory_space=pltpu.SMEM)
     vmem = pl.BlockSpec(memory_space=pltpu.VMEM)
     return pl.pallas_call(
         payoff_kernel,
         grid=(4,),
         out_shape=jax.ShapeDtypeStruct((4, WIDE, WIDE), jnp.bfloat16),
-        in_specs=[smem] + [vmem] * 4,
+        in_specs=[smem] * 2 + [vmem] * 3 + [pl.BlockSpec(memory_space=pl.ANY)],
         out_specs=pl.BlockSpec((1, WIDE, WIDE), lambda i: (i, 0, 0)),
         scratch_shapes=[pltpu.VMEM((8, 1408), jnp.float32), pltpu.VMEM((8, WIDE), jnp.float32)],
         compiler_params=pltpu.CompilerParams(vmem_limit_bytes=VMEM_LIMIT),
         cost_estimate=pl.CostEstimate(flops=4 * 4 * WIDE * WIDE, bytes_accessed=10 * WIDE * WIDE, transcendentals=0),
         name="payoff",
-    )(scal, ranks, compat, slot_a, slot_b)
-
-
-def reply_kernel(scal, payoff, select, scale, slot_a, slot_b, *rest):
-    blocks, out, high, rest_low = rest[:8], rest[8], rest[9], rest[10]
+    )(turn_cards, river_cards, ranks, compat, table, after)
+
+
+def reply_kernel(turn_card, river_card, payoff, select, scale, table, *rest):
+    blocks, (out, high, fine) = rest[:8], rest[8:]
     rl = pl.program_id(0)
-    t = scal[1]
-    r = scal[2 + 4 * scal[0] + rl]
+    t = turn_card[0]
+    r = river_card[0, 4 * lax.axis_index("hist") + rl]
     lane = lanes_of((8, 128))
     for s in range(8):
         for j in range(TILES):
@@ -219,40 +250,47 @@
             both = jnp.concatenate(pair, axis=0)
             upper = both.astype(jnp.bfloat16)
             high[16 * s : 16 * s + 16, 128 * j : 128 * j + 128] = upper
-            rest_low[16 * s : 16 * s + 16, 128 * j : 128 * j + 128] = (
+            fine[16 * s : 16 * s + 16, 128 * j : 128 * j + 128] = (
                 both - upper.astype(jnp.float32)
             ).astype(jnp.bfloat16)
     dot = functools.partial(jnp.dot, preferred_element_type=jnp.float32)
     chosen = jnp.concatenate(
-        [dot(select[...], high[...]).astype(jnp.bfloat16), dot(select[...], rest_low[...]).astype(jnp.bfloat16)],
+        [dot(select[...], high[...]).astype(jnp.bfloat16), dot(select[...], fine[...]).astype(jnp.bfloat16)],
         axis=0,
     )
-    value = dot(chosen, payoff[0])
-    value = (value[:128] + value[128:]) * scale[...]
-    reply = jnp.maximum(value[:64], value[64:])
 
     @pl.when(rl == 0)
     def _():
         out[...] = jnp.zeros_like(out)
 
     home = home_slots(lane, t, r)
-    for j in range(TILES):
-        moved = source_lanes(tile(slot_a, j), tile(slot_b, j), t, r) >= 0
-        for g in range(8):
-            part = reply[8 * g : 8 * g + 8, 128 * j : 128 * j + 128]
-            out[g, 1 + j] += jnp.where(moved, 0.0, part)
-            out[g, 0] += jnp.where((home >> 7) == j, pick(part, home & 127), 0.0)
-
-
-def replies(scal, payoff, select, scale, slot_a, slot_b, blocks):
+    home_tile, home_lane = home >> 7, home & 127
+    first = [jnp.zeros((8, 128), jnp.float32)] * 8
+    for start in range(0, WIDE, CHUNK):
+        value = dot(chosen, payoff[0, :, start : start + CHUNK])
+        value = (value[:128] + value[128:]) * scale[...]
+        reply = jnp.maximum(value[:64], value[64:])
+        for j in range(start // 128, min(start + CHUNK, WIDE) // 128):
+            moved = source_lanes(*cards_of(table, j), t, r) >= 0
+            for g in range(8):
+                part = reply[8 * g : 8 * g + 8, 128 * j - start : 128 * j - start + 128]
+                out[g, 1 + j] += jnp.where(moved, 0.0, part)
+                first[g] = jnp.where(home_tile == j, pick(part, home_lane), first[g])
+    for g in range(8):
+        out[g, 0] += first[g]
+
+
+def replies(turn_cards, river_cards, payoff, select, scale, table, blocks):
     smem = pl.BlockSpec(memory_space=pltpu.SMEM)
     vmem = pl.BlockSpec(memory_space=pltpu.VMEM)
-    block = pl.BlockSpec((1, ROWS, 8, 128), lambda i: (i, 0, 0, 0))
     return pl.pallas_call(
         reply_kernel,
         grid=(4,),
         out_shape=jax.ShapeDtypeStruct((8, TILES + 1, 8, 128), jnp.float32),
-        in_specs=[smem, pl.BlockSpec((1, WIDE, WIDE), lambda i: (i, 0, 0))] + [vmem] * 4 + [block] * 8,
+        in_specs=[smem] * 2
+        + [pl.BlockSpec((1, WIDE, WIDE), lambda i: (i, 0, 0))]
+        + [vmem] * 3
+        + [pl.BlockSpec((1, ROWS, 8, 128), lambda i: (i, 0, 0, 0))] * 8,
         out_specs=vmem,
         scratch_shapes=[pltpu.VMEM((128, WIDE), jnp.bfloat16)] * 2,
         compiler_params=pltpu.CompilerParams(vmem_limit_bytes=VMEM_LIMIT),
@@ -260,7 +298,7 @@
             flops=4 * 2 * 256 * WIDE * WIDE, bytes_accessed=8 * WIDE * WIDE, transcendentals=0
         ),
         name="reply",
-    )(scal, payoff, select, scale, slot_a, slot_b, *blocks)
+    )(turn_cards, river_cards, payoff, select, scale, table, *blocks)
 
 
 def flat(nodes):
@@ -270,10 +308,19 @@
 
 
 def turn_sum(value, size):
-    bit = 1
-    while bit < size:
-        value = value + lax.ppermute(value, "turn", [(i, i ^ bit) for i in range(size)])
-        bit *= 2
+    value = value + lax.ppermute(value, "turn", [(i, i ^ 1) for i in range(size)])
+    step = 2
+    while step < size:
+        near = [
+            lax.ppermute(
+                value,
+                "turn",
+                [(i, i - i % (4 * step) + (i + s * step) % (4 * step)) for i in range(size)],
+            )
+            for s in (1, 2, 3)
+        ]
+        value = (value + near[1]) + (near[0] + near[2])
+        step *= 4
     return value
 
 
@@ -281,32 +328,28 @@
     groups = lax.axis_size("hist")
     turns = lax.axis_size("turn")
     me = lax.axis_index("hist")
-    a, b = slot_cards()
-    slot_a = jnp.asarray(np.broadcast_to(a, (8, WIDE)))
-    slot_b = jnp.asarray(np.broadcast_to(b, (8, WIDE)))
+    table = jnp.asarray(np.stack(slot_cards()))
     compat = jnp.asarray(compat_table(), jnp.bfloat16)
-    scal = jnp.concatenate([me.reshape(1).astype(jnp.int32), turn_cards, river_cards[0]])
-    packed = pack(
-        scal,
-        river_policy.reshape(5304, 128),
-        jnp.transpose(flop_reach),
-        jnp.transpose(turn_policy[0]),
-        slot_a,
-        slot_b,
-    )
-    blocks = [packed[0]]
-    for s in range(1, groups):
-        blocks.append(lax.ppermute(packed[s], "hist", [(i, (i + s) % groups) for i in range(groups)]))
-    payoff = payoffs(scal, hand_rank[0], compat, slot_a, slot_b)
+    policy = river_policy.reshape(5304, 128)
+    common = (turn_cards, river_cards, policy, jnp.transpose(flop_reach), jnp.transpose(turn_policy[0]), table)
+
+    def send(block, s):
+        return lax.ppermute(block, "hist", [(i, (i + s) % groups) for i in range(groups)])
+
+    packed = pack(*common, [])
+    packed += pack(*common, packed)
+    got = [send(block, s) if s else block for block, s in zip(packed, ORDER)]
+    payoff = payoffs(turn_cards, river_cards, hand_rank[0], compat, table, packed[1])
     child = jnp.transpose(children).reshape(128)
-    place = (((me - (child >> 4)) & 7) << 4) + ((child & 1) << 3) + ((child >> 1) & 7)
+    turn_of = jnp.zeros((8,), jnp.int32).at[jnp.array(ORDER)].set(jnp.arange(8, dtype=jnp.int32))
+    place = (turn_of[(me - (child >> 4)) & 7] << 4) + ((child & 1) << 3) + ((child >> 1) & 7)
     select = (place[:, None] == jnp.arange(128)[None, :]).astype(jnp.bfloat16)
     scale = jnp.sum(
         jnp.where(child[:, None] == jnp.arange(128)[None, :], pot.astype(jnp.float32)[None, :], 0.0),
         axis=1,
         keepdims=True,
     )
-    partial = replies(scal, payoff, select, scale, slot_a, slot_b, blocks)
+    partial = replies(turn_cards, river_cards, payoff, select, scale, table, got)
     arrived = lax.all_to_all(partial, "hist", 0, 0, tiled=True)
     value = jnp.sum(arrived, axis=0) * (1.0 / 32.0)
     mean = turn_sum(value, turns) * (1.0 / turns)

time: 146 us -> 133 us (0.911)
  waiting for transfers between devices: 38.2 us -> 30.2 us
  starting transfers between devices: 31.1 us -> 28.1 us
  local copies, waits for them, and re-layouts: 7.1 us -> 4.67 us
    ppermute x12 -> x14, waiting for transfers between devices: 38.2 us -> 30.2 us  [the longest x7 19.4 us: send(): lax.ppermute(block, 'hist', [(i, (i + s) % groups) for i in range(groups)])]
    ppermute x12 -> x14, starting transfers between devices: 31.1 us -> 28.1 us  [the longest x7 19.7 us: send(): lax.ppermute(block, 'hist', [(i, (i + s) % groups) for i in range(groups)])]
    another operation x3 -> x1, local copies, waits for them, and re-layouts: 2.63 us -> 0.01 us
    all_to_all x1, blocking collectives: 18.7 us -> 20.2 us  [per_device(): lax.all_to_all(jnp.broadcast_to(both, (groups,) + both.shape), 'hist', 0,...]
    pallas_call x1 -> x2, Pallas kernels: 10.3 us -> 11.2 us  [pack(): pl.pallas_call(functools.partial(pack_kernel, not after), out_shape=[jax....]
  transfers between devices with their start and end apart: 12 -> 14, of which waited for: 9 -> 8; matrix products, arithmetic and copies ran while one was open for 1% -> 1% of each run, Pallas kernels for 6% -> 12%
where the time goes in v1:
time: 133 us
  blocking collectives  39 us (29%)
  waiting for transfers between devices  30.2 us (23%)
  Pallas kernels  28.5 us (21%)
  starting transfers between devices  28.1 us (21%)
  local copies, waits for them, and re-layouts  4.67 us (4%)
  between operations  1.48 us (1%)
    all_to_all x1, blocking collectives, per_device(): lax.all_to_all(jnp.broadcast_to(both, (groups,) + both.shape), 'hist', 0,...  20.2 us
    ppermute x7, starting transfers between devices, send(): lax.ppermute(block, 'hist', [(i, (i + s) % groups) for i in range(groups)])  19.7 us
    ppermute x7, waiting for transfers between devices, send(): lax.ppermute(block, 'hist', [(i, (i + s) % groups) for i in range(groups)])  19.4 us
    all_to_all x1, blocking collectives, per_device(): arrived = lax.all_to_all(partial, 'hist', 0, 0, tiled=True)  18.8 us
    pallas_call x2, Pallas kernels, pack(): pl.pallas_call(functools.partial(pack_kernel, not after), out_shape=[jax....  11.2 us
    ppermute x6, waiting for transfers between devices, turn_sum(): lax.ppermute(value, 'turn', [(i, i - i % (4 * step) + (i + s * step) % (4...  9.55 us
    pallas_call x1, Pallas kernels, replies(): pl.pallas_call(reply_kernel, grid=(4,), out_shape=jax.ShapeDtypeStruct((8...  8.94 us
    pallas_call x1, Pallas kernels, payoffs(): pl.pallas_call(payoff_kernel, grid=(4,), out_shape=jax.ShapeDtypeStruct((...  8.43 us
  transfers between devices with their start and end apart: 14, of which 8 were waited for; matrix products, arithmetic and copies ran while one was open for 1% of the time, Pallas kernels for 12%

profile of v1, /device:TPU:6, one launch (start us, length us, event | category | flops | bytes accessed | tf_op | source)
XLA Modules:
  0.0 133.0 jit_solution(9108025447190912390)
XLA Ops:
  1.3 4.0 %pack.2.rest_0_ = f32[4,17,8,128]{3,2,1,0:T(8,128)} custom-call(s32[1]{0:T(128)S(6)} %copy.34.turn_card, s32[1,32]{1,0:T(1,128)} %river_card.7, s32[5304,128]{1,0:T(8,128)} %bitcast.59, f32[16,1326]{1,0:T(8,128)} %bitcast.63, s32[16,1326]{1,0:T(8,128)} %bitcast.65, s32[2,1152]{1,0:T(2,128)} %constant.9.clone.table), custom_call_target="tpu_custom_call" | custom-call | flops 3000000 | bytes 4000000 | tf_op jit(solution)/shard_map/pack/pallas_call | solution.py:167
  5.3 7.3 %collective-permute-start = (f32[4,17,8,128]{3,2,1,0:T(8,128)}, f32[4,17,8,128]{3,2,1,0:T(8,128)S(1)}, u32[]{:S(2)}, u32[]{:S(2)}) collective-permute-start(f32[4,17,8,128]{3,2,1,0:T(8,128)} %pack.2.rest_0_), channel_id=1, source_target_pairs={{0,4},{1,5},{2,6},{3,7},{4,0},{5,1},{6,2},{7,3},{8,12},{9,13},{10,... | collective-permute-start | bytes 835592 | tf_op jit(solution)/shard_map/ppermute | solution.py:337
  12.5 7.2 %pack.3 = (f32[4,17,8,128]{3,2,1,0:T(8,128)}, f32[4,17,8,128]{3,2,1,0:T(8,128)}, f32[4,17,8,128]{3,2,1,0:T(8,128)}, f32[4,17,8,128]{3,2,1,0:T(8,128)}, f32[4,17,...) custom-call(s32[1]{0:T(128)S(6)} %copy.34.turn_card, s32[1,32]{1,0:T(1,128)} %river_card.7, ...), custom_call_target="tpu_custom_call" | custom-call | flops 3000000 | bytes 4000000 | tf_op jit(solution)/shard_map/pack/pallas_call | solution.py:167
  19.8 2.0 %collective-permute-start.1 = (f32[4,17,8,128]{3,2,1,0:T(8,128)}, f32[4,17,8,128]{3,2,1,0:T(8,128)S(1)}, u32[]{:S(2)}, u32[]{:S(2)}) collective-permute-start(f32[4,17,8,128]{3,2,1,0:T(8,128)} %get-tuple-element.9.after), channel_id=1, source_target_pairs={{0,3},{1,4},{2,5},{3,6},{4,7},{5,0},{6,1},{7,2},{8,11},{9,12},{10,... | collective-permute-start | bytes 835592 | tf_op jit(solution)/shard_map/ppermute | solution.py:337
  21.8 3.1 %collective-permute-start.2 = (f32[4,17,8,128]{3,2,1,0:T(8,128)}, f32[4,17,8,128]{3,2,1,0:T(8,128)S(1)}, u32[]{:S(2)}, u32[]{:S(2)}) collective-permute-start(f32[4,17,8,128]{3,2,1,0:T(8,128)} %get-tuple-element.10), channel_id=1, source_target_pairs={{0,5},{1,6},{2,7},{3,0},{4,1},{5,2},{6,3},{7,4},{8,13},{9,14},{10,... | collective-permute-start | bytes 835592 | tf_op jit(solution)/shard_map/ppermute | solution.py:337
  24.9 1.5 %collective-permute-start.3 = (f32[4,17,8,128]{3,2,1,0:T(8,128)}, f32[4,17,8,128]{3,2,1,0:T(8,128)S(1)}, u32[]{:S(2)}, u32[]{:S(2)}) collective-permute-start(f32[4,17,8,128]{3,2,1,0:T(8,128)} %get-tuple-element.11), channel_id=1, source_target_pairs={{0,2},{1,3},{2,4},{3,5},{4,6},{5,7},{6,0},{7,1},{8,10},{9,11},{10,... | collective-permute-start | bytes 835592 | tf_op jit(solution)/shard_map/ppermute | solution.py:337
  26.4 2.7 %collective-permute-start.4 = (f32[4,17,8,128]{3,2,1,0:T(8,128)}, f32[4,17,8,128]{3,2,1,0:T(8,128)S(1)}, u32[]{:S(2)}, u32[]{:S(2)}) collective-permute-start(f32[4,17,8,128]{3,2,1,0:T(8,128)} %get-tuple-element.12), channel_id=1, source_target_pairs={{0,6},{1,7},{2,0},{3,1},{4,2},{5,3},{6,4},{7,5},{8,14},{9,15},{10,... | collective-permute-start | bytes 835592 | tf_op jit(solution)/shard_map/ppermute | solution.py:337
  29.0 0.1 reshape.84
  29.1 0.1 and.29
  29.2 18.9 %collective-permute-done.1.rest_1_ = f32[4,17,8,128]{3,2,1,0:T(8,128)S(1)} collective-permute-done((f32[4,17,8,128]{3,2,1,0:T(8,128)}, f32[4,17,8,128]{3,2,1,0:T(8,128)S(1)}, u32[]{:S(2)}, u32[]{:S(2)}) %collective-permute-start.1) | collective-permute-done | bytes 278560 | tf_op jit(solution)/shard_map/ppermute | solution.py:337
  48.1 0.0 collective-permute-start.5
  48.1 0.0 collective-permute-done.2.rest_2_
  48.1 3.2 %collective-permute-start.6 = (f32[4,17,8,128]{3,2,1,0:T(8,128)}, f32[4,17,8,128]{3,2,1,0:T(8,128)S(1)}, u32[]{:S(2)}, u32[]{:S(2)}) collective-permute-start(f32[4,17,8,128]{3,2,1,0:T(8,128)} %get-tuple-element.14), channel_id=1, source_target_pairs={{0,7},{1,0},{2,1},{3,2},{4,3},{5,4},{6,5},{7,6},{8,15},{9,8},{10,9... | collective-permute-start | bytes 835592 | tf_op jit(solution)/shard_map/ppermute | solution.py:337
  51.3 0.2 select_reduce_fusion
  51.5 0.8 copy.23.scale
  52.3 8.4 %payoff.1 = bf16[4,1152,1152]{2,1,0:T(8,128)(2,1)} custom-call(s32[1]{0:T(128)S(6)} %copy.34.turn_card, s32[1,32]{1,0:T(1,128)} %river_card.7, s32[4,1326]{1,0:T(4,128)} %bitcast.67, bf16[1152,1152]{1,0:T(8,128)(2,1)} %constant.10.clone.compat, s32[2,1152]{1,0:T(2,128)} %constant.9.clone.table, f32[4,17,8,128]{3,2,1,0:T(8,128)} %get-tuple-element.9.after), custom_call_target="tpu_custom_call" | custom-call | flops 21233664 | bytes 13271040 | tf_op jit(solution)/shard_map/payoff/pallas_call | solution.py:224
  60.7 0.7 fusion.select
  61.4 0.0 collective-permute-done.3.rest_3_
  61.4 0.0 collective-permute-done.4.rest_4_
  61.4 0.0 collective-permute-done.5.rest_5_
  61.4 0.5 collective-permute-done.6.rest_6_
  62.0 0.0 collective-permute-done.rest_0_
  62.0 0.1 copy-done.3
  62.1 0.1 copy-done.4
  62.2 0.1 copy-done.5
  62.3 0.4 copy-done.6
  62.7 0.1 copy-done
  62.8 8.9 %reply.1 = f32[8,10,8,128]{3,2,1,0:T(8,128)} custom-call(s32[1]{0:T(128)S(6)} %copy.34.turn_card, s32[1,32]{1,0:T(1,128)} %river_card.7, bf16[4,1152,1152]{2,1,0:T(8,128)(2,1)} %payoff.1, bf16[128,128]{1,0:T(8,128)(2,1)} %fusion.select, f32[128,1]{1,0:T(8,128)} %copy.23.scale, s32[2,1152]{1,0:T(2,128)} %constant.9.clone.table, f32[4,17,8,128]{3,2,1,0:T(8,128)} %copy-done, ...), custom_call_target="tpu_custom_call" | custom-call | flops 2717908992 | bytes 10616832 | tf_op jit(solution)/shard_map/reply/pallas_call | solution.py:286
  71.7 18.8 %all_to_all.10 = f32[8,10,8,128]{3,2,1,0:T(8,128)S(1)} all-to-all(f32[8,10,8,128]{3,2,1,0:T(8,128)} %reply.1), channel_id=1, replica_groups=mesh['turn'=32,'hist'=8] {'hist'}, dimensions={0} | all-to-all | bytes 655360 | tf_op jit(solution)/shard_map/all_to_all | solution.py:353
  90.6 0.1 collective-permute-start.7
  90.7 1.2 collective-permute-done.7
  91.9 3.1 %collective-permute-start.10 = (f32[10,8,128]{2,1,0:T(8,128)S(1)}, f32[10,8,128]{2,1,0:T(8,128)S(1)}, u32[]{:S(2)}, u32[]{:S(2)}) collective-permute-start(f32[10,8,128]{2,1,0:T(8,128)S(1)} %get-tuple-element.19), channel_id=1, source_target_pairs={{0,48},{8,56},{16,0},{24,8},{32,16},{40,24},{48,32},{56,40},{64,11... | collective-permute-start | bytes 122888 | tf_op jit(solution)/shard_map/ppermute | solution.py:315
  95.0 0.6 collective-permute-start.8
  95.6 1.0 collective-permute-start.9
  96.6 0.3 collective-permute-done.10
  96.9 3.6 %collective-permute-done.8 = f32[10,8,128]{2,1,0:T(8,128)S(1)} collective-permute-done((f32[10,8,128]{2,1,0:T(8,128)S(1)}, f32[10,8,128]{2,1,0:T(8,128)S(1)}, u32[]{:S(2)}, u32[]{:S(2)}) %collective-permute-start.8) | collective-permute-done | bytes 40992 | tf_op jit(solution)/shard_map/ppermute | solution.py:315
  100.5 0.4 collective-permute-done.9
  100.9 1.5 %collective-permute-start.11 = (f32[10,8,128]{2,1,0:T(8,128)S(1)}, f32[10,8,128]{2,1,0:T(8,128)S(1)}, u32[]{:S(2)}, u32[]{:S(2)}) collective-permute-start(f32[10,8,128]{2,1,0:T(8,128)S(1)} %add_add_fusion), channel_id=1, source_target_pairs={{0,128},{8,136},{16,144},{24,152},{32,160},{40,168},{48,176},{56,1... | collective-permute-start | bytes 122888 | tf_op jit(solution)/shard_map/ppermute | solution.py:315
  102.4 2.1 %collective-permute-start.12 = (f32[10,8,128]{2,1,0:T(8,128)S(1)}, f32[10,8,128]{2,1,0:T(8,128)S(1)}, u32[]{:S(2)}, u32[]{:S(2)}) collective-permute-start(f32[10,8,128]{2,1,0:T(8,128)S(1)} %add_add_fusion), channel_id=1, source_target_pairs={{0,64},{8,72},{16,80},{24,88},{32,96},{40,104},{48,112},{56,120},{... | collective-permute-start | bytes 122888 | tf_op jit(solution)/shard_map/ppermute | solution.py:315
  104.5 0.0 collective-permute-start.13
  104.5 2.0 %collective-permute-done.11 = f32[10,8,128]{2,1,0:T(8,128)S(1)} collective-permute-done((f32[10,8,128]{2,1,0:T(8,128)S(1)}, f32[10,8,128]{2,1,0:T(8,128)S(1)}, u32[]{:S(2)}, u32[]{:S(2)}) %collective-permute-start.11) | collective-permute-done | bytes 40992 | tf_op jit(solution)/shard_map/ppermute | solution.py:315
  106.5 3.2 %collective-permute-done.13 = f32[10,8,128]{2,1,0:T(8,128)S(1)} collective-permute-done((f32[10,8,128]{2,1,0:T(8,128)S(1)}, f32[10,8,128]{2,1,0:T(8,128)S(1)}, u32[]{:S(2)}, u32[]{:S(2)}) %collective-permute-start.13) | collective-permute-done | bytes 40992 | tf_op jit(solution)/shard_map/ppermute | solution.py:315
  109.8 20.2 %all_to_all.11 = f32[8,2,10,8,128]{4,3,2,1,0:T(8,128)S(1)} all-to-all(f32[8,2,10,8,128]{4,3,2,1,0:T(8,128)S(1)} %broadcast_in_dim.30), channel_id=1, replica_groups=mesh['turn'=32,'hist'=8] {'hist'}, dimensions={0} | all-to-all | bytes 1310720 | tf_op jit(solution)/shard_map/all_to_all | solution.py:357
  130.0 0.1 copy_bitcast_fusion
  130.2 0.2 concatenate.7
  130.4 1.0 reshape.89
  131.4 0.2 concatenate.6
  131.6 1.3 %reshape_reshape.3 = f32[1,84864]{1,0:T(1,128)} reshape(f32[64,1326]{1,0:T(8,128)S(1)} %concatenate.6) | data formatting | bytes 678912 | tf_op jit(solution)/shard_map/reshape;reshape | solution.py:358
  (30 shorter events, 0.3 us)
Async XLA Ops:
  1.3 27.7 %copy-start.7 = (s32[64,2]{0,1:T(2,128)S(1)}, s32[64,2]{0,1:T(2,128)}, u32[]{:S(2)}) copy-start(s32[64,2]{0,1:T(2,128)} %param.17) | copy-start | bytes 1540
  1.3 27.8 %copy-start.8 = (s32[128]{0:T(128)S(1)}, s32[128]{0:T(128)}, u32[]{:S(2)}) copy-start(s32[128]{0:T(128)} %param.18) | copy-start | bytes 1540
  5.3 56.7 %collective-permute-start = (f32[4,17,8,128]{3,2,1,0:T(8,128)}, f32[4,17,8,128]{3,2,1,0:T(8,128)S(1)}, u32[]{:S(2)}, u32[]{:S(2)}) collective-permute-start(f32[4,17,8,128]{3,2,1,0:T(8,128)} %pack.2.rest_0_), channel_id=1, source_target_pairs={{0,4},{1,5},{2,6},{3,7},{4,0},{5,1},{6,2},{7,3},{8,12},{9,13},{10,... | collective-permute-start | bytes 835592 | tf_op jit(solution)/shard_map/ppermute | solution.py:337
  19.8 28.3 %collective-permute-start.1 = (f32[4,17,8,128]{3,2,1,0:T(8,128)}, f32[4,17,8,128]{3,2,1,0:T(8,128)S(1)}, u32[]{:S(2)}, u32[]{:S(2)}) collective-permute-start(f32[4,17,8,128]{3,2,1,0:T(8,128)} %get-tuple-element.9.after), channel_id=1, source_target_pairs={{0,3},{1,4},{2,5},{3,6},{4,7},{5,0},{6,1},{7,2},{8,11},{9,12},{10,... | collective-permute-start | bytes 835592 | tf_op jit(solution)/shard_map/ppermute | solution.py:337
  21.8 26.3 %collective-permute-start.2 = (f32[4,17,8,128]{3,2,1,0:T(8,128)}, f32[4,17,8,128]{3,2,1,0:T(8,128)S(1)}, u32[]{:S(2)}, u32[]{:S(2)}) collective-permute-start(f32[4,17,8,128]{3,2,1,0:T(8,128)} %get-tuple-element.10), channel_id=1, source_target_pairs={{0,5},{1,6},{2,7},{3,0},{4,1},{5,2},{6,3},{7,4},{8,13},{9,14},{10,... | collective-permute-start | bytes 835592 | tf_op jit(solution)/shard_map/ppermute | solution.py:337
  24.9 36.5 %collective-permute-start.3 = (f32[4,17,8,128]{3,2,1,0:T(8,128)}, f32[4,17,8,128]{3,2,1,0:T(8,128)S(1)}, u32[]{:S(2)}, u32[]{:S(2)}) collective-permute-start(f32[4,17,8,128]{3,2,1,0:T(8,128)} %get-tuple-element.11), channel_id=1, source_target_pairs={{0,2},{1,3},{2,4},{3,5},{4,6},{5,7},{6,0},{7,1},{8,10},{9,11},{10,... | collective-permute-start | bytes 835592 | tf_op jit(solution)/shard_map/ppermute | solution.py:337
  26.4 35.0 %collective-permute-start.4 = (f32[4,17,8,128]{3,2,1,0:T(8,128)}, f32[4,17,8,128]{3,2,1,0:T(8,128)S(1)}, u32[]{:S(2)}, u32[]{:S(2)}) collective-permute-start(f32[4,17,8,128]{3,2,1,0:T(8,128)} %get-tuple-element.12), channel_id=1, source_target_pairs={{0,6},{1,7},{2,0},{3,1},{4,2},{5,3},{6,4},{7,5},{8,14},{9,15},{10,... | collective-permute-start | bytes 835592 | tf_op jit(solution)/shard_map/ppermute | solution.py:337
  48.1 12.6 %copy-start.1 = (f32[4,17,8,128]{3,2,1,0:T(8,128)}, f32[4,17,8,128]{3,2,1,0:T(8,128)S(1)}, u32[]{:S(2)}) copy-start(f32[4,17,8,128]{3,2,1,0:T(8,128)S(1)} %collective-permute-done.1.rest_1_) | copy-start | bytes 835588
  48.1 13.3 %collective-permute-start.5 = (f32[4,17,8,128]{3,2,1,0:T(8,128)}, f32[4,17,8,128]{3,2,1,0:T(8,128)S(1)}, u32[]{:S(2)}, u32[]{:S(2)}) collective-permute-start(f32[4,17,8,128]{3,2,1,0:T(8,128)} %get-tuple-element.13), channel_id=1, source_target_pairs={{0,1},{1,2},{2,3},{3,4},{4,5},{5,6},{6,7},{7,0},{8,9},{9,10},{10,1... | collective-permute-start | bytes 835592 | tf_op jit(solution)/shard_map/ppermute | solution.py:337
  48.1 12.6 %copy-start.2 = (f32[4,17,8,128]{3,2,1,0:T(8,128)}, f32[4,17,8,128]{3,2,1,0:T(8,128)S(1)}, u32[]{:S(2)}) copy-start(f32[4,17,8,128]{3,2,1,0:T(8,128)S(1)} %collective-permute-done.2.rest_2_) | copy-start | bytes 835588
  48.1 13.9 %collective-permute-start.6 = (f32[4,17,8,128]{3,2,1,0:T(8,128)}, f32[4,17,8,128]{3,2,1,0:T(8,128)S(1)}, u32[]{:S(2)}, u32[]{:S(2)}) collective-permute-start(f32[4,17,8,128]{3,2,1,0:T(8,128)} %get-tuple-element.14), channel_id=1, source_target_pairs={{0,7},{1,0},{2,1},{3,2},{4,3},{5,4},{6,5},{7,6},{8,15},{9,8},{10,9... | collective-permute-start | bytes 835592 | tf_op jit(solution)/shard_map/ppermute | solution.py:337
  61.4 0.7 copy-start.3
  61.4 0.8 copy-start.4
  61.4 0.9 copy-start.5
  62.0 0.7 copy-start.6
  62.0 0.8 copy-start
  90.6 1.3 collective-permute-start.7
  91.9 5.0 %collective-permute-start.10 = (f32[10,8,128]{2,1,0:T(8,128)S(1)}, f32[10,8,128]{2,1,0:T(8,128)S(1)}, u32[]{:S(2)}, u32[]{:S(2)}) collective-permute-start(f32[10,8,128]{2,1,0:T(8,128)S(1)} %get-tuple-element.19), channel_id=1, source_target_pairs={{0,48},{8,56},{16,0},{24,8},{32,16},{40,24},{48,32},{56,40},{64,11... | collective-permute-start | bytes 122888 | tf_op jit(solution)/shard_map/ppermute | solution.py:315
  95.0 5.5 %collective-permute-start.8 = (f32[10,8,128]{2,1,0:T(8,128)S(1)}, f32[10,8,128]{2,1,0:T(8,128)S(1)}, u32[]{:S(2)}, u32[]{:S(2)}) collective-permute-start(f32[10,8,128]{2,1,0:T(8,128)S(1)} %get-tuple-element.19), channel_id=1, source_target_pairs={{0,32},{8,40},{16,48},{24,56},{32,0},{40,8},{48,16},{56,24},{64,96... | collective-permute-start | bytes 122888 | tf_op jit(solution)/shard_map/ppermute | solution.py:315
  95.6 5.3 %collective-permute-start.9 = (f32[10,8,128]{2,1,0:T(8,128)S(1)}, f32[10,8,128]{2,1,0:T(8,128)S(1)}, u32[]{:S(2)}, u32[]{:S(2)}) collective-permute-start(f32[10,8,128]{2,1,0:T(8,128)S(1)} %get-tuple-element.19), channel_id=1, source_target_pairs={{0,16},{8,24},{16,32},{24,40},{32,48},{40,56},{48,0},{56,8},{64,80... | collective-permute-start | bytes 122888 | tf_op jit(solution)/shard_map/ppermute | solution.py:315
  100.9 5.6 %collective-permute-start.11 = (f32[10,8,128]{2,1,0:T(8,128)S(1)}, f32[10,8,128]{2,1,0:T(8,128)S(1)}, u32[]{:S(2)}, u32[]{:S(2)}) collective-permute-start(f32[10,8,128]{2,1,0:T(8,128)S(1)} %add_add_fusion), channel_id=1, source_target_pairs={{0,128},{8,136},{16,144},{24,152},{32,160},{40,168},{48,176},{56,1... | collective-permute-start | bytes 122888 | tf_op jit(solution)/shard_map/ppermute | solution.py:315
  102.4 4.1 %collective-permute-start.12 = (f32[10,8,128]{2,1,0:T(8,128)S(1)}, f32[10,8,128]{2,1,0:T(8,128)S(1)}, u32[]{:S(2)}, u32[]{:S(2)}) collective-permute-start(f32[10,8,128]{2,1,0:T(8,128)S(1)} %add_add_fusion), channel_id=1, source_target_pairs={{0,64},{8,72},{16,80},{24,88},{32,96},{40,104},{48,112},{56,120},{... | collective-permute-start | bytes 122888 | tf_op jit(solution)/shard_map/ppermute | solution.py:315
  104.5 5.2 %collective-permute-start.13 = (f32[10,8,128]{2,1,0:T(8,128)S(1)}, f32[10,8,128]{2,1,0:T(8,128)S(1)}, u32[]{:S(2)}, u32[]{:S(2)}) collective-permute-start(f32[10,8,128]{2,1,0:T(8,128)S(1)} %add_add_fusion), channel_id=1, source_target_pairs={{0,192},{8,200},{16,208},{24,216},{32,224},{40,232},{48,240},{56,2... | collective-permute-start | bytes 122888 | tf_op jit(solution)/shard_map/ppermute | solution.py:315

commit v2 on v1

--- a/solution.py
+++ b/solution.py
@@ -15,9 +15,11 @@
 TILES = 9
 WIDE = TILES * 128
 ROWS = 17
-ORDER = (4, 3, 5, 2, 6, 1, 7, 0)
+ORDER = (2, 6, 3, 5, 0, 4, 1, 7)
+EARLY = 5
 CHUNK = 256
 VMEM_LIMIT = 56 * 1024 * 1024
+SMALL_LIMIT = 24 * 1024 * 1024
 
 
 def slot_cards():
@@ -89,8 +91,9 @@
     return [jnp.broadcast_to(table[i : i + 1, 128 * j : 128 * j + 128], (8, 128)) for i in range(2)]
 
 
-def pack_kernel(first, turn_card, river_card, policy_hbm, flop_reach, turn_policy, table, *rest):
-    outs, (policy, staged, raw, own, low, in_sem, out_sem) = (rest[:1] if first else rest[1:8]), rest[-7:]
+def pack_kernel(shifts, turn_card, river_card, policy_hbm, flop_reach, turn_policy, table, *rest):
+    policy, staged, raw, own, low, in_sem, out_sem = rest[-7:]
+    outs = rest[-7 - len(shifts) : -7]
     fetch = pltpu.make_async_copy(policy_hbm, policy, in_sem)
     fetch.start()
     me, t = lax.axis_index("hist"), turn_card[0]
@@ -141,16 +144,17 @@
     fetch.wait()
     stores = [pltpu.make_async_copy(staged.at[i], out, out_sem.at[i]) for i, out in enumerate(outs)]
 
-    @pl.loop(0, 2 * len(outs))
-    def _(step):
-        i, rl = step >> 1, 2 * (step & 1)
-        shift = 4 if first else jnp.where((i & 1) == 1, 5 + (i >> 1), 3 - (i >> 1))
-        river = ((me + shift) & 7) * 4 + rl
-        one_river(staged.at[i], rl, river)
-        one_river(staged.at[i], rl + 1, river + 1)
+    @pl.loop(0, len(outs))
+    def _(i):
+        shift = jnp.int32(shifts[0])
+        for k in range(1, len(shifts)):
+            shift = jnp.where(i == k, shifts[k], shift)
+        river = ((me + shift) & 7) * 4
+        for rl in range(4):
+            one_river(staged.at[i], rl, river + rl)
         for k, store in enumerate(stores):
 
-            @pl.when(step == 2 * k + 1)
+            @pl.when(i == k)
             def _(store=store):
                 store.start()
 
@@ -158,14 +162,14 @@
         store.wait()
 
 
-def pack(turn_cards, river_cards, policy, flop_reach, turn_policy, table, after):
-    count = 7 if after else 1
+def pack(shifts, turn_cards, river_cards, policy, flop_reach, turn_policy, table, after):
+    count = len(shifts)
     smem = pl.BlockSpec(memory_space=pltpu.SMEM)
     vmem = pl.BlockSpec(memory_space=pltpu.VMEM)
     anywhere = pl.BlockSpec(memory_space=pl.ANY)
     message = (4, ROWS, 8, 128)
     return pl.pallas_call(
-        functools.partial(pack_kernel, not after),
+        functools.partial(pack_kernel, shifts),
         out_shape=[jax.ShapeDtypeStruct(message, jnp.float32)] * count,
         in_specs=[smem] * 2 + [anywhere] + [vmem] * 3 + [anywhere] * len(after),
         out_specs=[anywhere] * count,
@@ -184,7 +188,7 @@
     )(turn_cards, river_cards, policy, flop_reach, turn_policy, table, *after)
 
 
-def payoff_kernel(turn_card, river_card, ranks, compat, table, after, out, rows, strip):
+def payoff_kernel(turn_card, river_card, ranks, compat, table, out, rows, strip):
     rl = pl.program_id(0)
     t = turn_card[0]
     r = river_card[0, 4 * lax.axis_index("hist") + rl]
@@ -218,87 +222,110 @@
             )
 
 
-def payoffs(turn_cards, river_cards, ranks, compat, table, after):
+def payoffs(turn_cards, river_cards, ranks, compat, table):
     smem = pl.BlockSpec(memory_space=pltpu.SMEM)
     vmem = pl.BlockSpec(memory_space=pltpu.VMEM)
     return pl.pallas_call(
         payoff_kernel,
         grid=(4,),
         out_shape=jax.ShapeDtypeStruct((4, WIDE, WIDE), jnp.bfloat16),
-        in_specs=[smem] * 2 + [vmem] * 3 + [pl.BlockSpec(memory_space=pl.ANY)],
+        in_specs=[smem] * 2 + [vmem] * 3,
         out_specs=pl.BlockSpec((1, WIDE, WIDE), lambda i: (i, 0, 0)),
         scratch_shapes=[pltpu.VMEM((8, 1408), jnp.float32), pltpu.VMEM((8, WIDE), jnp.float32)],
-        compiler_params=pltpu.CompilerParams(vmem_limit_bytes=VMEM_LIMIT),
+        compiler_params=pltpu.CompilerParams(vmem_limit_bytes=SMALL_LIMIT),
         cost_estimate=pl.CostEstimate(flops=4 * 4 * WIDE * WIDE, bytes_accessed=10 * WIDE * WIDE, transcendentals=0),
         name="payoff",
-    )(turn_cards, river_cards, ranks, compat, table, after)
-
-
-def reply_kernel(turn_card, river_card, payoff, select, scale, table, *rest):
-    blocks, (out, high, fine) = rest[:8], rest[8:]
-    rl = pl.program_id(0)
+    )(turn_cards, river_cards, ranks, compat, table)
+
+
+def split_block(block, row, high, fine):
+    lane = lanes_of((8, 128))
+    for j in range(TILES):
+        if j < 8:
+            pair = [block[j], block[8 + j]]
+        else:
+            tails = block[16]
+            pair = [jnp.where(lane < 64, v, 0.0) for v in (tails, pltpu.roll(tails, 64, 1))]
+        both = jnp.concatenate(pair, axis=0)
+        upper = both.astype(jnp.bfloat16)
+        high[row : row + 16, 128 * j : 128 * j + 128] = upper
+        fine[row : row + 16, 128 * j : 128 * j + 128] = (both - upper.astype(jnp.float32)).astype(jnp.bfloat16)
+
+
+def chosen_rows(select, high, fine):
+    parts = [jnp.dot(select[...], part[...], preferred_element_type=jnp.float32) for part in (high, fine)]
+    return jnp.concatenate([part.astype(jnp.bfloat16) for part in parts], axis=0)
+
+
+def choose_kernel(select, *rest):
+    blocks, (out, high, fine) = rest[:-3], rest[-3:]
+    for i, block in enumerate(blocks):
+        split_block(block.at[0], 16 * i, high, fine)
+    out[0] = chosen_rows(select, high, fine)
+
+
+def choose(select, blocks):
+    vmem = pl.BlockSpec(memory_space=pltpu.VMEM)
+    rows = 16 * len(blocks)
+    return pl.pallas_call(
+        choose_kernel,
+        grid=(4,),
+        out_shape=jax.ShapeDtypeStruct((4, 256, WIDE), jnp.bfloat16),
+        in_specs=[vmem] + [pl.BlockSpec((1, ROWS, 8, 128), lambda i: (i, 0, 0, 0))] * len(blocks),
+        out_specs=pl.BlockSpec((1, 256, WIDE), lambda i: (i, 0, 0)),
+        scratch_shapes=[pltpu.VMEM((rows, WIDE), jnp.bfloat16)] * 2,
+        compiler_params=pltpu.CompilerParams(vmem_limit_bytes=SMALL_LIMIT),
+        cost_estimate=pl.CostEstimate(flops=4 * 512 * rows * WIDE, bytes_accessed=5000000, transcendentals=0),
+        name="choose",
+    )(select, *blocks)
+
+
+def reply_kernel(turn_card, river_card, payoff, early, select, scale, table, *rest):
+    blocks, (out, high, fine) = rest[:-3], rest[-3:]
     t = turn_card[0]
-    r = river_card[0, 4 * lax.axis_index("hist") + rl]
+    me = lax.axis_index("hist")
     lane = lanes_of((8, 128))
-    for s in range(8):
-        for j in range(TILES):
-            if j < 8:
-                pair = [blocks[s][0, j], blocks[s][0, 8 + j]]
-            else:
-                tails = blocks[s][0, 16]
-                pair = [jnp.where(lane < 64, v, 0.0) for v in (tails, pltpu.roll(tails, 64, 1))]
-            both = jnp.concatenate(pair, axis=0)
-            upper = both.astype(jnp.bfloat16)
-            high[16 * s : 16 * s + 16, 128 * j : 128 * j + 128] = upper
-            fine[16 * s : 16 * s + 16, 128 * j : 128 * j + 128] = (
-                both - upper.astype(jnp.float32)
-            ).astype(jnp.bfloat16)
-    dot = functools.partial(jnp.dot, preferred_element_type=jnp.float32)
-    chosen = jnp.concatenate(
-        [dot(select[...], high[...]).astype(jnp.bfloat16), dot(select[...], fine[...]).astype(jnp.bfloat16)],
-        axis=0,
-    )
-
-    @pl.when(rl == 0)
-    def _():
-        out[...] = jnp.zeros_like(out)
-
-    home = home_slots(lane, t, r)
-    home_tile, home_lane = home >> 7, home & 127
-    first = [jnp.zeros((8, 128), jnp.float32)] * 8
-    for start in range(0, WIDE, CHUNK):
-        value = dot(chosen, payoff[0, :, start : start + CHUNK])
-        value = (value[:128] + value[128:]) * scale[...]
-        reply = jnp.maximum(value[:64], value[64:])
-        for j in range(start // 128, min(start + CHUNK, WIDE) // 128):
-            moved = source_lanes(*cards_of(table, j), t, r) >= 0
-            for g in range(8):
-                part = reply[8 * g : 8 * g + 8, 128 * j - start : 128 * j - start + 128]
-                out[g, 1 + j] += jnp.where(moved, 0.0, part)
-                first[g] = jnp.where(home_tile == j, pick(part, home_lane), first[g])
-    for g in range(8):
-        out[g, 0] += first[g]
-
-
-def replies(turn_cards, river_cards, payoff, select, scale, table, blocks):
+    out[...] = jnp.zeros_like(out)
+
+    @pl.loop(0, 4)
+    def _(rl):
+        r = river_card[0, 4 * me + rl]
+        for i, block in enumerate(blocks):
+            split_block(block.at[rl], 16 * i, high, fine)
+        chosen = early[rl] + chosen_rows(select, high, fine)
+        home = home_slots(lane, t, r)
+        home_tile, home_lane = home >> 7, home & 127
+        first = [jnp.zeros((8, 128), jnp.float32)] * 8
+        for start in range(0, WIDE, CHUNK):
+            value = jnp.dot(chosen, payoff[rl, :, start : start + CHUNK], preferred_element_type=jnp.float32)
+            value = (value[:128] + value[128:]) * scale[...]
+            reply = jnp.maximum(value[:64], value[64:])
+            for j in range(start // 128, min(start + CHUNK, WIDE) // 128):
+                moved = source_lanes(*cards_of(table, j), t, r) >= 0
+                for g in range(8):
+                    part = reply[8 * g : 8 * g + 8, 128 * j - start : 128 * j - start + 128]
+                    out[g, 1 + j] += jnp.where(moved, 0.0, part)
+                    first[g] = jnp.where(home_tile == j, pick(part, home_lane), first[g])
+        for g in range(8):
+            out[g, 0] += first[g]
+
+
+def replies(turn_cards, river_cards, payoff, early, select, scale, table, blocks):
     smem = pl.BlockSpec(memory_space=pltpu.SMEM)
     vmem = pl.BlockSpec(memory_space=pltpu.VMEM)
+    rows = 16 * len(blocks)
     return pl.pallas_call(
         reply_kernel,
-        grid=(4,),
         out_shape=jax.ShapeDtypeStruct((8, TILES + 1, 8, 128), jnp.float32),
-        in_specs=[smem] * 2
-        + [pl.BlockSpec((1, WIDE, WIDE), lambda i: (i, 0, 0))]
-        + [vmem] * 3
-        + [pl.BlockSpec((1, ROWS, 8, 128), lambda i: (i, 0, 0, 0))] * 8,
+        in_specs=[smem] * 2 + [vmem] * (5 + len(blocks)),
         out_specs=vmem,
-        scratch_shapes=[pltpu.VMEM((128, WIDE), jnp.bfloat16)] * 2,
-        compiler_params=pltpu.CompilerParams(vmem_limit_bytes=VMEM_LIMIT),
+        scratch_shapes=[pltpu.VMEM((rows, WIDE), jnp.bfloat16)] * 2,
+        compiler_params=pltpu.CompilerParams(vmem_limit_bytes=SMALL_LIMIT),
         cost_estimate=pl.CostEstimate(
             flops=4 * 2 * 256 * WIDE * WIDE, bytes_accessed=8 * WIDE * WIDE, transcendentals=0
         ),
         name="reply",
-    )(turn_cards, river_cards, payoff, select, scale, table, *blocks)
+    )(turn_cards, river_cards, payoff, early, select, scale, table, *blocks)
 
 
 def flat(nodes):
@@ -308,20 +335,18 @@
 
 
 def turn_sum(value, size):
-    value = value + lax.ppermute(value, "turn", [(i, i ^ 1) for i in range(size)])
+    pairs = [(i, i ^ 1) for i in range(size)]
+    half = value.shape[0] // 2
+    core = lax.axis_index("turn") & 1
+    keep = lax.dynamic_slice_in_dim(value, core * half, half, 0)
+    give = lax.dynamic_slice_in_dim(value, (1 - core) * half, half, 0)
+    total = keep + lax.ppermute(give, "turn", pairs)
     step = 2
     while step < size:
-        near = [
-            lax.ppermute(
-                value,
-                "turn",
-                [(i, i - i % (4 * step) + (i + s * step) % (4 * step)) for i in range(size)],
-            )
-            for s in (1, 2, 3)
-        ]
-        value = (value + near[1]) + (near[0] + near[2])
+        for flip in (1, 3):
+            total = total + lax.ppermute(total, "turn", [(i, i ^ (flip * step)) for i in range(size)])
         step *= 4
-    return value
+    return total, pairs, core
 
 
 def per_device(flop_reach, turn_policy, river_policy, hand_rank, turn_cards, river_cards, children, pot):
@@ -336,10 +361,17 @@
     def send(block, s):
         return lax.ppermute(block, "hist", [(i, (i + s) % groups) for i in range(groups)])
 
-    packed = pack(*common, [])
-    packed += pack(*common, packed)
-    got = [send(block, s) if s else block for block, s in zip(packed, ORDER)]
-    payoff = payoffs(turn_cards, river_cards, hand_rank[0], compat, table, packed[1])
+    got = {}
+
+    def exchange(shifts, after):
+        for s, block in zip(shifts, pack(shifts, *common, after)):
+            got[s] = send(block, s) if s else block
+        return [got[s] for s in shifts]
+
+    first = exchange((2, 6), [])
+    exchange((3, 5), [])
+    exchange((4, 1, 7, 0), first)
+    payoff = payoffs(turn_cards, river_cards, hand_rank[0], compat, table)
     child = jnp.transpose(children).reshape(128)
     turn_of = jnp.zeros((8,), jnp.int32).at[jnp.array(ORDER)].set(jnp.arange(8, dtype=jnp.int32))
     place = (turn_of[(me - (child >> 4)) & 7] << 4) + ((child & 1) << 3) + ((child >> 1) & 7)
@@ -349,13 +381,18 @@
         axis=1,
         keepdims=True,
     )
-    partial = replies(turn_cards, river_cards, payoff, select, scale, table, got)
+    early = choose(select[:, : 16 * EARLY], [got[s] for s in ORDER[:EARLY]])
+    late = [got[s] for s in ORDER[EARLY:]]
+    partial = replies(turn_cards, river_cards, payoff, early, select[:, 16 * EARLY :], scale, table, late)
     arrived = lax.all_to_all(partial, "hist", 0, 0, tiled=True)
     value = jnp.sum(arrived, axis=0) * (1.0 / 32.0)
-    mean = turn_sum(value, turns) * (1.0 / turns)
-    both = jnp.stack([value, mean])
+    half, pairs, core = turn_sum(value, turns)
+    both = jnp.concatenate([value, half * (1.0 / turns)], axis=0)
     spread = lax.all_to_all(jnp.broadcast_to(both, (groups,) + both.shape), "hist", 0, 0, tiled=True)
-    return (flat(spread[:, 0]).reshape(1, -1), flat(spread[:, 1]))
+    here = spread[:, TILES + 1 :]
+    there = lax.ppermute(here, "turn", pairs)
+    mean = jnp.concatenate([jnp.where(core == 0, here, there), jnp.where(core == 0, there, here)], axis=1)
+    return (flat(spread[:, : TILES + 1]).reshape(1, -1), flat(mean))
 
 
 def solution(mesh):

time: 133 us -> 129 us (0.970); the launches traced: 133 us -> 127 us
  blocking collectives: 39 us -> 0 us
  waiting for transfers between devices: 30.2 us -> 54.7 us
  starting transfers between devices: 28.1 us -> 35.7 us
    all_to_all x2 -> x0, blocking collectives: 39 us -> none  [the longest x1 20.2 us: per_device(): lax.all_to_all(jnp.broadcast_to(both, (groups,) + both.shape), 'hist', 0,...]
    all_to_all x0 -> x2, waiting for transfers between devices: none -> 26.3 us  [the longest x1 13.4 us: per_device(): arrived = lax.all_to_all(partial, 'hist', 0, 0, tiled=True)]
    all_to_all x0 -> x2, starting transfers between devices: none -> 8.62 us  [the longest x1 5.13 us: per_device(): arrived = lax.all_to_all(partial, 'hist', 0, 0, tiled=True)]
    pallas_call x3 -> x5, Pallas kernels: 20.1 us -> 24.4 us  [the longest x3 14.7 us: pack(): pl.pallas_call(functools.partial(pack_kernel, shifts), out_shape=[jax.Sha...]
    ppermute x7, waiting for transfers between devices: 19.4 us -> 15.6 us  [send(): lax.ppermute(block, 'hist', [(i, (i + s) % groups) for i in range(groups)])]
    pallas_call x1, Pallas kernels: 8.43 us -> 5.25 us  [payoffs(): pl.pallas_call(payoff_kernel, grid=(4,), out_shape=jax.ShapeDtypeStruct((...]
    ppermute x7 -> x6, starting transfers between devices: 8.38 us -> 6.1 us  [the longest x4 5.91 us: turn_sum(): lax.ppermute(total, 'turn', [(i, i ^ flip * step) for i in range(size)])]
    ppermute x7 -> x6, waiting for transfers between devices: 10.8 us -> 12.8 us  [the longest x4 11.6 us: turn_sum(): lax.ppermute(total, 'turn', [(i, i ^ flip * step) for i in range(size)])]
  transfers between devices with their start and end apart: 14 -> 15, of which waited for: 8 -> 11; matrix products, arithmetic and copies ran while one was open for 1% -> 2% of each run, Pallas kernels for 12% -> 14%
where the time goes in v2:
time: 129 us; the launch traced here: 127 us
  waiting for transfers between devices  54.7 us (42%)
  starting transfers between devices  35.7 us (28%)
  Pallas kernels  29.6 us (23%)
  local copies, waits for them, and re-layouts  4.78 us (4%)
  between operations  1.62 us (1%)
    ppermute x7, starting transfers between devices, send(): lax.ppermute(block, 'hist', [(i, (i + s) % groups) for i in range(groups)])  21 us
    ppermute x7, waiting for transfers between devices, send(): lax.ppermute(block, 'hist', [(i, (i + s) % groups) for i in range(groups)])  15.6 us
    pallas_call x3, Pallas kernels, pack(): pl.pallas_call(functools.partial(pack_kernel, shifts), out_shape=[jax.Sha...  14.7 us
    all_to_all x1, waiting for transfers between devices, per_device(): arrived = lax.all_to_all(partial, 'hist', 0, 0, tiled=True)  13.4 us
    all_to_all x1, waiting for transfers between devices, per_device(): lax.all_to_all(jnp.broadcast_to(both, (groups,) + both.shape), 'hist', 0,...  12.8 us
    ppermute x4, waiting for transfers between devices, turn_sum(): lax.ppermute(total, 'turn', [(i, i ^ flip * step) for i in range(size)])  11.6 us
    pallas_call x1, Pallas kernels, replies(): pl.pallas_call(reply_kernel, out_shape=jax.ShapeDtypeStruct((8, TILES + 1...  6.87 us
    ppermute x4, starting transfers between devices, turn_sum(): lax.ppermute(total, 'turn', [(i, i ^ flip * step) for i in range(size)])  5.91 us
  transfers between devices with their start and end apart: 15, of which 11 were waited for; matrix products, arithmetic and copies ran while one was open for 2% of the time, Pallas kernels for 14%

profile of v2, /device:TPU:6, one launch (start us, length us, event | category | flops | bytes accessed | tf_op | source)
XLA Modules:
  0.0 126.8 jit_solution(14233273288325640938)
XLA Ops:
  1.3 4.5 %pack.3 = (f32[4,17,8,128]{3,2,1,0:T(8,128)}, f32[4,17,8,128]{3,2,1,0:T(8,128)}) custom-call(s32[1]{0:T(128)S(6)} %copy.34.turn_card, s32[1,32]{1,0:T(1,128)} %river_card.9, s32[5304,128]{1,0:T(8,128)} %bitcast.56, f32[16,1326]{1,0:T(8,128)} %bitcast.61, s32[16,1326]{1,0:T(8,128)} %bitcast.64, s32[2,1152]{1,0:T(2,128)} %constant.13.clone.table), custom_call_target="tpu_custom_call" | custom-call | flops 3000000 | bytes 4000000 | tf_op jit(solution)/shard_map/pack/pallas_call | solution.py:171
  5.8 3.3 %collective-permute-start = (f32[4,17,8,128]{3,2,1,0:T(8,128)}, f32[4,17,8,128]{3,2,1,0:T(8,128)S(1)}, u32[]{:S(2)}, u32[]{:S(2)}) collective-permute-start(f32[4,17,8,128]{3,2,1,0:T(8,128)} %get-tuple-element.10), channel_id=1, source_target_pairs={{0,2},{1,3},{2,4},{3,5},{4,6},{5,7},{6,0},{7,1},{8,10},{9,11},{10,... | collective-permute-start | bytes 835592 | tf_op jit(solution)/shard_map/ppermute | solution.py:362
  9.2 0.0 copy-start.8
  9.2 3.2 %collective-permute-start.1 = (f32[4,17,8,128]{3,2,1,0:T(8,128)}, f32[4,17,8,128]{3,2,1,0:T(8,128)S(1)}, u32[]{:S(2)}, u32[]{:S(2)}) collective-permute-start(f32[4,17,8,128]{3,2,1,0:T(8,128)} %get-tuple-element.11), channel_id=1, source_target_pairs={{0,6},{1,7},{2,0},{3,1},{4,2},{5,3},{6,4},{7,5},{8,14},{9,15},{10,... | collective-permute-start | bytes 835592 | tf_op jit(solution)/shard_map/ppermute | solution.py:362
  12.4 4.5 %pack.4 = (f32[4,17,8,128]{3,2,1,0:T(8,128)}, f32[4,17,8,128]{3,2,1,0:T(8,128)}) custom-call(s32[1]{0:T(128)S(6)} %copy.34.turn_card, s32[1,32]{1,0:T(1,128)} %river_card.9, s32[5304,128]{1,0:T(8,128)} %bitcast.57, f32[16,1326]{1,0:T(8,128)} %bitcast.62, s32[16,1326]{1,0:T(8,128)} %bitcast.65, s32[2,1152]{1,0:T(2,128)} %constant.13.clone.table), custom_call_target="tpu_custom_call" | custom-call | flops 3000000 | bytes 4000000 | tf_op jit(solution)/shard_map/pack/pallas_call | solution.py:171
  16.9 2.1 %collective-permute-start.2 = (f32[4,17,8,128]{3,2,1,0:T(8,128)}, f32[4,17,8,128]{3,2,1,0:T(8,128)S(1)}, u32[]{:S(2)}, u32[]{:S(2)}) collective-permute-start(f32[4,17,8,128]{3,2,1,0:T(8,128)} %get-tuple-element.12), channel_id=1, source_target_pairs={{0,3},{1,4},{2,5},{3,6},{4,7},{5,0},{6,1},{7,2},{8,11},{9,12},{10,... | collective-permute-start | bytes 835592 | tf_op jit(solution)/shard_map/ppermute | solution.py:362
  19.0 3.0 %collective-permute-start.3 = (f32[4,17,8,128]{3,2,1,0:T(8,128)}, f32[4,17,8,128]{3,2,1,0:T(8,128)}, u32[]{:S(2)}, u32[]{:S(2)}) collective-permute-start(f32[4,17,8,128]{3,2,1,0:T(8,128)} %get-tuple-element.13), channel_id=1, source_target_pairs={{0,5},{1,6},{2,7},{3,0},{4,1},{5,2},{6,3},{7,4},{8,13},{9,14},{10,... | collective-permute-start | bytes 835592 | tf_op jit(solution)/shard_map/ppermute | solution.py:362
  22.0 0.1 and.33
  22.1 0.1 reshape.74
  22.2 0.0 collective-permute-done.rest_0_
  22.2 0.0 copy-start.1
  22.2 7.7 %collective-permute-done.1.rest_1_ = f32[4,17,8,128]{3,2,1,0:T(8,128)S(1)} collective-permute-done((f32[4,17,8,128]{3,2,1,0:T(8,128)}, f32[4,17,8,128]{3,2,1,0:T(8,128)S(1)}, u32[]{:S(2)}, u32[]{:S(2)}) %collective-permute-start.1) | collective-permute-done | bytes 278560 | tf_op jit(solution)/shard_map/ppermute | solution.py:362
  30.0 0.7 copy-done.3
  30.7 5.6 %pack.5 = (f32[4,17,8,128]{3,2,1,0:T(8,128)}, f32[4,17,8,128]{3,2,1,0:T(8,128)}, f32[4,17,8,128]{3,2,1,0:T(8,128)}, f32[4,17,8,128]{3,2,1,0:T(8,128)}) custom-call(s32[1]{0:T(128)S(6)} %copy.34.turn_card, s32[1,32]{1,0:T(1,128)} %river_card.9, s32[5304,128]{1,0:T(8,128)} %bitcast.58, f32[16,1326]{1,0:T(8,128)} %bitcast.63, s32[16,1326]{1,0:T(8,128)} %bitcast.66, ...), custom_call_target="tpu_custom_call" | custom-call | flops 3000000 | bytes 4000000 | tf_op jit(solution)/shard_map/pack/pallas_call | solution.py:171
  36.3 6.2 %collective-permute-start.4 = (f32[4,17,8,128]{3,2,1,0:T(8,128)}, f32[4,17,8,128]{3,2,1,0:T(8,128)}, u32[]{:S(2)}, u32[]{:S(2)}) collective-permute-start(f32[4,17,8,128]{3,2,1,0:T(8,128)} %get-tuple-element.15), channel_id=1, source_target_pairs={{0,4},{1,5},{2,6},{3,7},{4,0},{5,1},{6,2},{7,3},{8,12},{9,13},{10,... | collective-permute-start | bytes 835592 | tf_op jit(solution)/shard_map/ppermute | solution.py:362
  42.5 3.2 %collective-permute-start.6 = (f32[4,17,8,128]{3,2,1,0:T(8,128)}, f32[4,17,8,128]{3,2,1,0:T(8,128)}, u32[]{:S(2)}, u32[]{:S(2)}) collective-permute-start(f32[4,17,8,128]{3,2,1,0:T(8,128)} %get-tuple-element.17), channel_id=1, source_target_pairs={{0,7},{1,0},{2,1},{3,2},{4,3},{5,4},{6,5},{7,6},{8,15},{9,8},{10,9... | collective-permute-start | bytes 835592 | tf_op jit(solution)/shard_map/ppermute | solution.py:362
  45.7 0.1 fusion
  45.8 0.1 slice.50.select
  45.9 0.2 select_reduce_fusion
  46.1 0.1 copy.23.scale
  46.2 0.0 copy-start.2
  46.3 0.0 copy-start.4
  46.3 5.2 %payoff.1 = bf16[4,1152,1152]{2,1,0:T(8,128)(2,1)S(1)} custom-call(s32[1]{0:T(128)S(6)} %copy.34.turn_card, s32[1,32]{1,0:T(1,128)S(1)} %copy-done.8, s32[4,1326]{1,0:T(4,128)S(1)} %bitcast.55, bf16[1152,1152]{1,0:T(8,128)(2,1)S(1)} %copy-done, s32[2,1152]{1,0:T(2,128)S(1)} %copy-done.6), custom_call_target="tpu_custom_call" | custom-call | flops 21233664 | bytes 13271040 | tf_op jit(solution)/shard_map/payoff/pallas_call | solution.py:228
  51.6 2.8 %choose.1.early = bf16[4,256,1152]{2,1,0:T(8,128)(2,1)S(1)} custom-call(bf16[128,80]{1,0:T(8,128)(2,1)S(1)} %bitcast.54, f32[4,17,8,128]{3,2,1,0:T(8,128)S(1)} %copy-done.2, f32[4,17,8,128]{3,2,1,0:T(8,128)S(1)} %copy-done.4, f32[4,17,8,128]{3,2,1,0:T(8,128)S(1)} %collective-permute-done.2.rest_2_, f32[4,17,8,128]{3,2,1,0:T(8,128)} %collective-permute-done.3.rest_3_, ...), custom_call_target="tpu_custom_call" | custom-call | flops 188743680 | bytes 5000000 | tf_op jit(solution)/shard_map/choose/pallas_call | solution.py:270
  54.4 1.1 collective-permute-done.4.rest_0_
  55.5 6.3 %collective-permute-done.5.rest_1_ = f32[4,17,8,128]{3,2,1,0:T(8,128)} collective-permute-done((f32[4,17,8,128]{3,2,1,0:T(8,128)}, f32[4,17,8,128]{3,2,1,0:T(8,128)}, u32[]{:S(2)}, u32[]{:S(2)}) %collective-permute-start.5) | collective-permute-done | bytes 278560 | tf_op jit(solution)/shard_map/ppermute | solution.py:362
  61.8 0.4 collective-permute-done.6.rest_2_
  62.2 6.9 %reply.1 = f32[8,10,8,128]{3,2,1,0:T(8,128)} custom-call(s32[1]{0:T(128)S(6)} %copy.34.turn_card, s32[1,32]{1,0:T(1,128)S(1)} %copy-done.8, bf16[4,1152,1152]{2,1,0:T(8,128)(2,1)S(1)} %payoff.1, bf16[4,256,1152]{2,1,0:T(8,128)(2,1)S(1)} %choose.1.early, bf16[128,48]{1,0:T(8,128)(2,1)S(1)} %slice.50.select, f32[128,1]{1,0:T(8,128)S(1)} %copy.23.scale, ...), custom_call_target="tpu_custom_call" | custom-call | flops 2717908992 | bytes 10616832 | tf_op jit(solution)/shard_map/reply/pallas_call | solution.py:317
  69.1 5.1 %all-to-all-start = ((f32[8,10,8,128]{3,2,1,0:T(8,128)}), f32[8,10,8,128]{3,2,1,0:T(8,128)S(1)}, u32[]{:S(2)}, u32[]{:S(2)}) async-start(f32[8,10,8,128]{3,2,1,0:T(8,128)} %reply.1), calls=%async_computation | async-start | bytes 655360 | tf_op jit(solution)/shard_map/all_to_all | solution.py:387
  74.2 13.4 %all-to-all-done = f32[8,10,8,128]{3,2,1,0:T(8,128)S(1)} async-done(((f32[8,10,8,128]{3,2,1,0:T(8,128)}), f32[8,10,8,128]{3,2,1,0:T(8,128)S(1)}, u32[]{:S(2)}, u32[]{:S(2)}) %all-to-all-start) | async-done | bytes 327712 | tf_op jit(solution)/shard_map/all_to_all | solution.py:387
  87.7 0.1 collective-permute-start.7
  87.8 1.2 collective-permute-done.7
  89.0 1.6 %collective-permute-start.8 = (f32[5,8,128]{2,1,0:T(8,128)S(1)}, f32[5,8,128]{2,1,0:T(8,128)S(1)}, u32[]{:S(2)}, u32[]{:S(2)}) collective-permute-start(f32[5,8,128]{2,1,0:T(8,128)S(1)} %dynamic-slice_add_fusion), channel_id=1, source_target_pairs={{0,16},{8,24},{16,0},{24,8},{32,48},{40,56},{48,32},{56,40},{64,80... | collective-permute-start | bytes 61448 | tf_op jit(solution)/shard_map/ppermute | solution.py:347
  90.6 2.2 %collective-permute-done.8 = f32[5,8,128]{2,1,0:T(8,128)S(1)} collective-permute-done((f32[5,8,128]{2,1,0:T(8,128)S(1)}, f32[5,8,128]{2,1,0:T(8,128)S(1)}, u32[]{:S(2)}, u32[]{:S(2)}) %collective-permute-start.8) | collective-permute-done | bytes 20512 | tf_op jit(solution)/shard_map/ppermute | solution.py:347
  92.8 3.0 %collective-permute-start.9 = (f32[5,8,128]{2,1,0:T(8,128)S(1)}, f32[5,8,128]{2,1,0:T(8,128)S(1)}, u32[]{:S(2)}, u32[]{:S(2)}) collective-permute-start(f32[5,8,128]{2,1,0:T(8,128)S(1)} %add.59), channel_id=1, source_target_pairs={{0,48},{8,56},{16,32},{24,40},{32,16},{40,24},{48,0},{56,8},{64,11... | collective-permute-start | bytes 61448 | tf_op jit(solution)/shard_map/ppermute | solution.py:347
  95.8 2.0 %collective-permute-done.9 = f32[5,8,128]{2,1,0:T(8,128)S(1)} collective-permute-done((f32[5,8,128]{2,1,0:T(8,128)S(1)}, f32[5,8,128]{2,1,0:T(8,128)S(1)}, u32[]{:S(2)}, u32[]{:S(2)}) %collective-permute-start.9) | collective-permute-done | bytes 20512 | tf_op jit(solution)/shard_map/ppermute | solution.py:347
  97.8 0.8 collective-permute-start.10
  98.6 2.9 %collective-permute-done.10 = f32[5,8,128]{2,1,0:T(8,128)S(1)} collective-permute-done((f32[5,8,128]{2,1,0:T(8,128)S(1)}, f32[5,8,128]{2,1,0:T(8,128)S(1)}, u32[]{:S(2)}, u32[]{:S(2)}) %collective-permute-start.10) | collective-permute-done | bytes 20512 | tf_op jit(solution)/shard_map/ppermute | solution.py:347
  101.6 0.5 collective-permute-start.11
  102.1 4.5 %collective-permute-done.11 = f32[5,8,128]{2,1,0:T(8,128)S(1)} collective-permute-done((f32[5,8,128]{2,1,0:T(8,128)S(1)}, f32[5,8,128]{2,1,0:T(8,128)S(1)}, u32[]{:S(2)}, u32[]{:S(2)}) %collective-permute-start.11) | collective-permute-done | bytes 20512 | tf_op jit(solution)/shard_map/ppermute | solution.py:347
  106.6 0.8 broadcast_in_dim.30
  107.4 3.5 %all-to-all-start.1 = ((f32[8,15,8,128]{3,2,1,0:T(8,128)}), f32[8,15,8,128]{3,2,1,0:T(8,128)S(1)}, u32[]{:S(2)}, u32[]{:S(2)}) async-start(f32[8,15,8,128]{3,2,1,0:T(8,128)} %broadcast_in_dim.30), calls=%async_computation.1 | async-start | bytes 983040 | tf_op jit(solution)/shard_map/all_to_all | solution.py:391
  110.9 12.8 %all-to-all-done.1 = f32[8,15,8,128]{3,2,1,0:T(8,128)S(1)} async-done(((f32[8,15,8,128]{3,2,1,0:T(8,128)}), f32[8,15,8,128]{3,2,1,0:T(8,128)S(1)}, u32[]{:S(2)}, u32[]{:S(2)}) %all-to-all-start.1) | async-done | bytes 491552 | tf_op jit(solution)/shard_map/all_to_all | solution.py:391
  123.8 0.1 collective-permute-start.12
  124.0 0.2 concatenate.13
  124.2 1.3 %reshape_reshape.3 = f32[1,84864]{1,0:T(1,128)} reshape(f32[64,1326]{1,0:T(8,128)S(1)} %concatenate.13) | data formatting | bytes 678912 | tf_op jit(solution)/shard_map/reshape;reshape | solution.py:395
  125.6 0.2 concatenate.15
  125.8 1.0 reshape.80
  (42 shorter events, 0.3 us)
Async XLA Ops:
  1.3 20.7 %copy-start.9 = (s32[64,2]{0,1:T(2,128)S(1)}, s32[64,2]{0,1:T(2,128)}, u32[]{:S(2)}) copy-start(s32[64,2]{0,1:T(2,128)} %param.17) | copy-start | bytes 1540
  5.8 16.4 %collective-permute-start = (f32[4,17,8,128]{3,2,1,0:T(8,128)}, f32[4,17,8,128]{3,2,1,0:T(8,128)S(1)}, u32[]{:S(2)}, u32[]{:S(2)}) collective-permute-start(f32[4,17,8,128]{3,2,1,0:T(8,128)} %get-tuple-element.10), channel_id=1, source_target_pairs={{0,2},{1,3},{2,4},{3,5},{4,6},{5,7},{6,0},{7,1},{8,10},{9,11},{10,... | collective-permute-start | bytes 835592 | tf_op jit(solution)/shard_map/ppermute | solution.py:362
  9.2 36.7 %copy-start.10 = (s32[128]{0:T(128)S(1)}, s32[128]{0:T(128)}, u32[]{:S(2)}) copy-start(s32[128]{0:T(128)} %param.18) | copy-start | bytes 1540
  9.2 37.0 %copy-start = (bf16[1152,1152]{1,0:T(8,128)(2,1)S(1)}, bf16[1152,1152]{1,0:T(8,128)(2,1)}, u32[]{:S(2)}) copy-start(bf16[1152,1152]{1,0:T(8,128)(2,1)} %constant.14.clone.compat) | copy-start | bytes 7962628
  9.2 37.0 %copy-start.6 = (s32[2,1152]{1,0:T(2,128)S(1)}, s32[2,1152]{1,0:T(2,128)}, u32[]{:S(2)}) copy-start(s32[2,1152]{1,0:T(2,128)} %constant.13.clone.table) | copy-start | bytes 27652
  9.2 37.0 %copy-start.7 = (s32[1,4,1326]{2,1,0:T(4,128)S(1)}, s32[1,4,1326]{2,1,0:T(4,128)}, u32[]{:S(2)}) copy-start(s32[1,4,1326]{2,1,0:T(4,128)} %param.14) | copy-start | bytes 63652
  9.2 37.0 %copy-start.8 = (s32[1,32]{1,0:T(1,128)S(1)}, s32[1,32]{1,0:T(1,128)}, u32[]{:S(2)}) copy-start(s32[1,32]{1,0:T(1,128)} %river_card.9) | copy-start | bytes 388
  9.2 20.8 %collective-permute-start.1 = (f32[4,17,8,128]{3,2,1,0:T(8,128)}, f32[4,17,8,128]{3,2,1,0:T(8,128)S(1)}, u32[]{:S(2)}, u32[]{:S(2)}) collective-permute-start(f32[4,17,8,128]{3,2,1,0:T(8,128)} %get-tuple-element.11), channel_id=1, source_target_pairs={{0,6},{1,7},{2,0},{3,1},{4,2},{5,3},{6,4},{7,5},{8,14},{9,15},{10,... | collective-permute-start | bytes 835592 | tf_op jit(solution)/shard_map/ppermute | solution.py:362
  16.9 34.6 %collective-permute-start.2 = (f32[4,17,8,128]{3,2,1,0:T(8,128)}, f32[4,17,8,128]{3,2,1,0:T(8,128)S(1)}, u32[]{:S(2)}, u32[]{:S(2)}) collective-permute-start(f32[4,17,8,128]{3,2,1,0:T(8,128)} %get-tuple-element.12), channel_id=1, source_target_pairs={{0,3},{1,4},{2,5},{3,6},{4,7},{5,0},{6,1},{7,2},{8,11},{9,12},{10,... | collective-permute-start | bytes 835592 | tf_op jit(solution)/shard_map/ppermute | solution.py:362
  19.0 32.5 %collective-permute-start.3 = (f32[4,17,8,128]{3,2,1,0:T(8,128)}, f32[4,17,8,128]{3,2,1,0:T(8,128)}, u32[]{:S(2)}, u32[]{:S(2)}) collective-permute-start(f32[4,17,8,128]{3,2,1,0:T(8,128)} %get-tuple-element.13), channel_id=1, source_target_pairs={{0,5},{1,6},{2,7},{3,0},{4,1},{5,2},{6,3},{7,4},{8,13},{9,14},{10,... | collective-permute-start | bytes 835592 | tf_op jit(solution)/shard_map/ppermute | solution.py:362
  22.2 7.8 %copy-start.1 = (f32[4,17,8,128]{3,2,1,0:T(8,128)}, f32[4,17,8,128]{3,2,1,0:T(8,128)S(1)}, u32[]{:S(2)}) copy-start(f32[4,17,8,128]{3,2,1,0:T(8,128)S(1)} %collective-permute-done.rest_0_) | copy-start | bytes 835588
  30.0 0.7 copy-start.3
  36.3 19.2 %collective-permute-start.4 = (f32[4,17,8,128]{3,2,1,0:T(8,128)}, f32[4,17,8,128]{3,2,1,0:T(8,128)}, u32[]{:S(2)}, u32[]{:S(2)}) collective-permute-start(f32[4,17,8,128]{3,2,1,0:T(8,128)} %get-tuple-element.15), channel_id=1, source_target_pairs={{0,4},{1,5},{2,6},{3,7},{4,0},{5,1},{6,2},{7,3},{8,12},{9,13},{10,... | collective-permute-start | bytes 835592 | tf_op jit(solution)/shard_map/ppermute | solution.py:362
  42.5 19.3 %collective-permute-start.5 = (f32[4,17,8,128]{3,2,1,0:T(8,128)}, f32[4,17,8,128]{3,2,1,0:T(8,128)}, u32[]{:S(2)}, u32[]{:S(2)}) collective-permute-start(f32[4,17,8,128]{3,2,1,0:T(8,128)} %get-tuple-element.16), channel_id=1, source_target_pairs={{0,1},{1,2},{2,3},{3,4},{4,5},{5,6},{6,7},{7,0},{8,9},{9,10},{10,1... | collective-permute-start | bytes 835592 | tf_op jit(solution)/shard_map/ppermute | solution.py:362
  42.5 19.7 %collective-permute-start.6 = (f32[4,17,8,128]{3,2,1,0:T(8,128)}, f32[4,17,8,128]{3,2,1,0:T(8,128)}, u32[]{:S(2)}, u32[]{:S(2)}) collective-permute-start(f32[4,17,8,128]{3,2,1,0:T(8,128)} %get-tuple-element.17), channel_id=1, source_target_pairs={{0,7},{1,0},{2,1},{3,2},{4,3},{5,4},{6,5},{7,6},{8,15},{9,8},{10,9... | collective-permute-start | bytes 835592 | tf_op jit(solution)/shard_map/ppermute | solution.py:362
  46.2 5.3 %copy-start.2 = (f32[4,17,8,128]{3,2,1,0:T(8,128)S(1)}, f32[4,17,8,128]{3,2,1,0:T(8,128)}, u32[]{:S(2)}) copy-start(f32[4,17,8,128]{3,2,1,0:T(8,128)} %copy-done.1) | copy-start | bytes 835588
  46.3 5.3 %copy-start.4 = (f32[4,17,8,128]{3,2,1,0:T(8,128)S(1)}, f32[4,17,8,128]{3,2,1,0:T(8,128)}, u32[]{:S(2)}) copy-start(f32[4,17,8,128]{3,2,1,0:T(8,128)} %copy-done.3) | copy-start | bytes 835588
  46.3 5.3 %copy-start.5 = (f32[4,17,8,128]{3,2,1,0:T(8,128)S(1)}, f32[4,17,8,128]{3,2,1,0:T(8,128)}, u32[]{:S(2)}) copy-start(f32[4,17,8,128]{3,2,1,0:T(8,128)} %get-tuple-element.14.rest_4_) | copy-start | bytes 835588
  69.1 18.6 %all-to-all-start = ((f32[8,10,8,128]{3,2,1,0:T(8,128)}), f32[8,10,8,128]{3,2,1,0:T(8,128)S(1)}, u32[]{:S(2)}, u32[]{:S(2)}) async-start(f32[8,10,8,128]{3,2,1,0:T(8,128)} %reply.1), calls=%async_computation | async-start | bytes 655360 | tf_op jit(solution)/shard_map/all_to_all | solution.py:387
  87.7 1.3 %collective-permute-start.7 = (f32[5,8,128]{2,1,0:T(8,128)S(1)}, f32[5,8,128]{2,1,0:T(8,128)S(1)}, u32[]{:S(2)}, u32[]{:S(2)}) collective-permute-start(f32[5,8,128]{2,1,0:T(8,128)S(1)} %constant_dynamic-slice_fusion), channel_id=1, source_target_pairs={{0,8},{8,0},{16,24},{24,16},{32,40},{40,32},{48,56},{56,48},{64,72... | collective-permute-start | bytes 61448 | tf_op jit(solution)/shard_map/ppermute | solution.py:343
  89.0 3.8 %collective-permute-start.8 = (f32[5,8,128]{2,1,0:T(8,128)S(1)}, f32[5,8,128]{2,1,0:T(8,128)S(1)}, u32[]{:S(2)}, u32[]{:S(2)}) collective-permute-start(f32[5,8,128]{2,1,0:T(8,128)S(1)} %dynamic-slice_add_fusion), channel_id=1, source_target_pairs={{0,16},{8,24},{16,0},{24,8},{32,48},{40,56},{48,32},{56,40},{64,80... | collective-permute-start | bytes 61448 | tf_op jit(solution)/shard_map/ppermute | solution.py:347
  92.8 5.0 %collective-permute-start.9 = (f32[5,8,128]{2,1,0:T(8,128)S(1)}, f32[5,8,128]{2,1,0:T(8,128)S(1)}, u32[]{:S(2)}, u32[]{:S(2)}) collective-permute-start(f32[5,8,128]{2,1,0:T(8,128)S(1)} %add.59), channel_id=1, source_target_pairs={{0,48},{8,56},{16,32},{24,40},{32,16},{40,24},{48,0},{56,8},{64,11... | collective-permute-start | bytes 61448 | tf_op jit(solution)/shard_map/ppermute | solution.py:347
  97.8 3.8 %collective-permute-start.10 = (f32[5,8,128]{2,1,0:T(8,128)S(1)}, f32[5,8,128]{2,1,0:T(8,128)S(1)}, u32[]{:S(2)}, u32[]{:S(2)}) collective-permute-start(f32[5,8,128]{2,1,0:T(8,128)S(1)} %add.60), channel_id=1, source_target_pairs={{0,64},{8,72},{16,80},{24,88},{32,96},{40,104},{48,112},{56,120},{... | collective-permute-start | bytes 61448 | tf_op jit(solution)/shard_map/ppermute | solution.py:347
  101.6 5.0 %collective-permute-start.11 = (f32[5,8,128]{2,1,0:T(8,128)S(1)}, f32[5,8,128]{2,1,0:T(8,128)S(1)}, u32[]{:S(2)}, u32[]{:S(2)}) collective-permute-start(f32[5,8,128]{2,1,0:T(8,128)S(1)} %add.61), channel_id=1, source_target_pairs={{0,192},{8,200},{16,208},{24,216},{32,224},{40,232},{48,240},{56,2... | collective-permute-start | bytes 61448 | tf_op jit(solution)/shard_map/ppermute | solution.py:347
  107.4 16.3 %all-to-all-start.1 = ((f32[8,15,8,128]{3,2,1,0:T(8,128)}), f32[8,15,8,128]{3,2,1,0:T(8,128)S(1)}, u32[]{:S(2)}, u32[]{:S(2)}) async-start(f32[8,15,8,128]{3,2,1,0:T(8,128)} %broadcast_in_dim.30), calls=%async_computation.1 | async-start | bytes 983040 | tf_op jit(solution)/shard_map/all_to_all | solution.py:391
  123.8 1.7 %collective-permute-start.12 = (f32[8,5,8,128]{3,2,1,0:T(8,128)S(1)}, f32[8,5,8,128]{3,2,1,0:T(8,128)S(1)}, u32[]{:S(2)}, u32[]{:S(2)}) collective-permute-start(f32[8,5,8,128]{3,2,1,0:T(8,128)S(1)} %slice.55), channel_id=1, source_target_pairs={{0,8},{8,0},{16,24},{24,16},{32,40},{40,32},{48,56},{56,48},{64,72... | collective-permute-start | bytes 491528 | tf_op jit(solution)/shard_map/ppermute | solution.py:393

commit v3 on v2

--- a/solution.py
+++ b/solution.py
@@ -18,8 +18,9 @@
 ORDER = (2, 6, 3, 5, 0, 4, 1, 7)
 EARLY = 5
 CHUNK = 256
+FETCH = 56
 VMEM_LIMIT = 56 * 1024 * 1024
-SMALL_LIMIT = 24 * 1024 * 1024
+SMALL_LIMIT = 16 * 1024 * 1024
 
 
 def slot_cards():
@@ -91,11 +92,42 @@
     return [jnp.broadcast_to(table[i : i + 1, 128 * j : 128 * j + 128], (8, 128)) for i in range(2)]
 
 
-def pack_kernel(shifts, turn_card, river_card, policy_hbm, flop_reach, turn_policy, table, *rest):
-    policy, staged, raw, own, low, in_sem, out_sem = rest[-7:]
-    outs = rest[-7 - len(shifts) : -7]
-    fetch = pltpu.make_async_copy(policy_hbm, policy, in_sem)
-    fetch.start()
+def first_row(group, p):
+    return (p * 42432 + group * 4 * HANDS + LOW) >> 7
+
+
+def pack_kernel(shifts, turn_card_hbm, river_card_hbm, policy_hbm, flop_hbm, turn_hbm, table_hbm, *rest):
+    turn_card, river_card, flop_reach, turn_policy, table, policy, raw, own, low, in_sem, row_sem = rest[-11:]
+    outs = rest[-11 - len(shifts) : -11]
+    small = [
+        pltpu.make_async_copy(source, to, in_sem.at[i])
+        for i, (source, to) in enumerate(
+            zip(
+                (turn_card_hbm, river_card_hbm, flop_hbm, turn_hbm, table_hbm),
+                (turn_card, river_card, flop_reach, turn_policy, table),
+            )
+        )
+    ]
+    for fetch in small:
+        fetch.start()
+    fetches = []
+    for i, shift in enumerate(shifts):
+        for p in range(2):
+            base = first_row((lax.axis_index("hist") + shift) & 7, p)
+            for g in range(8):
+                wanted = ((663 * g + base) >> 3) << 3
+                start = jnp.minimum(wanted, 5304 - FETCH)
+                place = 16 + 72 * g - jnp.where(g > (base & 7), 8, 0) - (wanted - start)
+                fetches.append(
+                    pltpu.make_async_copy(
+                        policy_hbm.at[pl.ds(pl.multiple_of(start, 8), FETCH)],
+                        policy.at[i, p, pl.ds(pl.multiple_of(place, 8), FETCH)],
+                        row_sem.at[i, p, g],
+                    )
+                )
+                fetches[-1].start()
+    for fetch in small:
+        fetch.wait()
     me, t = lax.axis_index("hist"), turn_card[0]
     lane = lanes_of((8, 128))
     reach = flop_reach[...] * (turn_policy[...].astype(jnp.float32) * (1.0 / 256.0)) * (1.0 / 256.0)
@@ -110,22 +142,25 @@
         moved = pltpu.roll(reach, 1408 - LOW, 1)
         low[p] = jnp.where(wide < 95, moved, 0.0)[:, :128]
 
-    def one_river(out, rl, river):
+    def one_river(out, i, group, rl):
+        river = 4 * group + rl
         r = river_card[0, river]
         index = [source_lanes(*cards_of(table, j), t, r) for j in range(TILES)]
         tails = []
         for p in range(2):
 
-            def aligned(start, count):
+            base = first_row(group, p)
+
+            def aligned(start, count, p=p, base=base):
                 row, shift = start >> 7, start & 127
                 turn = (128 - shift) & 127
                 rolled = [
-                    pltpu.roll(policy[pl.ds(jnp.minimum(row + i, 662), 8, stride=663), :], turn, 1)
-                    for i in range(count + 1)
+                    pltpu.roll(policy[i, p, pl.ds(jnp.minimum(row + k, 662) - base + (base & 7) + 16, 8, stride=71), :], turn, 1)
+                    for k in range(count + 1)
                 ]
                 keep = lane < 128 - shift
                 return [
-                    jnp.where(keep, rolled[i], rolled[i + 1]).astype(jnp.float32) for i in range(count)
+                    jnp.where(keep, rolled[k], rolled[k + 1]).astype(jnp.float32) for k in range(count)
                 ]
 
             start = p * 42432 + river * HANDS + LOW
@@ -141,46 +176,36 @@
                     tails.append(value)
         out[rl, 16] = tails[0] + pltpu.roll(tails[1], 64, 1)
 
-    fetch.wait()
-    stores = [pltpu.make_async_copy(staged.at[i], out, out_sem.at[i]) for i, out in enumerate(outs)]
-
-    @pl.loop(0, len(outs))
-    def _(i):
-        shift = jnp.int32(shifts[0])
-        for k in range(1, len(shifts)):
-            shift = jnp.where(i == k, shifts[k], shift)
-        river = ((me + shift) & 7) * 4
-        for rl in range(4):
-            one_river(staged.at[i], rl, river + rl)
-        for k, store in enumerate(stores):
-
-            @pl.when(i == k)
-            def _(store=store):
-                store.start()
-
-    for store in stores:
-        store.wait()
+    for fetch in fetches:
+        fetch.wait()
+    for i, (shift, out) in enumerate(zip(shifts, outs)):
+
+        @pl.loop(0, 2)
+        def _(pair, i=i, out=out, group=(me + shift) & 7):
+            one_river(out, i, group, 2 * pair)
+            one_river(out, i, group, 2 * pair + 1)
 
 
 def pack(shifts, turn_cards, river_cards, policy, flop_reach, turn_policy, table, after):
+    anywhere = pl.BlockSpec(memory_space=pl.ANY)
     count = len(shifts)
-    smem = pl.BlockSpec(memory_space=pltpu.SMEM)
-    vmem = pl.BlockSpec(memory_space=pltpu.VMEM)
-    anywhere = pl.BlockSpec(memory_space=pl.ANY)
-    message = (4, ROWS, 8, 128)
     return pl.pallas_call(
         functools.partial(pack_kernel, shifts),
-        out_shape=[jax.ShapeDtypeStruct(message, jnp.float32)] * count,
-        in_specs=[smem] * 2 + [anywhere] + [vmem] * 3 + [anywhere] * len(after),
-        out_specs=[anywhere] * count,
+        out_shape=[jax.ShapeDtypeStruct((4, ROWS, 8, 128), jnp.float32)] * count,
+        in_specs=[anywhere] * (6 + len(after)),
+        out_specs=[pl.BlockSpec(memory_space=pltpu.VMEM)] * count,
         scratch_shapes=[
-            pltpu.VMEM((5304, 128), jnp.int32),
-            pltpu.VMEM((count,) + message, jnp.float32),
+            pltpu.SMEM((1,), jnp.int32),
+            pltpu.SMEM((1, 32), jnp.int32),
+            pltpu.VMEM((16, HANDS), jnp.float32),
+            pltpu.VMEM((16, HANDS), jnp.int32),
+            pltpu.VMEM((2, WIDE), jnp.int32),
+            pltpu.VMEM((count, 2, 584, 128), jnp.int32),
             pltpu.VMEM((176, 128), jnp.float32),
             pltpu.VMEM((2, 8, WIDE), jnp.float32),
             pltpu.VMEM((2, 8, 128), jnp.float32),
-            pltpu.SemaphoreType.DMA,
-            pltpu.SemaphoreType.DMA((count,)),
+            pltpu.SemaphoreType.DMA((5,)),
+            pltpu.SemaphoreType.DMA((count, 2, 8)),
         ],
         compiler_params=pltpu.CompilerParams(vmem_limit_bytes=VMEM_LIMIT),
         cost_estimate=pl.CostEstimate(flops=3000000, bytes_accessed=4000000, transcendentals=0),
@@ -285,29 +310,31 @@
     t = turn_card[0]
     me = lax.axis_index("hist")
     lane = lanes_of((8, 128))
-    out[...] = jnp.zeros_like(out)
-
-    @pl.loop(0, 4)
-    def _(rl):
-        r = river_card[0, 4 * me + rl]
-        for i, block in enumerate(blocks):
-            split_block(block.at[rl], 16 * i, high, fine)
-        chosen = early[rl] + chosen_rows(select, high, fine)
-        home = home_slots(lane, t, r)
-        home_tile, home_lane = home >> 7, home & 127
-        first = [jnp.zeros((8, 128), jnp.float32)] * 8
-        for start in range(0, WIDE, CHUNK):
-            value = jnp.dot(chosen, payoff[rl, :, start : start + CHUNK], preferred_element_type=jnp.float32)
-            value = (value[:128] + value[128:]) * scale[...]
-            reply = jnp.maximum(value[:64], value[64:])
-            for j in range(start // 128, min(start + CHUNK, WIDE) // 128):
-                moved = source_lanes(*cards_of(table, j), t, r) >= 0
-                for g in range(8):
-                    part = reply[8 * g : 8 * g + 8, 128 * j - start : 128 * j - start + 128]
-                    out[g, 1 + j] += jnp.where(moved, 0.0, part)
-                    first[g] = jnp.where(home_tile == j, pick(part, home_lane), first[g])
-        for g in range(8):
-            out[g, 0] += first[g]
+    rl = pl.program_id(0)
+
+    @pl.when(rl == 0)
+    def _():
+        out[...] = jnp.zeros_like(out)
+
+    r = river_card[0, 4 * me + rl]
+    for i, block in enumerate(blocks):
+        split_block(block.at[0], 16 * i, high, fine)
+    chosen = early[rl] + chosen_rows(select, high, fine)
+    home = home_slots(lane, t, r)
+    home_tile, home_lane = home >> 7, home & 127
+    first = [jnp.zeros((8, 128), jnp.float32)] * 8
+    for start in range(0, WIDE, CHUNK):
+        value = jnp.dot(chosen, payoff[rl, :, start : start + CHUNK], preferred_element_type=jnp.float32)
+        value = (value[:128] + value[128:]) * scale[...]
+        reply = jnp.maximum(value[:64], value[64:])
+        for j in range(start // 128, min(start + CHUNK, WIDE) // 128):
+            moved = source_lanes(*cards_of(table, j), t, r) >= 0
+            for g in range(8):
+                part = reply[8 * g : 8 * g + 8, 128 * j - start : 128 * j - start + 128]
+                out[g, 1 + j] += jnp.where(moved, 0.0, part)
+                first[g] = jnp.where(home_tile == j, pick(part, home_lane), first[g])
+    for g in range(8):
+        out[g, 0] += first[g]
 
 
 def replies(turn_cards, river_cards, payoff, early, select, scale, table, blocks):
@@ -316,8 +343,11 @@
     rows = 16 * len(blocks)
     return pl.pallas_call(
         reply_kernel,
+        grid=(4,),
         out_shape=jax.ShapeDtypeStruct((8, TILES + 1, 8, 128), jnp.float32),
-        in_specs=[smem] * 2 + [vmem] * (5 + len(blocks)),
+        in_specs=[smem] * 2
+        + [vmem] * 5
+        + [pl.BlockSpec((1, ROWS, 8, 128), lambda i: (i, 0, 0, 0))] * len(blocks),
         out_specs=vmem,
         scratch_shapes=[pltpu.VMEM((rows, WIDE), jnp.bfloat16)] * 2,
         compiler_params=pltpu.CompilerParams(vmem_limit_bytes=SMALL_LIMIT),
@@ -370,7 +400,7 @@
 
     first = exchange((2, 6), [])
     exchange((3, 5), [])
-    exchange((4, 1, 7, 0), first)
+    exchange((4, 1, 7, 0), [])
     payoff = payoffs(turn_cards, river_cards, hand_rank[0], compat, table)
     child = jnp.transpose(children).reshape(128)
     turn_of = jnp.zeros((8,), jnp.int32).at[jnp.array(ORDER)].set(jnp.arange(8, dtype=jnp.int32))

time: 129 us -> 127 us (0.984)
  Pallas kernels: 29.6 us -> 27.6 us
    pallas_call x3, Pallas kernels: 14.7 us -> 12.8 us  [pack(): pl.pallas_call(functools.partial(pack_kernel, shifts), out_shape=[jax.Sha...]
  transfers between devices with their start and end apart: 15 -> 15, of which waited for: 11 -> 10; matrix products, arithmetic and copies ran while one was open for 2% -> 3% of each run, Pallas kernels for 14% -> 14%
where the time goes in v3:
time: 127 us; the launch traced here: 125 us
  waiting for transfers between devices  55 us (43%)
  starting transfers between devices  34.8 us (27%)
  Pallas kernels  27.6 us (22%)
  local copies, waits for them, and re-layouts  6.04 us (5%)
  between operations  1.53 us (1%)
    ppermute x7, starting transfers between devices, send(): lax.ppermute(block, 'hist', [(i, (i + s) % groups) for i in range(groups)])  20 us
    ppermute x7, waiting for transfers between devices, send(): lax.ppermute(block, 'hist', [(i, (i + s) % groups) for i in range(groups)])  16.3 us
    all_to_all x1, waiting for transfers between devices, per_device(): arrived = lax.all_to_all(partial, 'hist', 0, 0, tiled=True)  13 us
    all_to_all x1, waiting for transfers between devices, per_device(): lax.all_to_all(jnp.broadcast_to(both, (groups,) + both.shape), 'hist', 0,...  12.8 us
    pallas_call x3, Pallas kernels, pack(): pl.pallas_call(functools.partial(pack_kernel, shifts), out_shape=[jax.Sha...  12.8 us
    ppermute x4, waiting for transfers between devices, turn_sum(): lax.ppermute(total, 'turn', [(i, i ^ flip * step) for i in range(size)])  11.7 us
    pallas_call x1, Pallas kernels, replies(): pl.pallas_call(reply_kernel, grid=(4,), out_shape=jax.ShapeDtypeStruct((8...  6.75 us
    ppermute x4, starting transfers between devices, turn_sum(): lax.ppermute(total, 'turn', [(i, i ^ flip * step) for i in range(size)])  5.9 us
  transfers between devices with their start and end apart: 15, of which 10 were waited for; matrix products, arithmetic and copies ran while one was open for 3% of the time, Pallas kernels for 14%

profile of v3, /device:TPU:6, one launch (start us, length us, event | category | flops | bytes accessed | tf_op | source)
XLA Modules:
  0.0 125.3 jit_solution(3453572724660985084)
XLA Ops:
  1.3 3.6 %pack.3 = (f32[4,17,8,128]{3,2,1,0:T(8,128)}, f32[4,17,8,128]{3,2,1,0:T(8,128)}) custom-call(s32[1]{0:T(128)S(6)} %copy.34.turn_card.turn_card_hbm, s32[1,32]{1,0:T(1,128)} %river_card.3, s32[5304,128]{1,0:T(8,128)} %bitcast.56, f32[16,1326]{1,0:T(8,128)} %bitcast.61, s32[16,1326]{1,0:T(8,128)} %bitcast.64, s32[2,1152]{1,0:T(2,128)} %constant.13.clone.table.table_hbm), custom_call_target="tpu_custom_call" | custom-call | flops 3000000 | bytes 4000000 | tf_op jit(solution)/shard_map/pack/pallas_call | solution.py:192
  4.9 3.3 %collective-permute-start = (f32[4,17,8,128]{3,2,1,0:T(8,128)}, f32[4,17,8,128]{3,2,1,0:T(8,128)S(1)}, u32[]{:S(2)}, u32[]{:S(2)}) collective-permute-start(f32[4,17,8,128]{3,2,1,0:T(8,128)} %get-tuple-element.10), channel_id=1, source_target_pairs={{0,2},{1,3},{2,4},{3,5},{4,6},{5,7},{6,0},{7,1},{8,10},{9,11},{10,... | collective-permute-start | bytes 835592 | tf_op jit(solution)/shard_map/ppermute | solution.py:392
  8.3 0.0 copy-start.6
  8.3 3.2 %collective-permute-start.1 = (f32[4,17,8,128]{3,2,1,0:T(8,128)}, f32[4,17,8,128]{3,2,1,0:T(8,128)S(1)}, u32[]{:S(2)}, u32[]{:S(2)}) collective-permute-start(f32[4,17,8,128]{3,2,1,0:T(8,128)} %get-tuple-element.11), channel_id=1, source_target_pairs={{0,6},{1,7},{2,0},{3,1},{4,2},{5,3},{6,4},{7,5},{8,14},{9,15},{10,... | collective-permute-start | bytes 835592 | tf_op jit(solution)/shard_map/ppermute | solution.py:392
  11.5 3.6 %pack.4 = (f32[4,17,8,128]{3,2,1,0:T(8,128)}, f32[4,17,8,128]{3,2,1,0:T(8,128)}) custom-call(s32[1]{0:T(128)S(6)} %copy.34.turn_card.turn_card_hbm, s32[1,32]{1,0:T(1,128)} %river_card.3, s32[5304,128]{1,0:T(8,128)} %bitcast.57, f32[16,1326]{1,0:T(8,128)} %bitcast.62, s32[16,1326]{1,0:T(8,128)} %bitcast.65, s32[2,1152]{1,0:T(2,128)} %constant.13.clone.table.table_hbm), custom_call_target="tpu_custom_call" | custom-call | flops 3000000 | bytes 4000000 | tf_op jit(solution)/shard_map/pack/pallas_call | solution.py:192
  15.1 2.1 %collective-permute-start.2 = (f32[4,17,8,128]{3,2,1,0:T(8,128)}, f32[4,17,8,128]{3,2,1,0:T(8,128)S(1)}, u32[]{:S(2)}, u32[]{:S(2)}) collective-permute-start(f32[4,17,8,128]{3,2,1,0:T(8,128)} %get-tuple-element.12), channel_id=1, source_target_pairs={{0,3},{1,4},{2,5},{3,6},{4,7},{5,0},{6,1},{7,2},{8,11},{9,12},{10,... | collective-permute-start | bytes 835592 | tf_op jit(solution)/shard_map/ppermute | solution.py:392
  17.2 3.0 %collective-permute-start.3 = (f32[4,17,8,128]{3,2,1,0:T(8,128)}, f32[4,17,8,128]{3,2,1,0:T(8,128)}, u32[]{:S(2)}, u32[]{:S(2)}) collective-permute-start(f32[4,17,8,128]{3,2,1,0:T(8,128)} %get-tuple-element.13), channel_id=1, source_target_pairs={{0,5},{1,6},{2,7},{3,0},{4,1},{5,2},{6,3},{7,4},{8,13},{9,14},{10,... | collective-permute-start | bytes 835592 | tf_op jit(solution)/shard_map/ppermute | solution.py:392
  20.2 5.5 %pack.5 = (f32[4,17,8,128]{3,2,1,0:T(8,128)}, f32[4,17,8,128]{3,2,1,0:T(8,128)}, f32[4,17,8,128]{3,2,1,0:T(8,128)}, f32[4,17,8,128]{3,2,1,0:T(8,128)}) custom-call(s32[1]{0:T(128)S(6)} %copy.34.turn_card.turn_card_hbm, s32[1,32]{1,0:T(1,128)} %river_card.3, s32[5304,128]{1,0:T(8,128)} %bitcast.58, f32[16,1326]{1,0:T(8,128)} %bitcast.63, ...), custom_call_target="tpu_custom_call" | custom-call | flops 3000000 | bytes 4000000 | tf_op jit(solution)/shard_map/pack/pallas_call | solution.py:192
  25.7 5.1 %collective-permute-start.4 = (f32[4,17,8,128]{3,2,1,0:T(8,128)}, f32[4,17,8,128]{3,2,1,0:T(8,128)}, u32[]{:S(2)}, u32[]{:S(2)}) collective-permute-start(f32[4,17,8,128]{3,2,1,0:T(8,128)} %get-tuple-element.15), channel_id=1, source_target_pairs={{0,4},{1,5},{2,6},{3,7},{4,0},{5,1},{6,2},{7,3},{8,12},{9,13},{10,... | collective-permute-start | bytes 835592 | tf_op jit(solution)/shard_map/ppermute | solution.py:392
  30.8 0.1 and.33
  30.9 0.1 reshape.74
  31.0 0.0 collective-permute-done.rest_0_
  31.0 1.1 collective-permute-start.5
  32.1 0.0 collective-permute-done.1.rest_1_
  32.1 2.2 %collective-permute-start.6 = (f32[4,17,8,128]{3,2,1,0:T(8,128)}, f32[4,17,8,128]{3,2,1,0:T(8,128)}, u32[]{:S(2)}, u32[]{:S(2)}) collective-permute-start(f32[4,17,8,128]{3,2,1,0:T(8,128)} %get-tuple-element.17), channel_id=1, source_target_pairs={{0,7},{1,0},{2,1},{3,2},{4,3},{5,4},{6,5},{7,6},{8,15},{9,8},{10,9... | collective-permute-start | bytes 835592 | tf_op jit(solution)/shard_map/ppermute | solution.py:392
  34.3 0.1 fusion
  34.4 0.7 slice.50.select
  35.1 0.2 select_reduce_fusion
  35.3 0.8 copy.23.scale
  36.0 0.7 copy-done.5
  36.8 5.2 %payoff.1 = bf16[4,1152,1152]{2,1,0:T(8,128)(2,1)S(1)} custom-call(s32[1]{0:T(128)S(6)} %copy.34.turn_card.turn_card_hbm, s32[1,32]{1,0:T(1,128)S(1)} %copy-done.6, s32[4,1326]{1,0:T(4,128)S(1)} %bitcast.55, bf16[1152,1152]{1,0:T(8,128)(2,1)S(1)} %copy-done, s32[2,1152]{1,0:T(2,128)S(1)} %copy-done.3), custom_call_target="tpu_custom_call" | custom-call | flops 21233664 | bytes 13271040 | tf_op jit(solution)/shard_map/payoff/pallas_call | solution.py:253
  42.0 0.0 copy-start.2
  42.0 0.0 copy-start.4
  42.0 7.8 %collective-permute-done.2.rest_2_ = f32[4,17,8,128]{3,2,1,0:T(8,128)S(1)} collective-permute-done((f32[4,17,8,128]{3,2,1,0:T(8,128)}, f32[4,17,8,128]{3,2,1,0:T(8,128)S(1)}, u32[]{:S(2)}, u32[]{:S(2)}) %collective-permute-start.2) | collective-permute-done | bytes 278560 | tf_op jit(solution)/shard_map/ppermute | solution.py:392
  49.8 2.8 %choose.1.early = bf16[4,256,1152]{2,1,0:T(8,128)(2,1)S(1)} custom-call(bf16[128,80]{1,0:T(8,128)(2,1)S(1)} %bitcast.54, f32[4,17,8,128]{3,2,1,0:T(8,128)S(1)} %collective-permute-done.rest_0_, f32[4,17,8,128]{3,2,1,0:T(8,128)S(1)} %collective-permute-done.1.rest_1_, f32[4,17,8,128]{3,2,1,0:T(8,128)S(1)} %collective-permute-done.2.rest_2_, ...), custom_call_target="tpu_custom_call" | custom-call | flops 188743680 | bytes 5000000 | tf_op jit(solution)/shard_map/choose/pallas_call | solution.py:295
  52.7 7.0 %collective-permute-done.5.rest_1_ = f32[4,17,8,128]{3,2,1,0:T(8,128)} collective-permute-done((f32[4,17,8,128]{3,2,1,0:T(8,128)}, f32[4,17,8,128]{3,2,1,0:T(8,128)}, u32[]{:S(2)}, u32[]{:S(2)}) %collective-permute-start.5) | collective-permute-done | bytes 278560 | tf_op jit(solution)/shard_map/ppermute | solution.py:392
  59.7 1.5 %collective-permute-done.6.rest_2_ = f32[4,17,8,128]{3,2,1,0:T(8,128)} collective-permute-done((f32[4,17,8,128]{3,2,1,0:T(8,128)}, f32[4,17,8,128]{3,2,1,0:T(8,128)}, u32[]{:S(2)}, u32[]{:S(2)}) %collective-permute-start.6) | collective-permute-done | bytes 278560 | tf_op jit(solution)/shard_map/ppermute | solution.py:392
  61.2 6.8 %reply.1 = f32[8,10,8,128]{3,2,1,0:T(8,128)} custom-call(s32[1]{0:T(128)S(6)} %copy.34.turn_card.turn_card_hbm, s32[1,32]{1,0:T(1,128)S(1)} %copy-done.6, bf16[4,1152,1152]{2,1,0:T(8,128)(2,1)S(1)} %payoff.1, bf16[4,256,1152]{2,1,0:T(8,128)(2,1)S(1)} %choose.1.early, bf16[128,48]{1,0:T(8,128)(2,1)S(1)} %copy-done.4, f32[128,1]{1,0:T(8,128)S(1)} %copy-done.2, ...), custom_call_target="tpu_custom_call" | custom-call | flops 2717908992 | bytes 10616832 | tf_op jit(solution)/shard_map/reply/pallas_call | solution.py:344
  68.0 5.3 %all-to-all-start = ((f32[8,10,8,128]{3,2,1,0:T(8,128)}), f32[8,10,8,128]{3,2,1,0:T(8,128)S(1)}, u32[]{:S(2)}, u32[]{:S(2)}) async-start(f32[8,10,8,128]{3,2,1,0:T(8,128)} %reply.1), calls=%async_computation | async-start | bytes 655360 | tf_op jit(solution)/shard_map/all_to_all | solution.py:417
  73.2 13.0 %all-to-all-done = f32[8,10,8,128]{3,2,1,0:T(8,128)S(1)} async-done(((f32[8,10,8,128]{3,2,1,0:T(8,128)}), f32[8,10,8,128]{3,2,1,0:T(8,128)S(1)}, u32[]{:S(2)}, u32[]{:S(2)}) %all-to-all-start) | async-done | bytes 327712 | tf_op jit(solution)/shard_map/all_to_all | solution.py:417
  86.2 0.1 collective-permute-start.7
  86.3 1.2 collective-permute-done.7
  87.5 1.6 %collective-permute-start.8 = (f32[5,8,128]{2,1,0:T(8,128)S(1)}, f32[5,8,128]{2,1,0:T(8,128)S(1)}, u32[]{:S(2)}, u32[]{:S(2)}) collective-permute-start(f32[5,8,128]{2,1,0:T(8,128)S(1)} %dynamic-slice_add_fusion), channel_id=1, source_target_pairs={{0,16},{8,24},{16,0},{24,8},{32,48},{40,56},{48,32},{56,40},{64,80... | collective-permute-start | bytes 61448 | tf_op jit(solution)/shard_map/ppermute | solution.py:377
  89.1 2.2 %collective-permute-done.8 = f32[5,8,128]{2,1,0:T(8,128)S(1)} collective-permute-done((f32[5,8,128]{2,1,0:T(8,128)S(1)}, f32[5,8,128]{2,1,0:T(8,128)S(1)}, u32[]{:S(2)}, u32[]{:S(2)}) %collective-permute-start.8) | collective-permute-done | bytes 20512 | tf_op jit(solution)/shard_map/ppermute | solution.py:377
  91.3 3.0 %collective-permute-start.9 = (f32[5,8,128]{2,1,0:T(8,128)S(1)}, f32[5,8,128]{2,1,0:T(8,128)S(1)}, u32[]{:S(2)}, u32[]{:S(2)}) collective-permute-start(f32[5,8,128]{2,1,0:T(8,128)S(1)} %add.59), channel_id=1, source_target_pairs={{0,48},{8,56},{16,32},{24,40},{32,16},{40,24},{48,0},{56,8},{64,11... | collective-permute-start | bytes 61448 | tf_op jit(solution)/shard_map/ppermute | solution.py:377
  94.3 2.0 %collective-permute-done.9 = f32[5,8,128]{2,1,0:T(8,128)S(1)} collective-permute-done((f32[5,8,128]{2,1,0:T(8,128)S(1)}, f32[5,8,128]{2,1,0:T(8,128)S(1)}, u32[]{:S(2)}, u32[]{:S(2)}) %collective-permute-start.9) | collective-permute-done | bytes 20512 | tf_op jit(solution)/shard_map/ppermute | solution.py:377
  96.3 0.8 collective-permute-start.10
  97.1 3.0 %collective-permute-done.10 = f32[5,8,128]{2,1,0:T(8,128)S(1)} collective-permute-done((f32[5,8,128]{2,1,0:T(8,128)S(1)}, f32[5,8,128]{2,1,0:T(8,128)S(1)}, u32[]{:S(2)}, u32[]{:S(2)}) %collective-permute-start.10) | collective-permute-done | bytes 20512 | tf_op jit(solution)/shard_map/ppermute | solution.py:377
  100.1 0.5 collective-permute-start.11
  100.6 4.5 %collective-permute-done.11 = f32[5,8,128]{2,1,0:T(8,128)S(1)} collective-permute-done((f32[5,8,128]{2,1,0:T(8,128)S(1)}, f32[5,8,128]{2,1,0:T(8,128)S(1)}, u32[]{:S(2)}, u32[]{:S(2)}) %collective-permute-start.11) | collective-permute-done | bytes 20512 | tf_op jit(solution)/shard_map/ppermute | solution.py:377
  105.1 0.8 broadcast_in_dim.30
  105.9 3.5 %all-to-all-start.1 = ((f32[8,15,8,128]{3,2,1,0:T(8,128)}), f32[8,15,8,128]{3,2,1,0:T(8,128)S(1)}, u32[]{:S(2)}, u32[]{:S(2)}) async-start(f32[8,15,8,128]{3,2,1,0:T(8,128)} %broadcast_in_dim.30), calls=%async_computation.1 | async-start | bytes 983040 | tf_op jit(solution)/shard_map/all_to_all | solution.py:421
  109.4 12.8 %all-to-all-done.1 = f32[8,15,8,128]{3,2,1,0:T(8,128)S(1)} async-done(((f32[8,15,8,128]{3,2,1,0:T(8,128)}), f32[8,15,8,128]{3,2,1,0:T(8,128)S(1)}, u32[]{:S(2)}, u32[]{:S(2)}) %all-to-all-start.1) | async-done | bytes 491552 | tf_op jit(solution)/shard_map/all_to_all | solution.py:421
  122.3 0.1 collective-permute-start.12
  122.5 0.2 concatenate.13
  122.7 1.3 %reshape_reshape.3 = f32[1,84864]{1,0:T(1,128)} reshape(f32[64,1326]{1,0:T(8,128)S(1)} %concatenate.13) | data formatting | bytes 678912 | tf_op jit(solution)/shard_map/reshape;reshape | solution.py:425
  124.1 0.2 concatenate.15
  124.3 1.0 reshape.80
  (38 shorter events, 0.3 us)
Async XLA Ops:
  4.9 26.1 %collective-permute-start = (f32[4,17,8,128]{3,2,1,0:T(8,128)}, f32[4,17,8,128]{3,2,1,0:T(8,128)S(1)}, u32[]{:S(2)}, u32[]{:S(2)}) collective-permute-start(f32[4,17,8,128]{3,2,1,0:T(8,128)} %get-tuple-element.10), channel_id=1, source_target_pairs={{0,2},{1,3},{2,4},{3,5},{4,6},{5,7},{6,0},{7,1},{8,10},{9,11},{10,... | collective-permute-start | bytes 835592 | tf_op jit(solution)/shard_map/ppermute | solution.py:392
  8.3 22.5 %copy-start.7 = (s32[64,2]{0,1:T(2,128)S(1)}, s32[64,2]{0,1:T(2,128)}, u32[]{:S(2)}) copy-start(s32[64,2]{0,1:T(2,128)} %param.17) | copy-start | bytes 1540
  8.3 26.8 %copy-start.8 = (s32[128]{0:T(128)S(1)}, s32[128]{0:T(128)}, u32[]{:S(2)}) copy-start(s32[128]{0:T(128)} %param.18) | copy-start | bytes 1540
  8.3 27.8 %copy-start = (bf16[1152,1152]{1,0:T(8,128)(2,1)S(1)}, bf16[1152,1152]{1,0:T(8,128)(2,1)}, u32[]{:S(2)}) copy-start(bf16[1152,1152]{1,0:T(8,128)(2,1)} %constant.14.clone.compat) | copy-start | bytes 7962628
  8.3 27.8 %copy-start.3 = (s32[2,1152]{1,0:T(2,128)S(1)}, s32[2,1152]{1,0:T(2,128)}, u32[]{:S(2)}) copy-start(s32[2,1152]{1,0:T(2,128)} %constant.13.clone.table.table_hbm) | copy-start | bytes 27652
  8.3 27.8 %copy-start.6 = (s32[1,32]{1,0:T(1,128)S(1)}, s32[1,32]{1,0:T(1,128)}, u32[]{:S(2)}) copy-start(s32[1,32]{1,0:T(1,128)} %river_card.3) | copy-start | bytes 388
  8.3 23.8 %collective-permute-start.1 = (f32[4,17,8,128]{3,2,1,0:T(8,128)}, f32[4,17,8,128]{3,2,1,0:T(8,128)S(1)}, u32[]{:S(2)}, u32[]{:S(2)}) collective-permute-start(f32[4,17,8,128]{3,2,1,0:T(8,128)} %get-tuple-element.11), channel_id=1, source_target_pairs={{0,6},{1,7},{2,0},{3,1},{4,2},{5,3},{6,4},{7,5},{8,14},{9,15},{10,... | collective-permute-start | bytes 835592 | tf_op jit(solution)/shard_map/ppermute | solution.py:392
  15.1 34.8 %collective-permute-start.2 = (f32[4,17,8,128]{3,2,1,0:T(8,128)}, f32[4,17,8,128]{3,2,1,0:T(8,128)S(1)}, u32[]{:S(2)}, u32[]{:S(2)}) collective-permute-start(f32[4,17,8,128]{3,2,1,0:T(8,128)} %get-tuple-element.12), channel_id=1, source_target_pairs={{0,3},{1,4},{2,5},{3,6},{4,7},{5,0},{6,1},{7,2},{8,11},{9,12},{10,... | collective-permute-start | bytes 835592 | tf_op jit(solution)/shard_map/ppermute | solution.py:392
  17.2 32.7 %collective-permute-start.3 = (f32[4,17,8,128]{3,2,1,0:T(8,128)}, f32[4,17,8,128]{3,2,1,0:T(8,128)}, u32[]{:S(2)}, u32[]{:S(2)}) collective-permute-start(f32[4,17,8,128]{3,2,1,0:T(8,128)} %get-tuple-element.13), channel_id=1, source_target_pairs={{0,5},{1,6},{2,7},{3,0},{4,1},{5,2},{6,3},{7,4},{8,13},{9,14},{10,... | collective-permute-start | bytes 835592 | tf_op jit(solution)/shard_map/ppermute | solution.py:392
  25.7 26.9 %collective-permute-start.4 = (f32[4,17,8,128]{3,2,1,0:T(8,128)}, f32[4,17,8,128]{3,2,1,0:T(8,128)}, u32[]{:S(2)}, u32[]{:S(2)}) collective-permute-start(f32[4,17,8,128]{3,2,1,0:T(8,128)} %get-tuple-element.15), channel_id=1, source_target_pairs={{0,4},{1,5},{2,6},{3,7},{4,0},{5,1},{6,2},{7,3},{8,12},{9,13},{10,... | collective-permute-start | bytes 835592 | tf_op jit(solution)/shard_map/ppermute | solution.py:392
  31.0 28.7 %collective-permute-start.5 = (f32[4,17,8,128]{3,2,1,0:T(8,128)}, f32[4,17,8,128]{3,2,1,0:T(8,128)}, u32[]{:S(2)}, u32[]{:S(2)}) collective-permute-start(f32[4,17,8,128]{3,2,1,0:T(8,128)} %get-tuple-element.16), channel_id=1, source_target_pairs={{0,1},{1,2},{2,3},{3,4},{4,5},{5,6},{6,7},{7,0},{8,9},{9,10},{10,1... | collective-permute-start | bytes 835592 | tf_op jit(solution)/shard_map/ppermute | solution.py:392
  32.1 29.1 %collective-permute-start.6 = (f32[4,17,8,128]{3,2,1,0:T(8,128)}, f32[4,17,8,128]{3,2,1,0:T(8,128)}, u32[]{:S(2)}, u32[]{:S(2)}) collective-permute-start(f32[4,17,8,128]{3,2,1,0:T(8,128)} %get-tuple-element.17), channel_id=1, source_target_pairs={{0,7},{1,0},{2,1},{3,2},{4,3},{5,4},{6,5},{7,6},{8,15},{9,8},{10,9... | collective-permute-start | bytes 835592 | tf_op jit(solution)/shard_map/ppermute | solution.py:392
  36.0 0.7 copy-start.5
  36.8 13.1 %copy-start.1 = (f32[4,17,8,128]{3,2,1,0:T(8,128)S(1)}, f32[4,17,8,128]{3,2,1,0:T(8,128)}, u32[]{:S(2)}) copy-start(f32[4,17,8,128]{3,2,1,0:T(8,128)} %get-tuple-element.14.rest_4_) | copy-start | bytes 835588
  42.0 19.2 %copy-start.2 = (f32[128,1]{1,0:T(8,128)S(1)}, f32[128,1]{1,0:T(8,128)}, u32[]{:S(2)}) copy-start(f32[128,1]{1,0:T(8,128)} %copy.23.scale) | copy-start | bytes 1540
  42.0 19.2 %copy-start.4 = (bf16[128,48]{1,0:T(8,128)(2,1)S(1)}, bf16[128,48]{1,0:T(8,128)(2,1)}, u32[]{:S(2)}) copy-start(bf16[128,48]{1,0:T(8,128)(2,1)} %slice.50.select) | copy-start | bytes 36868
  68.0 18.2 %all-to-all-start = ((f32[8,10,8,128]{3,2,1,0:T(8,128)}), f32[8,10,8,128]{3,2,1,0:T(8,128)S(1)}, u32[]{:S(2)}, u32[]{:S(2)}) async-start(f32[8,10,8,128]{3,2,1,0:T(8,128)} %reply.1), calls=%async_computation | async-start | bytes 655360 | tf_op jit(solution)/shard_map/all_to_all | solution.py:417
  86.2 1.3 %collective-permute-start.7 = (f32[5,8,128]{2,1,0:T(8,128)S(1)}, f32[5,8,128]{2,1,0:T(8,128)S(1)}, u32[]{:S(2)}, u32[]{:S(2)}) collective-permute-start(f32[5,8,128]{2,1,0:T(8,128)S(1)} %constant_dynamic-slice_fusion), channel_id=1, source_target_pairs={{0,8},{8,0},{16,24},{24,16},{32,40},{40,32},{48,56},{56,48},{64,72... | collective-permute-start | bytes 61448 | tf_op jit(solution)/shard_map/ppermute | solution.py:373
  87.5 3.8 %collective-permute-start.8 = (f32[5,8,128]{2,1,0:T(8,128)S(1)}, f32[5,8,128]{2,1,0:T(8,128)S(1)}, u32[]{:S(2)}, u32[]{:S(2)}) collective-permute-start(f32[5,8,128]{2,1,0:T(8,128)S(1)} %dynamic-slice_add_fusion), channel_id=1, source_target_pairs={{0,16},{8,24},{16,0},{24,8},{32,48},{40,56},{48,32},{56,40},{64,80... | collective-permute-start | bytes 61448 | tf_op jit(solution)/shard_map/ppermute | solution.py:377
  91.3 5.0 %collective-permute-start.9 = (f32[5,8,128]{2,1,0:T(8,128)S(1)}, f32[5,8,128]{2,1,0:T(8,128)S(1)}, u32[]{:S(2)}, u32[]{:S(2)}) collective-permute-start(f32[5,8,128]{2,1,0:T(8,128)S(1)} %add.59), channel_id=1, source_target_pairs={{0,48},{8,56},{16,32},{24,40},{32,16},{40,24},{48,0},{56,8},{64,11... | collective-permute-start | bytes 61448 | tf_op jit(solution)/shard_map/ppermute | solution.py:377
  96.3 3.8 %collective-permute-start.10 = (f32[5,8,128]{2,1,0:T(8,128)S(1)}, f32[5,8,128]{2,1,0:T(8,128)S(1)}, u32[]{:S(2)}, u32[]{:S(2)}) collective-permute-start(f32[5,8,128]{2,1,0:T(8,128)S(1)} %add.60), channel_id=1, source_target_pairs={{0,64},{8,72},{16,80},{24,88},{32,96},{40,104},{48,112},{56,120},{... | collective-permute-start | bytes 61448 | tf_op jit(solution)/shard_map/ppermute | solution.py:377
  100.1 5.0 %collective-permute-start.11 = (f32[5,8,128]{2,1,0:T(8,128)S(1)}, f32[5,8,128]{2,1,0:T(8,128)S(1)}, u32[]{:S(2)}, u32[]{:S(2)}) collective-permute-start(f32[5,8,128]{2,1,0:T(8,128)S(1)} %add.61), channel_id=1, source_target_pairs={{0,192},{8,200},{16,208},{24,216},{32,224},{40,232},{48,240},{56,2... | collective-permute-start | bytes 61448 | tf_op jit(solution)/shard_map/ppermute | solution.py:377
  105.9 16.3 %all-to-all-start.1 = ((f32[8,15,8,128]{3,2,1,0:T(8,128)}), f32[8,15,8,128]{3,2,1,0:T(8,128)S(1)}, u32[]{:S(2)}, u32[]{:S(2)}) async-start(f32[8,15,8,128]{3,2,1,0:T(8,128)} %broadcast_in_dim.30), calls=%async_computation.1 | async-start | bytes 983040 | tf_op jit(solution)/shard_map/all_to_all | solution.py:421
  122.3 1.7 %collective-permute-start.12 = (f32[8,5,8,128]{3,2,1,0:T(8,128)S(1)}, f32[8,5,8,128]{3,2,1,0:T(8,128)S(1)}, u32[]{:S(2)}, u32[]{:S(2)}) collective-permute-start(f32[8,5,8,128]{3,2,1,0:T(8,128)S(1)} %slice.55), channel_id=1, source_target_pairs={{0,8},{8,0},{16,24},{24,16},{32,40},{40,32},{48,56},{56,48},{64,72... | collective-permute-start | bytes 491528 | tf_op jit(solution)/shard_map/ppermute | solution.py:423

commit v4 on v3

--- a/solution.py
+++ b/solution.py
@@ -17,10 +17,10 @@
 ROWS = 17
 ORDER = (2, 6, 3, 5, 0, 4, 1, 7)
 EARLY = 5
-CHUNK = 256
+CHUNK = 1152
 FETCH = 56
 VMEM_LIMIT = 56 * 1024 * 1024
-SMALL_LIMIT = 16 * 1024 * 1024
+SMALL_LIMIT = 24 * 1024 * 1024
 
 
 def slot_cards():
@@ -263,50 +263,59 @@
     )(turn_cards, river_cards, ranks, compat, table)
 
 
-def split_block(block, row, high, fine):
+def split(value):
+    upper = value.astype(jnp.bfloat16)
+    return upper, (value - upper.astype(jnp.float32)).astype(jnp.bfloat16)
+
+
+def split_blocks(blocks, rows):
     lane = lanes_of((8, 128))
-    for j in range(TILES):
-        if j < 8:
-            pair = [block[j], block[8 + j]]
-        else:
-            tails = block[16]
-            pair = [jnp.where(lane < 64, v, 0.0) for v in (tails, pltpu.roll(tails, 64, 1))]
-        both = jnp.concatenate(pair, axis=0)
-        upper = both.astype(jnp.bfloat16)
-        high[row : row + 16, 128 * j : 128 * j + 128] = upper
-        fine[row : row + 16, 128 * j : 128 * j + 128] = (both - upper.astype(jnp.float32)).astype(jnp.bfloat16)
-
-
-def chosen_rows(select, high, fine):
-    parts = [jnp.dot(select[...], part[...], preferred_element_type=jnp.float32) for part in (high, fine)]
-    return jnp.concatenate([part.astype(jnp.bfloat16) for part in parts], axis=0)
-
-
-def choose_kernel(select, *rest):
-    blocks, (out, high, fine) = rest[:-3], rest[-3:]
+    below = 16 * len(blocks)
     for i, block in enumerate(blocks):
-        split_block(block.at[0], 16 * i, high, fine)
-    out[0] = chosen_rows(select, high, fine)
-
-
-def choose(select, blocks):
+        for j in range(TILES):
+            if j < 8:
+                pair = [block[0, j], block[0, 8 + j]]
+            else:
+                tails = block[0, 16]
+                pair = [jnp.where(lane < 64, v, 0.0) for v in (tails, pltpu.roll(tails, 64, 1))]
+            upper, lower = split(jnp.concatenate(pair, axis=0))
+            rows[16 * i : 16 * i + 16, 128 * j : 128 * j + 128] = upper
+            rows[below + 16 * i : below + 16 * i + 16, 128 * j : 128 * j + 128] = lower
+
+
+def early_kernel(payoff, select, *rest):
+    blocks, (out, rows) = rest[:-2], rest[-2:]
+    rl = pl.program_id(0)
+    split_blocks(blocks, rows)
+    below = 16 * len(blocks)
+    parts = [
+        jnp.dot(select[...], rows[begin : begin + below], preferred_element_type=jnp.float32).astype(jnp.bfloat16)
+        for begin in (0, below)
+    ]
+    value = jnp.dot(jnp.concatenate(parts, axis=0), payoff[rl], preferred_element_type=jnp.float32)
+    out[0] = value[:128] + value[128:]
+
+
+def early_values(payoff, select, blocks):
     vmem = pl.BlockSpec(memory_space=pltpu.VMEM)
     rows = 16 * len(blocks)
     return pl.pallas_call(
-        choose_kernel,
+        early_kernel,
         grid=(4,),
-        out_shape=jax.ShapeDtypeStruct((4, 256, WIDE), jnp.bfloat16),
-        in_specs=[vmem] + [pl.BlockSpec((1, ROWS, 8, 128), lambda i: (i, 0, 0, 0))] * len(blocks),
-        out_specs=pl.BlockSpec((1, 256, WIDE), lambda i: (i, 0, 0)),
-        scratch_shapes=[pltpu.VMEM((rows, WIDE), jnp.bfloat16)] * 2,
+        out_shape=jax.ShapeDtypeStruct((4, 128, WIDE), jnp.float32),
+        in_specs=[vmem] * 2 + [pl.BlockSpec((1, ROWS, 8, 128), lambda i: (i, 0, 0, 0))] * len(blocks),
+        out_specs=pl.BlockSpec((1, 128, WIDE), lambda i: (i, 0, 0)),
+        scratch_shapes=[pltpu.VMEM((2 * rows, WIDE), jnp.bfloat16)],
         compiler_params=pltpu.CompilerParams(vmem_limit_bytes=SMALL_LIMIT),
-        cost_estimate=pl.CostEstimate(flops=4 * 512 * rows * WIDE, bytes_accessed=5000000, transcendentals=0),
-        name="choose",
-    )(select, *blocks)
+        cost_estimate=pl.CostEstimate(
+            flops=4 * 2 * 256 * WIDE * WIDE, bytes_accessed=8 * WIDE * WIDE, transcendentals=0
+        ),
+        name="early",
+    )(payoff, select, *blocks)
 
 
 def reply_kernel(turn_card, river_card, payoff, early, select, scale, table, *rest):
-    blocks, (out, high, fine) = rest[:-3], rest[-3:]
+    blocks, (out, rows) = rest[:-2], rest[-2:]
     t = turn_card[0]
     me = lax.axis_index("hist")
     lane = lanes_of((8, 128))
@@ -317,15 +326,16 @@
         out[...] = jnp.zeros_like(out)
 
     r = river_card[0, 4 * me + rl]
-    for i, block in enumerate(blocks):
-        split_block(block.at[0], 16 * i, high, fine)
-    chosen = early[rl] + chosen_rows(select, high, fine)
+    split_blocks(blocks, rows)
+    below = 16 * len(blocks)
     home = home_slots(lane, t, r)
     home_tile, home_lane = home >> 7, home & 127
     first = [jnp.zeros((8, 128), jnp.float32)] * 8
     for start in range(0, WIDE, CHUNK):
-        value = jnp.dot(chosen, payoff[rl, :, start : start + CHUNK], preferred_element_type=jnp.float32)
-        value = (value[:128] + value[128:]) * scale[...]
+        late = jnp.dot(rows[...], payoff[rl, :, start : start + CHUNK], preferred_element_type=jnp.float32)
+        parts = jnp.concatenate(split(late[:below] + late[below:]), axis=0)
+        value = jnp.dot(select[...], parts, preferred_element_type=jnp.float32)
+        value = (value + early[rl, :, start : start + CHUNK]) * scale[...]
         reply = jnp.maximum(value[:64], value[64:])
         for j in range(start // 128, min(start + CHUNK, WIDE) // 128):
             moved = source_lanes(*cards_of(table, j), t, r) >= 0
@@ -349,7 +359,7 @@
         + [vmem] * 5
         + [pl.BlockSpec((1, ROWS, 8, 128), lambda i: (i, 0, 0, 0))] * len(blocks),
         out_specs=vmem,
-        scratch_shapes=[pltpu.VMEM((rows, WIDE), jnp.bfloat16)] * 2,
+        scratch_shapes=[pltpu.VMEM((2 * rows, WIDE), jnp.bfloat16)],
         compiler_params=pltpu.CompilerParams(vmem_limit_bytes=SMALL_LIMIT),
         cost_estimate=pl.CostEstimate(
             flops=4 * 2 * 256 * WIDE * WIDE, bytes_accessed=8 * WIDE * WIDE, transcendentals=0
@@ -411,9 +421,10 @@
         axis=1,
         keepdims=True,
     )
-    early = choose(select[:, : 16 * EARLY], [got[s] for s in ORDER[:EARLY]])
+    early = early_values(payoff, select[:, : 16 * EARLY], [got[s] for s in ORDER[:EARLY]])
     late = [got[s] for s in ORDER[EARLY:]]
-    partial = replies(turn_cards, river_cards, payoff, early, select[:, 16 * EARLY :], scale, table, late)
+    twice = jnp.concatenate([select[:, 16 * EARLY :]] * 2, axis=1)
+    partial = replies(turn_cards, river_cards, payoff, early, twice, scale, table, late)
     arrived = lax.all_to_all(partial, "hist", 0, 0, tiled=True)
     value = jnp.sum(arrived, axis=0) * (1.0 / 32.0)
     half, pairs, core = turn_sum(value, turns)

time: 127 us -> 126 us (level)
  waiting for transfers between devices: 55 us -> 51.3 us
  Pallas kernels: 27.6 us -> 28.9 us
    ppermute x7, waiting for transfers between devices: 16.3 us -> 13.4 us  [send(): lax.ppermute(block, 'hist', [(i, (i + s) % groups) for i in range(groups)])]
    pallas_call x1, Pallas kernels: 2.81 us -> 5.72 us  [early_values(): pl.pallas_call(early_kernel, grid=(4,), out_shape=jax.ShapeDtypeStruct((4...]
    pallas_call x1, Pallas kernels: 6.75 us -> 5.18 us  [replies(): pl.pallas_call(reply_kernel, grid=(4,), out_shape=jax.ShapeDtypeStruct((8...]
  transfers between devices with their start and end apart: 15 -> 15, of which waited for: 10 -> 10; matrix products, arithmetic and copies ran while one was open for 3% -> 3% of each run, Pallas kernels for 14% -> 16%
where the time goes in v4:
time: 126 us; the launch traced here: 124 us
  waiting for transfers between devices  51.3 us (41%)
  starting transfers between devices  35.6 us (28%)
  Pallas kernels  28.9 us (23%)
  local copies, waits for them, and re-layouts  5.41 us (4%)
  between operations  1.53 us (1%)
    ppermute x7, starting transfers between devices, send(): lax.ppermute(block, 'hist', [(i, (i + s) % groups) for i in range(groups)])  20 us
    ppermute x7, waiting for transfers between devices, send(): lax.ppermute(block, 'hist', [(i, (i + s) % groups) for i in range(groups)])  13.4 us
    all_to_all x1, waiting for transfers between devices, per_device(): lax.all_to_all(jnp.broadcast_to(both, (groups,) + both.shape), 'hist', 0,...  12.8 us
    pallas_call x3, Pallas kernels, pack(): pl.pallas_call(functools.partial(pack_kernel, shifts), out_shape=[jax.Sha...  12.7 us
    all_to_all x1, waiting for transfers between devices, per_device(): arrived = lax.all_to_all(partial, 'hist', 0, 0, tiled=True)  12.2 us
    ppermute x4, waiting for transfers between devices, turn_sum(): lax.ppermute(total, 'turn', [(i, i ^ flip * step) for i in range(size)])  11.6 us
    all_to_all x1, starting transfers between devices, per_device(): arrived = lax.all_to_all(partial, 'hist', 0, 0, tiled=True)  6 us
    ppermute x4, starting transfers between devices, turn_sum(): lax.ppermute(total, 'turn', [(i, i ^ flip * step) for i in range(size)])  5.9 us
  transfers between devices with their start and end apart: 15, of which 10 were waited for; matrix products, arithmetic and copies ran while one was open for 3% of the time, Pallas kernels for 16%

profile of v4, /device:TPU:6, one launch (start us, length us, event | category | flops | bytes accessed | tf_op | source)
XLA Modules:
  0.0 123.8 jit_solution(15183207567399777354)
XLA Ops:
  1.3 3.6 %pack.3 = (f32[4,17,8,128]{3,2,1,0:T(8,128)}, f32[4,17,8,128]{3,2,1,0:T(8,128)}) custom-call(s32[1]{0:T(128)S(6)} %copy.34.turn_card.turn_card_hbm, s32[1,32]{1,0:T(1,128)} %river_card.3, s32[5304,128]{1,0:T(8,128)} %bitcast.56, f32[16,1326]{1,0:T(8,128)} %bitcast.61, s32[16,1326]{1,0:T(8,128)} %bitcast.64, s32[2,1152]{1,0:T(2,128)} %constant.13.clone.table.table_hbm), custom_call_target="tpu_custom_call" | custom-call | flops 3000000 | bytes 4000000 | tf_op jit(solution)/shard_map/pack/pallas_call | solution.py:192
  4.9 3.3 %collective-permute-start = (f32[4,17,8,128]{3,2,1,0:T(8,128)}, f32[4,17,8,128]{3,2,1,0:T(8,128)S(1)}, u32[]{:S(2)}, u32[]{:S(2)}) collective-permute-start(f32[4,17,8,128]{3,2,1,0:T(8,128)} %get-tuple-element.10), channel_id=1, source_target_pairs={{0,2},{1,3},{2,4},{3,5},{4,6},{5,7},{6,0},{7,1},{8,10},{9,11},{10,... | collective-permute-start | bytes 835592 | tf_op jit(solution)/shard_map/ppermute | solution.py:402
  8.3 0.0 copy-start.6
  8.3 3.2 %collective-permute-start.1 = (f32[4,17,8,128]{3,2,1,0:T(8,128)}, f32[4,17,8,128]{3,2,1,0:T(8,128)S(1)}, u32[]{:S(2)}, u32[]{:S(2)}) collective-permute-start(f32[4,17,8,128]{3,2,1,0:T(8,128)} %get-tuple-element.11), channel_id=1, source_target_pairs={{0,6},{1,7},{2,0},{3,1},{4,2},{5,3},{6,4},{7,5},{8,14},{9,15},{10,... | collective-permute-start | bytes 835592 | tf_op jit(solution)/shard_map/ppermute | solution.py:402
  11.5 3.6 %pack.4 = (f32[4,17,8,128]{3,2,1,0:T(8,128)}, f32[4,17,8,128]{3,2,1,0:T(8,128)}) custom-call(s32[1]{0:T(128)S(6)} %copy.34.turn_card.turn_card_hbm, s32[1,32]{1,0:T(1,128)} %river_card.3, s32[5304,128]{1,0:T(8,128)} %bitcast.57, f32[16,1326]{1,0:T(8,128)} %bitcast.62, s32[16,1326]{1,0:T(8,128)} %bitcast.65, s32[2,1152]{1,0:T(2,128)} %constant.13.clone.table.table_hbm), custom_call_target="tpu_custom_call" | custom-call | flops 3000000 | bytes 4000000 | tf_op jit(solution)/shard_map/pack/pallas_call | solution.py:192
  15.1 2.1 %collective-permute-start.2 = (f32[4,17,8,128]{3,2,1,0:T(8,128)}, f32[4,17,8,128]{3,2,1,0:T(8,128)}, u32[]{:S(2)}, u32[]{:S(2)}) collective-permute-start(f32[4,17,8,128]{3,2,1,0:T(8,128)} %get-tuple-element.12), channel_id=1, source_target_pairs={{0,3},{1,4},{2,5},{3,6},{4,7},{5,0},{6,1},{7,2},{8,11},{9,12},{10,... | collective-permute-start | bytes 835592 | tf_op jit(solution)/shard_map/ppermute | solution.py:402
  17.2 3.0 %collective-permute-start.3 = (f32[4,17,8,128]{3,2,1,0:T(8,128)}, f32[4,17,8,128]{3,2,1,0:T(8,128)}, u32[]{:S(2)}, u32[]{:S(2)}) collective-permute-start(f32[4,17,8,128]{3,2,1,0:T(8,128)} %get-tuple-element.13), channel_id=1, source_target_pairs={{0,5},{1,6},{2,7},{3,0},{4,1},{5,2},{6,3},{7,4},{8,13},{9,14},{10,... | collective-permute-start | bytes 835592 | tf_op jit(solution)/shard_map/ppermute | solution.py:402
  20.2 5.5 %pack.5 = (f32[4,17,8,128]{3,2,1,0:T(8,128)}, f32[4,17,8,128]{3,2,1,0:T(8,128)}, f32[4,17,8,128]{3,2,1,0:T(8,128)}, f32[4,17,8,128]{3,2,1,0:T(8,128)}) custom-call(s32[1]{0:T(128)S(6)} %copy.34.turn_card.turn_card_hbm, s32[1,32]{1,0:T(1,128)} %river_card.3, s32[5304,128]{1,0:T(8,128)} %bitcast.58, f32[16,1326]{1,0:T(8,128)} %bitcast.63, ...), custom_call_target="tpu_custom_call" | custom-call | flops 3000000 | bytes 4000000 | tf_op jit(solution)/shard_map/pack/pallas_call | solution.py:192
  25.7 5.1 %collective-permute-start.4 = (f32[4,17,8,128]{3,2,1,0:T(8,128)}, f32[4,17,8,128]{3,2,1,0:T(8,128)S(1)}, u32[]{:S(2)}, u32[]{:S(2)}) collective-permute-start(f32[4,17,8,128]{3,2,1,0:T(8,128)} %get-tuple-element.15), channel_id=1, source_target_pairs={{0,4},{1,5},{2,6},{3,7},{4,0},{5,1},{6,2},{7,3},{8,12},{9,13},{10,... | collective-permute-start | bytes 835592 | tf_op jit(solution)/shard_map/ppermute | solution.py:402
  30.8 0.1 and.33
  30.8 0.1 reshape.74
  30.9 0.1 fusion
  31.0 0.1 slice.50
  31.1 0.2 select_reduce_fusion
  31.3 0.0 collective-permute-done.rest_0_
  31.3 1.1 collective-permute-start.5
  32.4 0.0 collective-permute-done.1.rest_1_
  32.4 2.2 %collective-permute-start.6 = (f32[4,17,8,128]{3,2,1,0:T(8,128)}, f32[4,17,8,128]{3,2,1,0:T(8,128)}, u32[]{:S(2)}, u32[]{:S(2)}) collective-permute-start(f32[4,17,8,128]{3,2,1,0:T(8,128)} %get-tuple-element.17), channel_id=1, source_target_pairs={{0,7},{1,0},{2,1},{3,2},{4,3},{5,4},{6,5},{7,6},{8,15},{9,8},{10,9... | collective-permute-start | bytes 835592 | tf_op jit(solution)/shard_map/ppermute | solution.py:402
  34.6 0.7 pad_maximum_fusion.1.select
  35.3 0.7 copy.23.scale
  36.1 0.7 copy-done.5
  36.8 5.2 %payoff.1 = bf16[4,1152,1152]{2,1,0:T(8,128)(2,1)S(1)} custom-call(s32[1]{0:T(128)S(6)} %copy.34.turn_card.turn_card_hbm, s32[1,32]{1,0:T(1,128)S(1)} %copy-done.6, s32[4,1326]{1,0:T(4,128)S(1)} %bitcast.55, bf16[1152,1152]{1,0:T(8,128)(2,1)S(1)} %copy-done, s32[2,1152]{1,0:T(2,128)S(1)} %copy-done.3), custom_call_target="tpu_custom_call" | custom-call | flops 21233664 | bytes 13271040 | tf_op jit(solution)/shard_map/payoff/pallas_call | solution.py:253
  42.0 7.9 %collective-permute-done.2.rest_2_ = f32[4,17,8,128]{3,2,1,0:T(8,128)} collective-permute-done((f32[4,17,8,128]{3,2,1,0:T(8,128)}, f32[4,17,8,128]{3,2,1,0:T(8,128)}, u32[]{:S(2)}, u32[]{:S(2)}) %collective-permute-start.2) | collective-permute-done | bytes 278560 | tf_op jit(solution)/shard_map/ppermute | solution.py:402
  50.0 0.0 copy-start.4
  50.0 5.7 %early.1 = f32[4,128,1152]{2,1,0:T(8,128)S(1)} custom-call(bf16[4,1152,1152]{2,1,0:T(8,128)(2,1)S(1)} %payoff.1, bf16[128,80]{1,0:T(8,128)(2,1)S(1)} %bitcast.54, f32[4,17,8,128]{3,2,1,0:T(8,128)S(1)} %collective-permute-done.rest_0_, f32[4,17,8,128]{3,2,1,0:T(8,128)S(1)} %collective-permute-done.1.rest_1_, ...), custom_call_target="tpu_custom_call" | custom-call | flops 2717908992 | bytes 10616832 | tf_op jit(solution)/shard_map/early/pallas_call | solution.py:302
  55.7 3.9 %collective-permute-done.5.rest_1_ = f32[4,17,8,128]{3,2,1,0:T(8,128)} collective-permute-done((f32[4,17,8,128]{3,2,1,0:T(8,128)}, f32[4,17,8,128]{3,2,1,0:T(8,128)}, u32[]{:S(2)}, u32[]{:S(2)}) %collective-permute-start.5) | collective-permute-done | bytes 278560 | tf_op jit(solution)/shard_map/ppermute | solution.py:402
  59.7 1.6 %collective-permute-done.6.rest_2_ = f32[4,17,8,128]{3,2,1,0:T(8,128)} collective-permute-done((f32[4,17,8,128]{3,2,1,0:T(8,128)}, f32[4,17,8,128]{3,2,1,0:T(8,128)}, u32[]{:S(2)}, u32[]{:S(2)}) %collective-permute-start.6) | collective-permute-done | bytes 278560 | tf_op jit(solution)/shard_map/ppermute | solution.py:402
  61.2 5.2 %reply.1 = f32[8,10,8,128]{3,2,1,0:T(8,128)} custom-call(s32[1]{0:T(128)S(6)} %copy.34.turn_card.turn_card_hbm, s32[1,32]{1,0:T(1,128)S(1)} %copy-done.6, bf16[4,1152,1152]{2,1,0:T(8,128)(2,1)S(1)} %payoff.1, f32[4,128,1152]{2,1,0:T(8,128)S(1)} %early.1, bf16[128,96]{1,0:T(8,128)(2,1)S(1)} %copy-done.4, f32[128,1]{1,0:T(8,128)S(1)} %copy-done.2, ...), custom_call_target="tpu_custom_call" | custom-call | flops 2717908992 | bytes 10616832 | tf_op jit(solution)/shard_map/reply/pallas_call | solution.py:354
  66.4 6.0 %all-to-all-start = ((f32[8,10,8,128]{3,2,1,0:T(8,128)}), f32[8,10,8,128]{3,2,1,0:T(8,128)S(1)}, u32[]{:S(2)}, u32[]{:S(2)}) async-start(f32[8,10,8,128]{3,2,1,0:T(8,128)} %reply.1), calls=%async_computation | async-start | bytes 655360 | tf_op jit(solution)/shard_map/all_to_all | solution.py:428
  72.4 12.2 %all-to-all-done = f32[8,10,8,128]{3,2,1,0:T(8,128)S(1)} async-done(((f32[8,10,8,128]{3,2,1,0:T(8,128)}), f32[8,10,8,128]{3,2,1,0:T(8,128)S(1)}, u32[]{:S(2)}, u32[]{:S(2)}) %all-to-all-start) | async-done | bytes 327712 | tf_op jit(solution)/shard_map/all_to_all | solution.py:428
  84.7 0.1 collective-permute-start.7
  84.8 1.2 collective-permute-done.7
  85.9 1.6 %collective-permute-start.8 = (f32[5,8,128]{2,1,0:T(8,128)S(1)}, f32[5,8,128]{2,1,0:T(8,128)S(1)}, u32[]{:S(2)}, u32[]{:S(2)}) collective-permute-start(f32[5,8,128]{2,1,0:T(8,128)S(1)} %dynamic-slice_add_fusion), channel_id=1, source_target_pairs={{0,16},{8,24},{16,0},{24,8},{32,48},{40,56},{48,32},{56,40},{64,80... | collective-permute-start | bytes 61448 | tf_op jit(solution)/shard_map/ppermute | solution.py:387
  87.5 2.2 %collective-permute-done.8 = f32[5,8,128]{2,1,0:T(8,128)S(1)} collective-permute-done((f32[5,8,128]{2,1,0:T(8,128)S(1)}, f32[5,8,128]{2,1,0:T(8,128)S(1)}, u32[]{:S(2)}, u32[]{:S(2)}) %collective-permute-start.8) | collective-permute-done | bytes 20512 | tf_op jit(solution)/shard_map/ppermute | solution.py:387
  89.7 3.0 %collective-permute-start.9 = (f32[5,8,128]{2,1,0:T(8,128)S(1)}, f32[5,8,128]{2,1,0:T(8,128)S(1)}, u32[]{:S(2)}, u32[]{:S(2)}) collective-permute-start(f32[5,8,128]{2,1,0:T(8,128)S(1)} %add.59), channel_id=1, source_target_pairs={{0,48},{8,56},{16,32},{24,40},{32,16},{40,24},{48,0},{56,8},{64,11... | collective-permute-start | bytes 61448 | tf_op jit(solution)/shard_map/ppermute | solution.py:387
  92.8 2.0 %collective-permute-done.9 = f32[5,8,128]{2,1,0:T(8,128)S(1)} collective-permute-done((f32[5,8,128]{2,1,0:T(8,128)S(1)}, f32[5,8,128]{2,1,0:T(8,128)S(1)}, u32[]{:S(2)}, u32[]{:S(2)}) %collective-permute-start.9) | collective-permute-done | bytes 20512 | tf_op jit(solution)/shard_map/ppermute | solution.py:387
  94.7 0.8 collective-permute-start.10
  95.6 3.0 %collective-permute-done.10 = f32[5,8,128]{2,1,0:T(8,128)S(1)} collective-permute-done((f32[5,8,128]{2,1,0:T(8,128)S(1)}, f32[5,8,128]{2,1,0:T(8,128)S(1)}, u32[]{:S(2)}, u32[]{:S(2)}) %collective-permute-start.10) | collective-permute-done | bytes 20512 | tf_op jit(solution)/shard_map/ppermute | solution.py:387
  98.5 0.5 collective-permute-start.11
  99.0 4.5 %collective-permute-done.11 = f32[5,8,128]{2,1,0:T(8,128)S(1)} collective-permute-done((f32[5,8,128]{2,1,0:T(8,128)S(1)}, f32[5,8,128]{2,1,0:T(8,128)S(1)}, u32[]{:S(2)}, u32[]{:S(2)}) %collective-permute-start.11) | collective-permute-done | bytes 20512 | tf_op jit(solution)/shard_map/ppermute | solution.py:387
  103.5 0.8 broadcast_in_dim.30
  104.4 3.5 %all-to-all-start.1 = ((f32[8,15,8,128]{3,2,1,0:T(8,128)}), f32[8,15,8,128]{3,2,1,0:T(8,128)S(1)}, u32[]{:S(2)}, u32[]{:S(2)}) async-start(f32[8,15,8,128]{3,2,1,0:T(8,128)} %broadcast_in_dim.30), calls=%async_computation.1 | async-start | bytes 983040 | tf_op jit(solution)/shard_map/all_to_all | solution.py:432
  107.9 12.8 %all-to-all-done.1 = f32[8,15,8,128]{3,2,1,0:T(8,128)S(1)} async-done(((f32[8,15,8,128]{3,2,1,0:T(8,128)}), f32[8,15,8,128]{3,2,1,0:T(8,128)S(1)}, u32[]{:S(2)}, u32[]{:S(2)}) %all-to-all-start.1) | async-done | bytes 491552 | tf_op jit(solution)/shard_map/all_to_all | solution.py:432
  120.7 0.1 collective-permute-start.12
  120.9 0.2 concatenate.17
  121.1 1.3 %reshape_reshape.3 = f32[1,84864]{1,0:T(1,128)} reshape(f32[64,1326]{1,0:T(8,128)S(1)} %concatenate.17) | data formatting | bytes 678912 | tf_op jit(solution)/shard_map/reshape;reshape | solution.py:436
  122.6 0.2 concatenate.19
  122.8 1.0 reshape.80
  (39 shorter events, 0.3 us)
Async XLA Ops:
  4.9 26.4 %collective-permute-start = (f32[4,17,8,128]{3,2,1,0:T(8,128)}, f32[4,17,8,128]{3,2,1,0:T(8,128)S(1)}, u32[]{:S(2)}, u32[]{:S(2)}) collective-permute-start(f32[4,17,8,128]{3,2,1,0:T(8,128)} %get-tuple-element.10), channel_id=1, source_target_pairs={{0,2},{1,3},{2,4},{3,5},{4,6},{5,7},{6,0},{7,1},{8,10},{9,11},{10,... | collective-permute-start | bytes 835592 | tf_op jit(solution)/shard_map/ppermute | solution.py:402
  8.3 22.5 %copy-start.7 = (s32[64,2]{0,1:T(2,128)S(1)}, s32[64,2]{0,1:T(2,128)}, u32[]{:S(2)}) copy-start(s32[64,2]{0,1:T(2,128)} %param.17) | copy-start | bytes 1540
  8.3 22.8 %copy-start.8 = (s32[128]{0:T(128)S(1)}, s32[128]{0:T(128)}, u32[]{:S(2)}) copy-start(s32[128]{0:T(128)} %param.18) | copy-start | bytes 1540
  8.3 27.8 %copy-start = (bf16[1152,1152]{1,0:T(8,128)(2,1)S(1)}, bf16[1152,1152]{1,0:T(8,128)(2,1)}, u32[]{:S(2)}) copy-start(bf16[1152,1152]{1,0:T(8,128)(2,1)} %constant.14.clone.compat) | copy-start | bytes 7962628
  8.3 27.8 %copy-start.3 = (s32[2,1152]{1,0:T(2,128)S(1)}, s32[2,1152]{1,0:T(2,128)}, u32[]{:S(2)}) copy-start(s32[2,1152]{1,0:T(2,128)} %constant.13.clone.table.table_hbm) | copy-start | bytes 27652
  8.3 27.8 %copy-start.6 = (s32[1,32]{1,0:T(1,128)S(1)}, s32[1,32]{1,0:T(1,128)}, u32[]{:S(2)}) copy-start(s32[1,32]{1,0:T(1,128)} %river_card.3) | copy-start | bytes 388
  8.3 24.1 %collective-permute-start.1 = (f32[4,17,8,128]{3,2,1,0:T(8,128)}, f32[4,17,8,128]{3,2,1,0:T(8,128)S(1)}, u32[]{:S(2)}, u32[]{:S(2)}) collective-permute-start(f32[4,17,8,128]{3,2,1,0:T(8,128)} %get-tuple-element.11), channel_id=1, source_target_pairs={{0,6},{1,7},{2,0},{3,1},{4,2},{5,3},{6,4},{7,5},{8,14},{9,15},{10,... | collective-permute-start | bytes 835592 | tf_op jit(solution)/shard_map/ppermute | solution.py:402
  15.1 34.9 %collective-permute-start.2 = (f32[4,17,8,128]{3,2,1,0:T(8,128)}, f32[4,17,8,128]{3,2,1,0:T(8,128)}, u32[]{:S(2)}, u32[]{:S(2)}) collective-permute-start(f32[4,17,8,128]{3,2,1,0:T(8,128)} %get-tuple-element.12), channel_id=1, source_target_pairs={{0,3},{1,4},{2,5},{3,6},{4,7},{5,0},{6,1},{7,2},{8,11},{9,12},{10,... | collective-permute-start | bytes 835592 | tf_op jit(solution)/shard_map/ppermute | solution.py:402
  17.2 32.8 %collective-permute-start.3 = (f32[4,17,8,128]{3,2,1,0:T(8,128)}, f32[4,17,8,128]{3,2,1,0:T(8,128)}, u32[]{:S(2)}, u32[]{:S(2)}) collective-permute-start(f32[4,17,8,128]{3,2,1,0:T(8,128)} %get-tuple-element.13), channel_id=1, source_target_pairs={{0,5},{1,6},{2,7},{3,0},{4,1},{5,2},{6,3},{7,4},{8,13},{9,14},{10,... | collective-permute-start | bytes 835592 | tf_op jit(solution)/shard_map/ppermute | solution.py:402
  25.7 30.0 %collective-permute-start.4 = (f32[4,17,8,128]{3,2,1,0:T(8,128)}, f32[4,17,8,128]{3,2,1,0:T(8,128)S(1)}, u32[]{:S(2)}, u32[]{:S(2)}) collective-permute-start(f32[4,17,8,128]{3,2,1,0:T(8,128)} %get-tuple-element.15), channel_id=1, source_target_pairs={{0,4},{1,5},{2,6},{3,7},{4,0},{5,1},{6,2},{7,3},{8,12},{9,13},{10,... | collective-permute-start | bytes 835592 | tf_op jit(solution)/shard_map/ppermute | solution.py:402
  31.3 28.3 %collective-permute-start.5 = (f32[4,17,8,128]{3,2,1,0:T(8,128)}, f32[4,17,8,128]{3,2,1,0:T(8,128)}, u32[]{:S(2)}, u32[]{:S(2)}) collective-permute-start(f32[4,17,8,128]{3,2,1,0:T(8,128)} %get-tuple-element.16), channel_id=1, source_target_pairs={{0,1},{1,2},{2,3},{3,4},{4,5},{5,6},{6,7},{7,0},{8,9},{9,10},{10,1... | collective-permute-start | bytes 835592 | tf_op jit(solution)/shard_map/ppermute | solution.py:402
  32.4 28.8 %collective-permute-start.6 = (f32[4,17,8,128]{3,2,1,0:T(8,128)}, f32[4,17,8,128]{3,2,1,0:T(8,128)}, u32[]{:S(2)}, u32[]{:S(2)}) collective-permute-start(f32[4,17,8,128]{3,2,1,0:T(8,128)} %get-tuple-element.17), channel_id=1, source_target_pairs={{0,7},{1,0},{2,1},{3,2},{4,3},{5,4},{6,5},{7,6},{8,15},{9,8},{10,9... | collective-permute-start | bytes 835592 | tf_op jit(solution)/shard_map/ppermute | solution.py:402
  36.1 0.7 copy-start.5
  36.8 13.2 %copy-start.1 = (f32[4,17,8,128]{3,2,1,0:T(8,128)S(1)}, f32[4,17,8,128]{3,2,1,0:T(8,128)}, u32[]{:S(2)}) copy-start(f32[4,17,8,128]{3,2,1,0:T(8,128)} %get-tuple-element.14.rest_4_) | copy-start | bytes 835588
  50.0 11.3 %copy-start.2 = (f32[128,1]{1,0:T(8,128)S(1)}, f32[128,1]{1,0:T(8,128)}, u32[]{:S(2)}) copy-start(f32[128,1]{1,0:T(8,128)} %copy.23.scale) | copy-start | bytes 1540
  50.0 11.2 %copy-start.4 = (bf16[128,96]{1,0:T(8,128)(2,1)S(1)}, bf16[128,96]{1,0:T(8,128)(2,1)}, u32[]{:S(2)}) copy-start(bf16[128,96]{1,0:T(8,128)(2,1)} %pad_maximum_fusion.1.select) | copy-start | bytes 73732
  66.4 18.2 %all-to-all-start = ((f32[8,10,8,128]{3,2,1,0:T(8,128)}), f32[8,10,8,128]{3,2,1,0:T(8,128)S(1)}, u32[]{:S(2)}, u32[]{:S(2)}) async-start(f32[8,10,8,128]{3,2,1,0:T(8,128)} %reply.1), calls=%async_computation | async-start | bytes 655360 | tf_op jit(solution)/shard_map/all_to_all | solution.py:428
  84.7 1.3 %collective-permute-start.7 = (f32[5,8,128]{2,1,0:T(8,128)S(1)}, f32[5,8,128]{2,1,0:T(8,128)S(1)}, u32[]{:S(2)}, u32[]{:S(2)}) collective-permute-start(f32[5,8,128]{2,1,0:T(8,128)S(1)} %constant_dynamic-slice_fusion), channel_id=1, source_target_pairs={{0,8},{8,0},{16,24},{24,16},{32,40},{40,32},{48,56},{56,48},{64,72... | collective-permute-start | bytes 61448 | tf_op jit(solution)/shard_map/ppermute | solution.py:383
  85.9 3.8 %collective-permute-start.8 = (f32[5,8,128]{2,1,0:T(8,128)S(1)}, f32[5,8,128]{2,1,0:T(8,128)S(1)}, u32[]{:S(2)}, u32[]{:S(2)}) collective-permute-start(f32[5,8,128]{2,1,0:T(8,128)S(1)} %dynamic-slice_add_fusion), channel_id=1, source_target_pairs={{0,16},{8,24},{16,0},{24,8},{32,48},{40,56},{48,32},{56,40},{64,80... | collective-permute-start | bytes 61448 | tf_op jit(solution)/shard_map/ppermute | solution.py:387
  89.7 5.0 %collective-permute-start.9 = (f32[5,8,128]{2,1,0:T(8,128)S(1)}, f32[5,8,128]{2,1,0:T(8,128)S(1)}, u32[]{:S(2)}, u32[]{:S(2)}) collective-permute-start(f32[5,8,128]{2,1,0:T(8,128)S(1)} %add.59), channel_id=1, source_target_pairs={{0,48},{8,56},{16,32},{24,40},{32,16},{40,24},{48,0},{56,8},{64,11... | collective-permute-start | bytes 61448 | tf_op jit(solution)/shard_map/ppermute | solution.py:387
  94.7 3.8 %collective-permute-start.10 = (f32[5,8,128]{2,1,0:T(8,128)S(1)}, f32[5,8,128]{2,1,0:T(8,128)S(1)}, u32[]{:S(2)}, u32[]{:S(2)}) collective-permute-start(f32[5,8,128]{2,1,0:T(8,128)S(1)} %add.60), channel_id=1, source_target_pairs={{0,64},{8,72},{16,80},{24,88},{32,96},{40,104},{48,112},{56,120},{... | collective-permute-start | bytes 61448 | tf_op jit(solution)/shard_map/ppermute | solution.py:387
  98.5 5.0 %collective-permute-start.11 = (f32[5,8,128]{2,1,0:T(8,128)S(1)}, f32[5,8,128]{2,1,0:T(8,128)S(1)}, u32[]{:S(2)}, u32[]{:S(2)}) collective-permute-start(f32[5,8,128]{2,1,0:T(8,128)S(1)} %add.61), channel_id=1, source_target_pairs={{0,192},{8,200},{16,208},{24,216},{32,224},{40,232},{48,240},{56,2... | collective-permute-start | bytes 61448 | tf_op jit(solution)/shard_map/ppermute | solution.py:387
  104.4 16.3 %all-to-all-start.1 = ((f32[8,15,8,128]{3,2,1,0:T(8,128)}), f32[8,15,8,128]{3,2,1,0:T(8,128)S(1)}, u32[]{:S(2)}, u32[]{:S(2)}) async-start(f32[8,15,8,128]{3,2,1,0:T(8,128)} %broadcast_in_dim.30), calls=%async_computation.1 | async-start | bytes 983040 | tf_op jit(solution)/shard_map/all_to_all | solution.py:432
  120.7 1.7 %collective-permute-start.12 = (f32[8,5,8,128]{3,2,1,0:T(8,128)S(1)}, f32[8,5,8,128]{3,2,1,0:T(8,128)S(1)}, u32[]{:S(2)}, u32[]{:S(2)}) collective-permute-start(f32[8,5,8,128]{3,2,1,0:T(8,128)S(1)} %slice.55), channel_id=1, source_target_pairs={{0,8},{8,0},{16,24},{24,16},{32,40},{40,32},{48,56},{56,48},{64,72... | collective-permute-start | bytes 491528 | tf_op jit(solution)/shard_map/ppermute | solution.py:434
